TPU v7x, 256 devices: a whole 4x4x8 slice. The times are simulated.
256 devices in a mesh: frames: 4 (over x), space: 64 (over z, y, core).
Axes of the slice: x: 4, y: 4, z: 8, core: 2. Of those that a mesh axis runs over, the one named last changes fastest.
Arguments:
- queries: bfloat16 [65536, 2240], P(('frames', 'space')), may hold values from -6 to 6
- key_inputs: bfloat16 [65536, 2240], P(('frames', 'space')), may hold values from -6 to 6
- value_inputs: bfloat16 [65536, 2240], P(('frames', 'space')), may hold values from -10 to 10
- out_cotangent: bfloat16 [65536, 2240], P(('frames', 'space')), may hold values from -3072 to 3072
- frame_ids: int32 [65536], P(('frames', 'space')), may hold values from 0 to 1, as said below
Outputs:
- grad_queries: bfloat16 [65536, 2240], P(('frames', 'space'))
- grad_keys: bfloat16 [65536, 2240], P(('frames', 'space'))
- grad_values: bfloat16 [65536, 2240], P(('frames', 'space'))
Inputs may be any that keep to these rules, and one draw needn't show every extreme that they name: `frame_ids`: on each device's 256 tokens the numbers never fall; the first is 0 and the last 1.
All inputs are finite; a program needn't handle non-finite values.
Results may differ from a plain program's by a relative error of at most 0.002.
Values sent between devices are 32-bit elements; how exact they have to be, the bound alone decides.
No kernel may reach another device: no remote copies, remote signals or barrier semaphores. Data moves between devices by JAX's collectives and lax.ppermute only.
A program may use at most 128 MiB of HBM per device.

v0:
```python
import jax
import jax.numpy as jnp
from jax import lax
from jax.sharding import PartitionSpec as P

H = 20
E = 112
FG = 2


HIGH = lax.Precision.HIGHEST


def carried_in(value, axis, join, neutral, backward):
    count, mine = (lax.axis_size(axis), lax.axis_index(axis))
    pieces = jax.tree.map(lambda part: lax.all_gather(part, axis), value)
    if backward:
        pieces = jax.tree.map(lambda part: part[::-1], pieces)
        mine = count - 1 - mine
    total = jax.tree.map(
        lambda part, zero: jnp.full_like(part, 0) + jnp.asarray(zero, part.dtype), value, neutral
    )

    def step(position, total):
        longer = join(total, jax.tree.map(lambda part: part[position], pieces))
        return jax.tree.map(lambda new, old: jnp.where(position < mine, new, old), longer, total)

    return lax.fori_loop(0, count - 1, step, total)


def add_pair(earlier, later):
    return (earlier[0] + later[0], earlier[1] + later[1])


def on_device(queries, key_inputs, value_inputs, out_cotangent, frame_ids):
    count = queries.shape[0]
    shape = (count, H, E)
    masks = (frame_ids[:, None] == jnp.arange(FG, dtype=jnp.int32)[None, :]).astype(jnp.bfloat16)
    masks_wide = masks.astype(jnp.float32)
    phi_key = jax.nn.relu(key_inputs).reshape(shape)
    value_rows = value_inputs.reshape(shape)
    key_states = jnp.stack(
        [
            jnp.einsum(
                "the,thd->hed",
                phi_key * masks[:, frame, None, None],
                value_rows,
                preferred_element_type=jnp.float32,
            )
            for frame in range(FG)
        ],
        axis=2,
    ).reshape(H * E, FG * E)
    key_sums = jnp.einsum("tf,the->fhe", masks, phi_key, preferred_element_type=jnp.float32)
    group_states, group_sums = lax.psum((key_states, key_sums), "space")
    block = group_states.reshape(H * E, FG, E)
    prefix, sums_prefix = carried_in(
        (jnp.sum(block, axis=1), jnp.sum(group_sums, axis=0)),
        "frames",
        add_pair,
        (jnp.zeros((H * E, E), jnp.float32), jnp.zeros((H, E), jnp.float32)),
        False,
    )
    cumulative = (prefix[:, None, :] + jnp.cumsum(block, axis=1)).reshape(H, E, FG, E)
    cum_sums = sums_prefix[None] + jnp.cumsum(group_sums, axis=0)
    phi_query = jax.nn.relu(queries).reshape(shape).astype(jnp.float32)
    numer = jnp.zeros(shape, jnp.float32)
    denom = jnp.ones((count, H), jnp.float32)
    for frame in range(FG):
        masked = phi_query * masks_wide[:, frame, None, None]
        numer = numer + jnp.einsum(
            "the,hed->thd", masked, cumulative[:, :, frame, :], precision=HIGH
        )
        denom = denom + jnp.einsum("the,he->th", masked, cum_sums[frame], precision=HIGH)
    output = numer / denom[..., None]
    cotangent = out_cotangent.reshape(shape).astype(jnp.float32)
    grad_numer = cotangent / denom[..., None]
    grad_denom = -jnp.sum(cotangent * output, axis=-1) / denom
    grad_phi_query = jnp.zeros(shape, jnp.float32)
    query_states = []
    for frame in range(FG):
        weight = masks_wide[:, frame, None, None]
        through = jnp.einsum("thd,hed->the", grad_numer, cumulative[:, :, frame, :], precision=HIGH)
        grad_phi_query = grad_phi_query + weight * (
            through + grad_denom[..., None] * cum_sums[frame][None]
        )
        query_states.append(
            jnp.einsum("the,thd->hed", phi_query * weight, grad_numer, precision=HIGH)
        )
    query_states = jnp.stack(query_states, axis=2).reshape(H * E, FG * E)
    query_sums = jnp.einsum(
        "tf,the->fhe", masks_wide, phi_query * grad_denom[..., None], precision=HIGH
    )
    group_grads, group_grad_sums = lax.psum((query_states, query_sums), "space")
    block = group_grads.reshape(H * E, FG, E)
    suffix, sums_suffix = carried_in(
        (jnp.sum(block, axis=1), jnp.sum(group_grad_sums, axis=0)),
        "frames",
        add_pair,
        (jnp.zeros((H * E, E), jnp.float32), jnp.zeros((H, E), jnp.float32)),
        True,
    )
    reverse_cum = (suffix[:, None, :] + lax.cumsum(block, axis=1, reverse=True)).reshape(
        H, E, FG, E
    )
    reverse_sums = sums_suffix[None] + lax.cumsum(group_grad_sums, axis=0, reverse=True)
    phi_key_wide = phi_key.astype(jnp.float32)
    value_wide = value_rows.astype(jnp.float32)
    grad_phi_key = jnp.zeros(shape, jnp.float32)
    grad_value = jnp.zeros(shape, jnp.float32)
    for frame in range(FG):
        weight = masks_wide[:, frame, None, None]
        carried = reverse_cum[:, :, frame, :]
        grad_phi_key = grad_phi_key + weight * (
            jnp.einsum("thd,hed->the", value_wide, carried, precision=HIGH)
            + reverse_sums[frame][None]
        )
        grad_value = grad_value + weight * jnp.einsum(
            "the,hed->thd", phi_key_wide, carried, precision=HIGH
        )
    width = H * E
    grad_queries = jnp.where(queries > 0, grad_phi_query.reshape(count, width), 0.0).astype(
        jnp.bfloat16
    )
    grad_keys = jnp.where(key_inputs > 0, grad_phi_key.reshape(count, width), 0.0).astype(
        jnp.bfloat16
    )
    grad_values = grad_value.reshape(count, width).astype(jnp.bfloat16)
    return (grad_queries, grad_keys, grad_values)


def solution(mesh):
    placed = (
        P(("frames", "space"), None),
        P(("frames", "space"), None),
        P(("frames", "space"), None),
        P(("frames", "space"), None),
        P(("frames", "space")),
    )
    return jax.shard_map(
        on_device,
        mesh=mesh,
        in_specs=placed,
        out_specs=(
            P(("frames", "space"), None),
            P(("frames", "space"), None),
            P(("frames", "space"), None),
        ),
        check_vma=False,
    )
```

profile of v0, /device:TPU:1, one launch (start us, length us, event | category | flops | bytes accessed | tf_op | source)
XLA Modules:
  0.0 1012.3 jit_solution(12207723042077832778)
XLA Ops:
  9.9 3.1 copy.22
  13.0 3.9 reshape.63
  16.9 192.4 %all-reduce.3.cloned.1.call-done = f32[2240,224]{1,0:T(8,128)} async-done(((f32[2240,224]{1,0:T(8,128)}), f32[2240,224]{1,0:T(8,128)}) %all-reduce.3.cloned.1.call-update) | async-done | bytes 2007056 | tf_op jit(solution)/shard_map/psum | solution.py:55
  209.4 3.0 copy.23
  212.4 2.9 reduce_sum.45
  215.8 246.2 %psum.29 = f32[2,20,112]{2,0,1:T(2,128)S(1)} all-reduce(f32[2,20,112]{2,0,1:T(2,128)S(1)} %fusion.43), channel_id=1, replica_groups=mesh['frames'=4,'space'=64] {'space'}, use_global_device_ids=true, to_apply=%region_2.3 | all-reduce | flops 4480 | bytes 35840 | tf_op jit(solution)/shard_map/psum | solution.py:55
  462.1 9.8 all-gather.5
  472.9 10.9 %while.32 = (s32[]{:T(128)}, f32[2240,112]{1,0:T(8,128)}, f32[20,112]{1,0:T(8,128)S(1)}, s32[]{:T(128)}, f32[4,2240,112]{1,2,0:T(8,128)}, /*index=5*/f32[4,20,112]{2,1,0:T(8,128)S(1)}, s32[]{:T(128)}, s32[]{:T(128)}) while((s32[]{:T(128)}, f32[2240,112]{1,0:T(8,128)}, f32[20,112]{1,0:T(8,128)S(1)}, s32[]{:T(128)}, ...), condition=%wide.region_5.6_spmd.clone, body=%wide.region_4.5_spmd.clone.sunk | while | flops 759364 | bytes 7051643 | solution.py:28
  483.9 2.7 fusion.5
  486.6 2.6 fusion.2
  491.8 2.5 fusion.24
  494.5 3.2 copy.28
  497.7 3.9 reshape.66
  501.9 191.9 %all-reduce.5.cloned.1.call-done = f32[2240,224]{1,0:T(8,128)} async-done(((f32[2240,224]{1,0:T(8,128)}), f32[2240,224]{1,0:T(8,128)}) %all-reduce.5.cloned.1.call-update) | async-done | bytes 2007056 | tf_op jit(solution)/shard_map/psum | solution.py:94
  693.8 3.0 copy.29
  696.8 2.8 reduce_sum.48
  699.7 4.2 reduce_window_sum.46
  708.2 2.8 fusion.6
  712.3 246.2 %psum.31 = f32[2,20,112]{2,0,1:T(2,128)S(1)} all-reduce(f32[2,20,112]{2,0,1:T(2,128)S(1)} %fusion.7), channel_id=1, replica_groups=mesh['frames'=4,'space'=64] {'space'}, use_global_device_ids=true, to_apply=%region_11.12 | all-reduce | flops 4480 | bytes 35840 | tf_op jit(solution)/shard_map/psum | solution.py:94
  959.2 9.6 all-gather.7
  968.8 4.1 fusion.34
  972.9 2.8 fusion.11
  980.3 4.5 reverse
  984.8 10.9 %while.33 = (s32[]{:T(128)}, f32[2240,112]{1,0:T(8,128)}, f32[20,112]{1,0:T(8,128)S(1)}, s32[]{:T(128)}, f32[4,2240,112]{1,2,0:T(8,128)}, /*index=5*/f32[4,20,112]{2,1,0:T(8,128)S(1)}, s32[]{:T(128)}, s32[]{:T(128)}) while((s32[]{:T(128)}, f32[2240,112]{1,0:T(8,128)}, f32[20,112]{1,0:T(8,128)S(1)}, s32[]{:T(128)}, ...), condition=%wide.region_14.15_spmd.clone, body=%wide.region_13.14_spmd.clone.sunk | while | flops 759364 | bytes 7051643 | solution.py:28
  (107 shorter events, 50.0 us)
Async XLA Ops:
  7.2 1.6 copy-start
  7.2 1.5 copy-start.12
  7.2 202.2 %all-reduce.3.cloned.1.call-start = ((), (), s32[]{:S(2)}) async-start(), calls=%async_computation | async-start | bytes 4587520 | tf_op jit(solution)/shard_map/psum | solution.py:55
  8.7 206.7 %copy-start.1 = (bf16[256,2240]{0,1:T(8,128)(2,1)}, bf16[256,2240]{0,1:T(8,128)(2,1)S(1)}, u32[]{:S(2)}) copy-start(bf16[256,2240]{0,1:T(8,128)(2,1)S(1)} %broadcast_maximum_fusion.1) | copy-start | bytes 3440644
  16.9 456.1 %all-gather.11.cloned.1.call-start = ((), (), s32[]{:S(2)}) async-start(), calls=%async_computation.2 | async-start | bytes 5160960 | tf_op jit(solution)/shard_map/all_gather | solution.py:16
  212.4 259.4 %copy-start.8 = (bf16[256,2240]{0,1:T(8,128)(2,1)S(1)}, bf16[256,2240]{0,1:T(8,128)(2,1)}, u32[]{:S(2)}) copy-start(bf16[256,2240]{0,1:T(8,128)(2,1)} %param.9) | copy-start | bytes 3440644
  215.3 478.5 %all-reduce.5.cloned.1.call-start = ((), (), s32[]{:S(2)}) async-start(), calls=%async_computation.1 | async-start | bytes 4587520 | tf_op jit(solution)/shard_map/psum | solution.py:94
  483.9 5.4 copy-start.4
  483.9 5.4 copy-start.14
  501.6 478.7 %all-gather.13.cloned.1.call-start = ((), (), s32[]{:S(2)}) async-start(), calls=%async_computation.3 | async-start | bytes 5160960 | tf_op jit(solution)/shard_map/all_gather | solution.py:16
  699.7 4.2 copy-start.3
  705.7 2.4 copy-start.6
  705.7 2.4 copy-start.15
  708.1 2.8 copy-start.13
  968.8 4.1 copy-start.7
  968.8 4.1 copy-start.16
  972.9 2.9 copy-start.9
  975.7 2.1 copy-start.5
  997.9 1.3 copy-start.2
  999.1 1.1 copy-start.11
  1000.3 1.6 copy-start.10
Sparse Core Ops, SparseCore 0:
  17.0 192.3 all-reduce.2
  215.4 50.6 all-gather.10
  501.7 192.0 all-reduce.4
  699.8 50.6 all-gather.12
where the time goes:
time: 1020 us; the launch traced here: 1010 us
  blocking collectives  512 us (50%)
  waiting for transfers between devices  384 us (38%)
  local copies, waits for them, and re-layouts  42.2 us (4%)
  matrix products  31.3 us (3%)
  other arithmetic  28.1 us (3%)
  between operations  14.2 us (1%)
    psum x1, blocking collectives, on_device(): group_states, group_sums = lax.psum((key_states, key_sums), 'space')  246 us
    psum x1, blocking collectives, on_device(): group_grads, group_grad_sums = lax.psum((query_states, query_sums), 'space')  246 us
    psum x1, waiting for transfers between devices, on_device(): group_states, group_sums = lax.psum((key_states, key_sums), 'space')  192 us
    psum x1, waiting for transfers between devices, on_device(): group_grads, group_grad_sums = lax.psum((query_states, query_sums), 'space')  192 us
  transfers between devices with their start and end apart: 4, of which 2 were waited for; matrix products, arithmetic and copies ran while one was open for 3% of the time, Pallas kernels for 0%

commit v1 on v0

v1 whole, which is shorter than its diff:
```python
import jax
import jax.numpy as jnp
from jax import lax
from jax.experimental import pallas as pl
from jax.experimental.pallas import tpu as pltpu
from jax.sharding import Mesh, PartitionSpec as P

H = 20
E = 112
FG = 2
LANES = 128
CORES = 2
HALF = H // CORES
F32 = jnp.float32
BF16 = jnp.bfloat16
VMEM_LIMIT = 40 * 1024 * 1024


def frame_rows(ids_ref, count):
    zeros = (ids_ref[...] == 0).astype(F32)
    first = jnp.sum(jnp.sum(zeros, axis=1, keepdims=True), axis=0, keepdims=True)
    row = lax.broadcasted_iota(jnp.int32, (count, LANES), 0).astype(F32)
    early = row < first
    mask = early.astype(F32)
    return early, mask.astype(BF16), (1.0 - mask).astype(BF16)


def by_frame(rows, first, second):
    return jnp.concatenate([rows * first, rows * second], axis=1)


def split(values):
    high = values.astype(BF16)
    return high, (values - high.astype(F32)).astype(BF16)


def head(ref, h):
    return ref[:, h * E : (h + 1) * E]


def widen(rows):
    return jnp.concatenate([rows, jnp.ones((rows.shape[0], LANES - E), rows.dtype)], axis=1)


def over_tokens(left, right):
    return lax.dot_general(left, right, (((0,), (0,)), ((), ())), preferred_element_type=F32)


def plain(left, right):
    return jnp.dot(left, right, preferred_element_type=F32)


def transposed(left, right):
    return lax.dot_general(left, right, (((1,), (1,)), ((), ())), preferred_element_type=F32)


def put(core, h, block, keep_ref, send_ref):
    rows = pl.ds((h % HALF) * E, E)

    @pl.when(core == h // HALF)
    def _():
        keep_ref[rows, :] = block

    @pl.when(core != h // HALF)
    def _():
        send_ref[rows, :] = block


def get(core, h, mine_ref, other_ref):
    rows = pl.ds((h % HALF) * E, E)
    return jnp.where(core == h // HALF, mine_ref[rows, :], other_ref[rows, :])


def key_kernel(ids_ref, key_ref, value_ref, keep_ref, send_ref):
    core = lax.axis_index("core")
    _, first, second = frame_rows(ids_ref, key_ref.shape[0])
    for h in range(H):
        phi = jnp.maximum(head(key_ref, h), 0)
        values = by_frame(widen(head(value_ref, h)), first, second)
        put(core, h, over_tokens(phi, values), keep_ref, send_ref)


def query_kernel(ids_ref, query_ref, cot_ref, mine_ref, other_ref, grad_ref, keep_ref, send_ref):
    core = lax.axis_index("core")
    count = query_ref.shape[0]
    early, first, second = frame_rows(ids_ref, count)
    for h in range(H):
        high, low = split(get(core, h, mine_ref, other_ref))
        query = head(query_ref, h)
        phi = jnp.maximum(query, 0)
        both = plain(phi, high) + plain(phi, low)
        numer = jnp.where(early, both[:, :LANES], both[:, LANES:])
        inverse = 1.0 / (numer[:, E : E + 1] + 1.0)
        cot = head(cot_ref, h)
        wide = cot.astype(F32)
        inner = -jnp.sum(wide * numer[:, :E], axis=1, keepdims=True) * inverse
        grads = jnp.concatenate(
            [wide * inverse, inner * inverse, jnp.zeros((count, LANES - E - 1), F32)], axis=1
        )
        grads_high, grads_low = split(grads)
        block = over_tokens(phi, by_frame(grads_high, first, second)) + over_tokens(
            phi, by_frame(grads_low, first, second)
        )
        put(core, h, block, keep_ref, send_ref)
        inner_high, rest = split(inner)
        inner_mid = (inner - inner_high.astype(F32)).astype(BF16)
        inner_low = (inner - inner_high.astype(F32) - inner_mid.astype(F32)).astype(BF16)
        left = jnp.concatenate(
            [cot, inner_high, inner_mid, inner_low, jnp.zeros((count, LANES - E - 3), BF16)], axis=1
        )
        left = by_frame(left, first, second)
        grad = (transposed(left, high) + transposed(left, low)) * inverse
        grad_ref[:, h * E : (h + 1) * E] = jnp.where(query.astype(F32) > 0, grad, 0.0).astype(BF16)


def value_kernel(ids_ref, key_ref, value_ref, mine_ref, other_ref, grad_key_ref, grad_value_ref):
    core = lax.axis_index("core")
    early, first, second = frame_rows(ids_ref, key_ref.shape[0])
    for h in range(H):
        high, low = split(get(core, h, mine_ref, other_ref))
        key = head(key_ref, h)
        phi = jnp.maximum(key, 0)
        both = plain(phi, high) + plain(phi, low)
        grad = jnp.where(early, both[:, :LANES], both[:, LANES:])
        grad_value_ref[:, h * E : (h + 1) * E] = grad[:, :E].astype(BF16)
        values = by_frame(widen(head(value_ref, h)), first, second)
        grad = transposed(values, high) + transposed(values, low)
        grad_key_ref[:, h * E : (h + 1) * E] = jnp.where(key.astype(F32) > 0, grad, 0.0).astype(BF16)


def call(kernel, outs, *operands):
    return pl.pallas_call(
        kernel,
        out_shape=outs,
        compiler_params=pltpu.CompilerParams(vmem_limit_bytes=VMEM_LIMIT),
    )(*operands)


def swap_cores(block):
    return lax.ppermute(block, "core", [(0, 1), (1, 0)])


def exchange(block, axis):
    return lax.all_to_all(block, axis, 0, 0, tiled=False)


def carried(keep, send, backward):
    y, z, frames = lax.axis_size("y"), lax.axis_size("z"), lax.axis_size("frames")
    rows = keep.shape[0] // y
    part = -(-rows // (8 * z)) * 8
    summed = (keep + swap_cores(send)).reshape(y, rows, FG * LANES)
    summed = jnp.sum(exchange(summed, "y"), axis=0)
    summed = jnp.pad(summed, ((0, z * part - rows), (0, 0))).reshape(z, part, FG * LANES)
    summed = jnp.sum(exchange(summed, "z"), axis=0)
    frame0, frame1 = summed[:, :LANES], summed[:, LANES:]
    total = frame0 + frame1
    me = lax.axis_index("frames")
    carry = jnp.zeros_like(total)
    for hop in range(1, frames):
        step = -hop if backward else hop
        moved = lax.ppermute(total, "frames", [(i, (i + step) % frames) for i in range(frames)])
        reaches = (me + hop < frames) if backward else (me >= hop)
        carry = carry + jnp.where(reaches, moved, 0.0)
    if backward:
        done = jnp.concatenate([carry + total, carry + frame1], axis=1)
    else:
        done = jnp.concatenate([carry + frame0, carry + total], axis=1)
    done = exchange(jnp.broadcast_to(done[None], (z,) + done.shape), "z")
    done = done.reshape(z * part, FG * LANES)[:rows]
    done = exchange(jnp.broadcast_to(done[None], (y,) + done.shape), "y")
    done = done.reshape(y * rows, FG * LANES)
    return done, swap_cores(done)


def on_device(queries, key_inputs, value_inputs, out_cotangent, frame_ids):
    ids = frame_ids.reshape(-1, LANES)
    states = jax.ShapeDtypeStruct((HALF * E, FG * LANES), F32)
    grads = jax.ShapeDtypeStruct(queries.shape, BF16)
    keep, send = call(key_kernel, (states, states), ids, key_inputs, value_inputs)
    mine, other = carried(keep, send, False)
    grad_queries, keep, send = call(
        query_kernel, (grads, states, states), ids, queries, out_cotangent, mine, other
    )
    mine, other = carried(keep, send, True)
    grad_keys, grad_values = call(
        value_kernel, (grads, grads), ids, key_inputs, value_inputs, mine, other
    )
    return grad_queries, grad_keys, grad_values


def solution(mesh):
    sizes = mesh.shape
    y = 4
    z = sizes["space"] // (y * CORES)
    fine = Mesh(
        mesh.devices.reshape(sizes["frames"], z, y, CORES), ("frames", "z", "y", "core")
    )
    space = ("frames", "z", "y", "core")
    rows = P(space, None)
    return jax.shard_map(
        on_device,
        mesh=fine,
        in_specs=(rows, rows, rows, rows, P(space)),
        out_specs=(rows, rows, rows),
        check_vma=False,
    )
```

time: 1020 us -> 210 us (0.21)
  blocking collectives: 512 us -> 122 us
  waiting for transfers between devices: 384 us -> 10.4 us
  Pallas kernels: 0 us -> 32.1 us
  matrix products: 31.3 us -> 0 us
  other arithmetic: 28.1 us -> 2.01 us
  local copies, waits for them, and re-layouts: 42.2 us -> 18 us
  starting transfers between devices: 0.38 us -> 24 us
  between operations: 14.2 us -> 0.85 us
    psum x2 -> x0, blocking collectives: 492 us -> none  [the longest x1 246 us: on_device(): group_states, group_sums = lax.psum((key_states, key_sums), 'space')]
    psum x2 -> x0, waiting for transfers between devices: 384 us -> none  [the longest x1 192 us: on_device(): group_states, group_sums = lax.psum((key_states, key_sums), 'space')]
    all_to_all x0 -> x8, blocking collectives: none -> 122 us  [exchange(): return lax.all_to_all(block, axis, 0, 0, tiled=False)]
    pallas_call x0 -> x3, Pallas kernels: none -> 32.1 us  [call(): pl.pallas_call(kernel, out_shape=outs, compiler_params=pltpu.CompilerPara...]
    dot_general x16 -> x0, matrix products: 31.3 us -> none  [the longest x2 6.89 us: on_device(): jnp.einsum('thd,hed->the', grad_numer, cumulative[:, :, frame, :], precis...]
    ppermute x0 -> x10, starting transfers between devices: none -> 24 us  [the longest x4 16 us: swap_cores(): return lax.ppermute(block, 'core', [(0, 1), (1, 0)])]
    all_gather x2 -> x0, blocking collectives: 19.3 us -> none  [carried_in(): pieces = jax.tree.map(lambda part: lax.all_gather(part, axis), value)]
    unnamed x36 -> x21, local copies, waits for them, and re-layouts: 0.93 us -> 15.9 us
  transfers between devices with their start and end apart: 4 -> 10, of which waited for: 2 -> 7; matrix products, arithmetic and copies ran while one was open for 3% -> 3% of each run, Pallas kernels for 0% -> 0%
where the time goes in v1:
time: 210 us
  blocking collectives  122 us (58%)
  Pallas kernels  32.1 us (15%)
  starting transfers between devices  24 us (11%)
  local copies, waits for them, and re-layouts  18 us (9%)
  waiting for transfers between devices  10.4 us (5%)
    all_to_all x8, blocking collectives, exchange(): return lax.all_to_all(block, axis, 0, 0, tiled=False)  122 us
    pallas_call x3, Pallas kernels, call(): pl.pallas_call(kernel, out_shape=outs, compiler_params=pltpu.CompilerPara...  32.1 us
    ppermute x4, starting transfers between devices, swap_cores(): return lax.ppermute(block, 'core', [(0, 1), (1, 0)])  16 us
    unnamed x21, local copies, waits for them, and re-layouts  15.9 us
    ppermute x6, starting transfers between devices, carried(): lax.ppermute(total, 'frames', [(i, (i + step) % frames) for i in range(fr...  7.95 us
    ppermute x4, waiting for transfers between devices, swap_cores(): return lax.ppermute(block, 'core', [(0, 1), (1, 0)])  5.42 us
    ppermute x6, waiting for transfers between devices, carried(): lax.ppermute(total, 'frames', [(i, (i + step) % frames) for i in range(fr...  4.94 us
  transfers between devices with their start and end apart: 10, of which 7 were waited for; matrix products, arithmetic and copies ran while one was open for 3% of the time, Pallas kernels for 0%

profile of v1, /device:TPU:1, one launch (start us, length us, event | category | flops | bytes accessed | tf_op | source)
XLA Modules:
  0.0 209.6 jit_solution(14424945361685972009)
XLA Ops:
  0.6 1.7 copy.17.key_ref
  3.1 5.8 %shard_map.76 = (f32[1120,256]{1,0:T(8,128)S(1)}, f32[1120,256]{1,0:T(8,128)S(1)}) custom-call(s32[2,128]{1,0:T(2,128)S(1)} %bitcast.11, bf16[256,2240]{1,0:T(8,128)(2,1)S(1)} %copy.17.key_ref, bf16[256,2240]{1,0:T(8,128)(2,1)S(1)} %copy.18.value_ref), custom_call_target="tpu_custom_call" | custom-call | tf_op jit(solution)/shard_map/pallas_call | solution.py:132
  8.8 3.3 %collective-permute-start = (f32[1120,256]{1,0:T(8,128)S(1)}, f32[1120,256]{1,0:T(8,128)S(1)}, u32[]{:S(2)}, u32[]{:S(2)}) collective-permute-start(f32[1120,256]{1,0:T(8,128)S(1)} %get-tuple-element.11), channel_id=1, source_target_pairs={{0,1},{1,0},{2,3},{3,2},{4,5},{5,4},{6,7},{7,6},{8,9},{9,8},{10,11... | collective-permute-start | bytes 3440648 | tf_op jit(solution)/shard_map/ppermute | solution.py:140
  12.1 2.4 %collective-permute-done = f32[1120,256]{1,0:T(8,128)S(1)} collective-permute-done((f32[1120,256]{1,0:T(8,128)S(1)}, f32[1120,256]{1,0:T(8,128)S(1)}, u32[]{:S(2)}, u32[]{:S(2)}) %collective-permute-start) | collective-permute-done | bytes 1146912 | tf_op jit(solution)/shard_map/ppermute | solution.py:140
  14.7 17.9 %all_to_all.40 = f32[4,280,256]{2,1,0:T(8,128)S(1)} all-to-all(f32[4,280,256]{2,1,0:T(8,128)S(1)} %bitcast.14), channel_id=1, replica_groups=mesh['frames'=4,'z'=8,'y'=4,'core'=2] {'y'}, dimensions={0} | all-to-all | bytes 2293760 | tf_op jit(solution)/shard_map/all_to_all | solution.py:144
  34.4 18.3 %all_to_all.41 = f32[8,40,256]{2,1,0:T(8,128)S(1)} all-to-all(f32[8,40,256]{2,1,0:T(8,128)S(1)} %bitcast.16), channel_id=1, replica_groups=mesh['frames'=4,'z'=8,'y'=4,'core'=2] {'z'}, dimensions={0} | all-to-all | bytes 655360 | tf_op jit(solution)/shard_map/all_to_all | solution.py:144
  54.1 2.4 %collective-permute-start.2 = (f32[40,128]{1,0:T(8,128)S(1)}, f32[40,128]{1,0:T(8,128)S(1)}, u32[]{:S(2)}, u32[]{:S(2)}) collective-permute-start(f32[40,128]{1,0:T(8,128)S(1)} %slice_add_fusion.1), channel_id=1, source_target_pairs={{0,128},{64,192},{128,0},{192,64},{1,129},{65,193},{129,1},{193,65... | collective-permute-start | bytes 61448 | tf_op jit(solution)/shard_map/ppermute | solution.py:161
  59.2 13.3 %all_to_all.42 = f32[8,40,256]{2,1,0:T(8,128)S(1)} all-to-all(f32[8,40,256]{2,1,0:T(8,128)S(1)} %broadcast_in_dim.38), channel_id=1, replica_groups=mesh['frames'=4,'z'=8,'y'=4,'core'=2] {'z'}, dimensions={0} | all-to-all | bytes 655360 | tf_op jit(solution)/shard_map/all_to_all | solution.py:144
  72.6 13.5 %all_to_all.43 = f32[4,280,256]{2,1,0:T(8,128)} all-to-all(f32[4,280,256]{2,1,0:T(8,128)S(1)} %broadcast_in_dim.40), channel_id=1, replica_groups=mesh['frames'=4,'z'=8,'y'=4,'core'=2] {'y'}, dimensions={0} | all-to-all | bytes 2293760 | tf_op jit(solution)/shard_map/all_to_all | solution.py:144
  86.1 6.8 %collective-permute-start.4 = (f32[1120,256]{1,0:T(8,128)}, f32[1120,256]{1,0:T(8,128)}, u32[]{:S(2)}, u32[]{:S(2)}) collective-permute-start(f32[1120,256]{1,0:T(8,128)} %bitcast.4.mine_ref), channel_id=1, source_target_pairs={{0,1},{1,0},{2,3},{3,2},{4,5},{5,4},{6,7},{7,6},{8,9},{9,8},{10,11... | collective-permute-start | bytes 3440648 | tf_op jit(solution)/shard_map/ppermute | solution.py:140
  92.9 1.6 copy.19.query_ref
  94.4 2.4 %copy.20.cot_ref = bf16[256,2240]{1,0:T(8,128)(2,1)} copy(bf16[256,2240]{0,1:T(8,128)(2,1)} %param.8) | data formatting | bytes 2293760 | tf_op args[3]
  98.1 21.9 %shard_map.77 = (bf16[256,2240]{1,0:T(8,128)(2,1)S(1)}, f32[1120,256]{1,0:T(8,128)S(1)}, f32[1120,256]{1,0:T(8,128)S(1)}) custom-call(s32[2,128]{1,0:T(2,128)S(1)} %bitcast.12, bf16[256,2240]{1,0:T(8,128)(2,1)S(1)} %copy.19.query_ref, bf16[256,2240]{1,0:T(8,128)(2,1)S(1)} %copy-done, f32[1120,256]{1,0:T(8,128)} %bitcast.4.mine_ref, ...), custom_call_target="tpu_custom_call" | custom-call | tf_op jit(solution)/shard_map/pallas_call | solution.py:132
  120.1 2.8 %collective-permute-done.5 = f32[1120,256]{1,0:T(8,128)S(1)} collective-permute-done((f32[1120,256]{1,0:T(8,128)S(1)}, f32[1120,256]{1,0:T(8,128)S(1)}, u32[]{:S(2)}, u32[]{:S(2)}) %collective-permute-start.5) | collective-permute-done | bytes 1146912 | tf_op jit(solution)/shard_map/ppermute | solution.py:140
  123.1 18.6 %all_to_all.44 = f32[4,280,256]{2,1,0:T(8,128)S(1)} all-to-all(f32[4,280,256]{2,1,0:T(8,128)S(1)} %bitcast.15), channel_id=1, replica_groups=mesh['frames'=4,'z'=8,'y'=4,'core'=2] {'y'}, dimensions={0} | all-to-all | bytes 2293760 | tf_op jit(solution)/shard_map/all_to_all | solution.py:144
  143.4 14.1 %all_to_all.45 = f32[8,40,256]{2,1,0:T(8,128)S(1)} all-to-all(f32[8,40,256]{2,1,0:T(8,128)S(1)} %bitcast.17), channel_id=1, replica_groups=mesh['frames'=4,'z'=8,'y'=4,'core'=2] {'z'}, dimensions={0} | all-to-all | bytes 655360 | tf_op jit(solution)/shard_map/all_to_all | solution.py:144
  157.5 2.4 %collective-permute-start.6 = (f32[40,128]{1,0:T(8,128)S(1)}, f32[40,128]{1,0:T(8,128)S(1)}, u32[]{:S(2)}, u32[]{:S(2)}) collective-permute-start(f32[40,128]{1,0:T(8,128)S(1)} %slice_add_fusion), channel_id=1, source_target_pairs={{0,192},{64,0},{128,64},{192,128},{1,193},{65,1},{129,65},{193,129... | collective-permute-start | bytes 61448 | tf_op jit(solution)/shard_map/ppermute | solution.py:161
  160.8 3.2 %collective-permute-done.7 = f32[40,128]{1,0:T(8,128)S(1)} collective-permute-done((f32[40,128]{1,0:T(8,128)S(1)}, f32[40,128]{1,0:T(8,128)S(1)}, u32[]{:S(2)}, u32[]{:S(2)}) %collective-permute-start.7) | collective-permute-done | bytes 20512 | tf_op jit(solution)/shard_map/ppermute | solution.py:161
  164.1 12.9 %all_to_all.46 = f32[8,40,256]{2,1,0:T(8,128)S(1)} all-to-all(f32[8,40,256]{2,1,0:T(8,128)S(1)} %broadcast_in_dim.41), channel_id=1, replica_groups=mesh['frames'=4,'z'=8,'y'=4,'core'=2] {'z'}, dimensions={0} | all-to-all | bytes 655360 | tf_op jit(solution)/shard_map/all_to_all | solution.py:144
  177.1 13.7 %all_to_all.47 = f32[4,280,256]{2,1,0:T(8,128)S(1)} all-to-all(f32[4,280,256]{2,1,0:T(8,128)S(1)} %broadcast_in_dim.43), channel_id=1, replica_groups=mesh['frames'=4,'z'=8,'y'=4,'core'=2] {'y'}, dimensions={0} | all-to-all | bytes 2293760 | tf_op jit(solution)/shard_map/all_to_all | solution.py:144
  190.8 5.8 %collective-permute-start.9 = (f32[1120,256]{1,0:T(8,128)S(1)}, f32[1120,256]{1,0:T(8,128)}, u32[]{:S(2)}, u32[]{:S(2)}) collective-permute-start(f32[1120,256]{1,0:T(8,128)S(1)} %bitcast.9), channel_id=1, source_target_pairs={{0,1},{1,0},{2,3},{3,2},{4,5},{5,4},{6,7},{7,6},{8,9},{9,8},{10,11... | collective-permute-start | bytes 3440648 | tf_op jit(solution)/shard_map/ppermute | solution.py:140
  196.6 2.4 %copy.23 = bf16[256,2240]{0,1:T(8,128)(2,1)} copy(bf16[256,2240]{1,0:T(8,128)(2,1)} %copy-done.1) | data formatting | bytes 2293760
  199.2 4.5 %shard_map.78 = (bf16[256,2240]{1,0:T(8,128)(2,1)S(1)}, bf16[256,2240]{1,0:T(8,128)(2,1)S(1)}) custom-call(s32[2,128]{1,0:T(2,128)S(1)} %bitcast.13, bf16[256,2240]{1,0:T(8,128)(2,1)S(1)} %copy.17.key_ref, bf16[256,2240]{1,0:T(8,128)(2,1)S(1)} %copy.18.value_ref, f32[1120,256]{1,0:T(8,128)S(1)} %bitcast.10, f32[1120,256]{1,0:T(8,128)} %collective-permute-done.9.other_ref), custom_call_target="tpu_custom_call" | custom-call | tf_op jit(solution)/shard_map/pallas_call | solution.py:132
  205.7 2.5 %copy.24 = bf16[256,2240]{0,1:T(8,128)(2,1)} copy(bf16[256,2240]{1,0:T(8,128)(2,1)} %copy-done.4) | data formatting | bytes 2293760
  (50 shorter events, 14.8 us)
Async XLA Ops:
  0.6 1.7 copy-start.6
  2.3 0.7 copy-start.5
  8.8 5.7 %collective-permute-start = (f32[1120,256]{1,0:T(8,128)S(1)}, f32[1120,256]{1,0:T(8,128)S(1)}, u32[]{:S(2)}, u32[]{:S(2)}) collective-permute-start(f32[1120,256]{1,0:T(8,128)S(1)} %get-tuple-element.11), channel_id=1, source_target_pairs={{0,1},{1,0},{2,3},{3,2},{4,5},{5,4},{6,7},{7,6},{8,9},{9,8},{10,11... | collective-permute-start | bytes 3440648 | tf_op jit(solution)/shard_map/ppermute | solution.py:140
  52.8 4.9 %collective-permute-start.1 = (f32[40,128]{1,0:T(8,128)S(1)}, f32[40,128]{1,0:T(8,128)S(1)}, u32[]{:S(2)}, u32[]{:S(2)}) collective-permute-start(f32[40,128]{1,0:T(8,128)S(1)} %slice_add_fusion.1), channel_id=1, source_target_pairs={{0,64},{64,128},{128,192},{192,0},{1,65},{65,129},{129,193},{193,1... | collective-permute-start | bytes 61448 | tf_op jit(solution)/shard_map/ppermute | solution.py:161
  54.1 4.1 %collective-permute-start.2 = (f32[40,128]{1,0:T(8,128)S(1)}, f32[40,128]{1,0:T(8,128)S(1)}, u32[]{:S(2)}, u32[]{:S(2)}) collective-permute-start(f32[40,128]{1,0:T(8,128)S(1)} %slice_add_fusion.1), channel_id=1, source_target_pairs={{0,128},{64,192},{128,0},{192,64},{1,129},{65,193},{129,1},{193,65... | collective-permute-start | bytes 61448 | tf_op jit(solution)/shard_map/ppermute | solution.py:161
  56.5 2.6 %collective-permute-start.3 = (f32[40,128]{1,0:T(8,128)S(1)}, f32[40,128]{1,0:T(8,128)S(1)}, u32[]{:S(2)}, u32[]{:S(2)}) collective-permute-start(f32[40,128]{1,0:T(8,128)S(1)} %slice_add_fusion.1), channel_id=1, source_target_pairs={{0,192},{64,0},{128,64},{192,128},{1,193},{65,1},{129,65},{193,129... | collective-permute-start | bytes 61448 | tf_op jit(solution)/shard_map/ppermute | solution.py:161
  86.1 10.8 %collective-permute-start.4 = (f32[1120,256]{1,0:T(8,128)}, f32[1120,256]{1,0:T(8,128)}, u32[]{:S(2)}, u32[]{:S(2)}) collective-permute-start(f32[1120,256]{1,0:T(8,128)} %bitcast.4.mine_ref), channel_id=1, source_target_pairs={{0,1},{1,0},{2,3},{3,2},{4,5},{5,4},{6,7},{7,6},{8,9},{9,8},{10,11... | collective-permute-start | bytes 3440648 | tf_op jit(solution)/shard_map/ppermute | solution.py:140
  96.8 1.3 copy-start
  120.0 3.1 %copy-start.1 = (bf16[256,2240]{1,0:T(8,128)(2,1)}, bf16[256,2240]{1,0:T(8,128)(2,1)S(1)}, u32[]{:S(2)}) copy-start(bf16[256,2240]{1,0:T(8,128)(2,1)S(1)} %get-tuple-element.20) | copy-start | bytes 3440644
  120.0 2.9 %collective-permute-start.5 = (f32[1120,256]{1,0:T(8,128)S(1)}, f32[1120,256]{1,0:T(8,128)S(1)}, u32[]{:S(2)}, u32[]{:S(2)}) collective-permute-start(f32[1120,256]{1,0:T(8,128)S(1)} %get-tuple-element.14), channel_id=1, source_target_pairs={{0,1},{1,0},{2,3},{3,2},{4,5},{5,4},{6,7},{7,6},{8,9},{9,8},{10,11... | collective-permute-start | bytes 3440648 | tf_op jit(solution)/shard_map/ppermute | solution.py:140
  157.5 3.3 %collective-permute-start.6 = (f32[40,128]{1,0:T(8,128)S(1)}, f32[40,128]{1,0:T(8,128)S(1)}, u32[]{:S(2)}, u32[]{:S(2)}) collective-permute-start(f32[40,128]{1,0:T(8,128)S(1)} %slice_add_fusion), channel_id=1, source_target_pairs={{0,192},{64,0},{128,64},{192,128},{1,193},{65,1},{129,65},{193,129... | collective-permute-start | bytes 61448 | tf_op jit(solution)/shard_map/ppermute | solution.py:161
  159.9 4.1 %collective-permute-start.7 = (f32[40,128]{1,0:T(8,128)S(1)}, f32[40,128]{1,0:T(8,128)S(1)}, u32[]{:S(2)}, u32[]{:S(2)}) collective-permute-start(f32[40,128]{1,0:T(8,128)S(1)} %slice_add_fusion), channel_id=1, source_target_pairs={{0,128},{64,192},{128,0},{192,64},{1,129},{65,193},{129,1},{193,65... | collective-permute-start | bytes 61448 | tf_op jit(solution)/shard_map/ppermute | solution.py:161
  159.9 4.1 %collective-permute-start.8 = (f32[40,128]{1,0:T(8,128)S(1)}, f32[40,128]{1,0:T(8,128)S(1)}, u32[]{:S(2)}, u32[]{:S(2)}) collective-permute-start(f32[40,128]{1,0:T(8,128)S(1)} %slice_add_fusion), channel_id=1, source_target_pairs={{0,64},{64,128},{128,192},{192,0},{1,65},{65,129},{129,193},{193,1... | collective-permute-start | bytes 61448 | tf_op jit(solution)/shard_map/ppermute | solution.py:161
  190.8 8.4 %collective-permute-start.9 = (f32[1120,256]{1,0:T(8,128)S(1)}, f32[1120,256]{1,0:T(8,128)}, u32[]{:S(2)}, u32[]{:S(2)}) collective-permute-start(f32[1120,256]{1,0:T(8,128)S(1)} %bitcast.9), channel_id=1, source_target_pairs={{0,1},{1,0},{2,3},{3,2},{4,5},{5,4},{6,7},{7,6},{8,9},{9,8},{10,11... | collective-permute-start | bytes 3440648 | tf_op jit(solution)/shard_map/ppermute | solution.py:140
  203.7 1.0 copy-start.2
  204.7 1.0 copy-start.4
  205.7 2.5 %copy-start.3 = (bf16[256,2240]{1,0:T(8,128)(2,1)S(1)}, bf16[256,2240]{1,0:T(8,128)(2,1)}, u32[]{:S(2)}) copy-start(bf16[256,2240]{1,0:T(8,128)(2,1)} %copy-done.2) | copy-start | bytes 3440644

commit v2 on v1

v2 whole, which is shorter than its diff:
```python
import jax
import jax.numpy as jnp
from jax import lax
from jax.experimental import pallas as pl
from jax.experimental.pallas import tpu as pltpu
from jax.sharding import PartitionSpec as P

H = 20
E = 112
LANES = 128
CORES = 2
HALF = H // CORES
ROWS = HALF * E
STATE_ROWS = 1152
WIDE = 2 * LANES
F32 = jnp.float32
BF16 = jnp.bfloat16
VMEM_LIMIT = 32 * 1024 * 1024
Y = 4


def frame_masks(ids_ref):
    early = ids_ref[...] == 0
    first = early.astype(F32)
    return early, first.astype(BF16), (1.0 - first).astype(BF16)


def by_frame(rows, first, second):
    return jnp.concatenate([rows * first, rows * second], axis=0)


def split(values):
    high = values.astype(BF16)
    return high, (values - high.astype(F32)).astype(BF16)


def with_ones(rows):
    return jnp.concatenate([rows, jnp.ones((LANES - E, rows.shape[1]), rows.dtype)], axis=0)


def with_rows(rows, *extra):
    at = lax.broadcasted_iota(jnp.int32, (LANES - E, rows.shape[1]), 0)
    tail = jnp.zeros((LANES - E, rows.shape[1]), F32)
    for place, row in enumerate(extra):
        tail = jnp.where(at == place, row, tail)
    return jnp.concatenate([rows, tail.astype(rows.dtype)], axis=0)


def over_tokens(left, right):
    return lax.dot_general(left, right, (((1,), (1,)), ((), ())), preferred_element_type=F32)


def over_columns(left, right):
    return jnp.dot(left, right, preferred_element_type=F32)


def over_rows(left, right):
    return lax.dot_general(left, right, (((0,), (0,)), ((), ())), preferred_element_type=F32)


def stacked(state, rows):
    return jnp.concatenate(split(state), axis=0), jnp.concatenate([rows, rows], axis=0)


def own_frame(both, early):
    return jnp.where(early, both[:LANES], both[LANES:])


def fill_up(state_ref):
    state_ref[ROWS:, :] = jnp.zeros((STATE_ROWS - ROWS, WIDE), F32)


def key_state(key, value, first, second):
    return over_tokens(jnp.maximum(key, 0), by_frame(with_ones(value), first, second))


def key_kernel(half_ref, ids_ref, key_ref, value_ref, state_ref):
    _, first, second = frame_masks(ids_ref)
    for h in range(HALF):
        rows = pl.ds(h * E, E)
        state_ref[rows, :] = key_state(key_ref[rows, :], value_ref[rows, :], first, second)
    fill_up(state_ref)


def query_kernel(half_ref, ids_ref, query_ref, cot_ref, state_ref, aux_ref, grad_state_ref):
    early, first, second = frame_masks(ids_ref)
    for h in range(HALF):
        rows = pl.ds(h * E, E)
        phi = jnp.maximum(query_ref[rows, :], 0)
        numer = own_frame(over_rows(*stacked(state_ref[rows, :], phi)), early)
        inverse = 1.0 / (numer[E : E + 1] + 1.0)
        wide = cot_ref[rows, :].astype(F32)
        inner = -jnp.sum(wide * numer[:E], axis=0, keepdims=True) * inverse
        aux_ref[h] = jnp.concatenate([inverse, inner], axis=0)
    for h in range(HALF):
        rows = pl.ds(h * E, E)
        inverse, inner = aux_ref[h, 0:1, :], aux_ref[h, 1:2, :]
        phi = by_frame(jnp.maximum(query_ref[rows, :], 0), first, second)
        wide = cot_ref[rows, :].astype(F32)
        high, low = split(with_rows(wide * inverse, inner * inverse))
        block = over_tokens(phi, high) + over_tokens(phi, low)
        grad_state_ref[rows, :] = jnp.concatenate([block[:E], block[E:]], axis=1)
    fill_up(grad_state_ref)


def query_grad_kernel(half_ref, ids_ref, query_ref, cot_ref, state_ref, aux_ref, *refs):
    grad_ref = refs[-1]
    _, first, second = frame_masks(ids_ref)
    for h in range(HALF):
        rows = pl.ds(h * E, E)
        high, low = split(state_ref[rows, :])
        inverse, inner = aux_ref[h, 0:1, :], aux_ref[h, 1:2, :]
        inner_high = inner.astype(BF16).astype(F32)
        inner_mid = (inner - inner_high).astype(BF16).astype(F32)
        inner_low = inner - inner_high - inner_mid
        cots = with_rows(cot_ref[rows, :], inner_high, inner_mid, inner_low)
        cots = by_frame(cots, first, second)
        grad = (over_columns(high, cots) + over_columns(low, cots)) * inverse
        grad_ref[rows, :] = jnp.where(query_ref[rows, :].astype(F32) > 0, grad, 0.0).astype(BF16)


def value_kernel(half_ref, ids_ref, key_ref, value_ref, state_ref, *refs):
    grad_key_ref, grad_value_ref = refs[-2:]
    early, first, second = frame_masks(ids_ref)
    for h in range(HALF):
        rows = pl.ds(h * E, E)
        state = state_ref[rows, :]
        high, low = split(state)
        key = key_ref[rows, :]
        grad = own_frame(over_rows(*stacked(state, jnp.maximum(key, 0))), early)
        grad_value_ref[rows, :] = grad[:E].astype(BF16)
        values = by_frame(with_ones(value_ref[rows, :]), first, second)
        grad = over_columns(high, values) + over_columns(low, values)
        grad_key_ref[rows, :] = jnp.where(key.astype(F32) > 0, grad, 0.0).astype(BF16)


def gather_kernel(parts_ref, sum_ref):
    rows, pieces, piece = parts_ref.shape[1], sum_ref.shape[0], sum_ref.shape[1]
    for at in range(pieces):
        filled = min(piece, rows - at * piece)
        if filled > 0:
            here = pl.ds(at * piece, filled)
            total = parts_ref[0, here, :]
            for part in range(1, parts_ref.shape[0]):
                total = total + parts_ref[part, here, :]
            sum_ref[at, :filled, :] = total
        if filled < piece:
            start = max(filled, 0)
            sum_ref[at, start:, :] = jnp.zeros((piece - start, WIDE), F32)


def params():
    return pltpu.CompilerParams(vmem_limit_bytes=VMEM_LIMIT)


def on_half(kernel, half, ids, halves, small, whole, outs):
    tokens = ids.shape[1]
    block = pl.BlockSpec((ROWS, tokens), lambda i, at: (at[0], 0))
    full = lambda shape: pl.BlockSpec(shape, lambda i, at: (0,) * len(shape))
    operands = [ids, *halves, *small, *whole]
    specs = [full(ids.shape)] + [block] * len(halves) + [full(a.shape) for a in small]
    specs += [pl.BlockSpec(memory_space=pl.ANY)] * len(whole)
    aliases = {1 + len(operands) - len(whole) + at: at for at in range(len(whole))}
    shapes = {
        "grad": ((H * E, tokens), BF16),
        "state": ((STATE_ROWS, WIDE), F32),
        "aux": ((HALF, 2, tokens), F32),
    }
    out_shape = [jax.ShapeDtypeStruct(*shapes[out]) for out in outs]
    out_specs = [block if out == "grad" else full(shapes[out][0]) for out in outs]
    return pl.pallas_call(
        kernel,
        out_shape=out_shape,
        grid_spec=pltpu.PrefetchScalarGridSpec(
            num_scalar_prefetch=1, grid=(1,), in_specs=specs, out_specs=out_specs
        ),
        input_output_aliases=aliases,
        compiler_params=params(),
        cost_estimate=pl.CostEstimate(
            flops=2 * 6 * ROWS * WIDE * tokens, bytes_accessed=4 * ROWS * tokens * 2, transcendentals=0
        ),
    )(half, *operands)


def swap_cores(block):
    return lax.ppermute(block, "space", [(i, i ^ 1) for i in range(lax.axis_size("space"))])


def groups(chips_z):
    device = lambda z, y, core: (z * Y + y) * CORES + core
    pairs = range(chips_z // 2)
    near = [
        [device(2 * pair + i, y, core) for i in range(2) for y in range(Y)]
        for core in range(CORES) for pair in pairs
    ]
    far = [
        [device(2 * pair + i, y, core) for pair in pairs]
        for core in range(CORES) for i in range(2) for y in range(Y)
    ]
    return near, far


def exchange(block, members):
    return lax.all_to_all(block, "space", 0, 0, axis_index_groups=members, tiled=False)


def carried(summed, backward, beside=None):
    frames = lax.axis_size("frames")
    near, far = groups(lax.axis_size("space") // (Y * CORES))
    chips, places = len(near[0]), len(far[0])
    rows = summed.shape[0] // chips
    part = -(-rows // (8 * places)) * 8
    summed = exchange(summed.reshape(chips, rows, WIDE), near)
    summed = pl.pallas_call(
        gather_kernel,
        out_shape=jax.ShapeDtypeStruct((places, part, WIDE), F32),
        compiler_params=params(),
    )(summed)
    summed = jnp.sum(exchange(summed, far), axis=0)
    frame0, frame1 = summed[:, :LANES], summed[:, LANES:]
    total = frame0 + frame1
    me = lax.axis_index("frames")
    carry = jnp.zeros_like(total)
    arrived = []
    for hop in range(1, frames):
        step = -hop if backward else hop
        arrived.append(
            lax.ppermute(total, "frames", [(i, (i + step) % frames) for i in range(frames)])
        )
    extra = None
    if beside is not None:
        extra = beside(total)
        arrived, extra = lax.optimization_barrier((arrived, extra))
    for hop, moved in enumerate(arrived, 1):
        reaches = (me + hop < frames) if backward else (me >= hop)
        carry = carry + jnp.where(reaches, moved, 0.0)
    if backward:
        done = jnp.concatenate([carry + total, carry + frame1], axis=1)
    else:
        done = jnp.concatenate([carry + frame0, carry + total], axis=1)
    done = exchange(jnp.broadcast_to(done[None], (places,) + done.shape), far)
    done = done.reshape(places * part, WIDE)[:rows]
    done = exchange(jnp.broadcast_to(done[None], (chips,) + done.shape), near)
    return done.reshape(chips * rows, WIDE), extra


def on_device(queries, key_inputs, value_inputs, out_cotangent, frame_ids):
    ids = frame_ids.reshape(1, -1)
    query, key, value, cot = (a.T for a in (queries, key_inputs, value_inputs, out_cotangent))
    core = (lax.axis_index("space") % CORES).astype(jnp.int32).reshape(1)
    there = 1 - core
    (send,) = on_half(key_kernel, there, ids, (key, value), (), (), ("state",))
    received = swap_cores(send)
    (keep,) = on_half(key_kernel, core, ids, (key, value), (), (), ("state",))
    mine, _ = carried(keep + received, False)
    other = swap_cores(mine)
    aux_mine, keep = on_half(query_kernel, core, ids, (query, cot), (mine,), (), ("aux", "state"))
    aux, send = on_half(query_kernel, there, ids, (query, cot), (other,), (), ("aux", "state"))
    received = swap_cores(send)
    late, _ = lax.optimization_barrier((other, send))
    grads = on_half(query_grad_kernel, there, ids, (query, cot), (late, aux), (), ("grad",))
    received, grads = lax.optimization_barrier((received, grads))

    def beside(total):
        late, _ = lax.optimization_barrier((aux_mine, total))
        return on_half(query_grad_kernel, core, ids, (query, cot), (mine, late), grads, ("grad",))

    mine, (grad_query,) = carried(keep + received, True, beside)
    other = swap_cores(mine)
    grads = on_half(value_kernel, core, ids, (key, value), (mine,), (), ("grad", "grad"))
    grad_key, grad_value = on_half(
        value_kernel, there, ids, (key, value), (other,), grads, ("grad", "grad")
    )
    return grad_query.T, grad_key.T, grad_value.T


def solution(mesh):
    rows = P(("frames", "space"), None)
    return jax.shard_map(
        on_device,
        mesh=mesh,
        in_specs=(rows, rows, rows, rows, P(("frames", "space"))),
        out_specs=(rows, rows, rows),
        check_vma=False,
    )
```

time: 210 us -> 167 us (0.80)
  Pallas kernels: 32.1 us -> 10.2 us
  blocking collectives: 122 us -> 105 us
  local copies, waits for them, and re-layouts: 18 us -> 5.39 us
  waiting for transfers between devices: 10.4 us -> 15.8 us
  starting transfers between devices: 24 us -> 27.9 us
    pallas_call x3 -> x10, Pallas kernels: 32.1 us -> 10.2 us  [the longest x8 10.1 us: on_half(): pl.pallas_call(kernel, out_shape=out_shape, grid_spec=pltpu.PrefetchScala...]
    all_to_all x8 -> x7, blocking collectives: 122 us -> 105 us  [exchange(): lax.all_to_all(block, 'space', 0, 0, axis_index_groups=members, tiled=False)]
    unnamed x21 -> x22, local copies, waits for them, and re-layouts: 15.9 us -> 5.15 us
    all_to_all x0 -> x1, waiting for transfers between devices: none -> 7.56 us  [exchange(): lax.all_to_all(block, 'space', 0, 0, axis_index_groups=members, tiled=False)]
    all_to_all x0 -> x1, starting transfers between devices: none -> 3.98 us  [exchange(): lax.all_to_all(block, 'space', 0, 0, axis_index_groups=members, tiled=False)]
  transfers between devices with their start and end apart: 10 -> 11, of which waited for: 7 -> 6; matrix products, arithmetic and copies ran while one was open for 3% -> 0% of each run, Pallas kernels for 0% -> 4%
where the time goes in v2:
time: 167 us; the launch traced here: 166 us
  blocking collectives  105 us (63%)
  starting transfers between devices  27.9 us (17%)
  waiting for transfers between devices  15.8 us (9%)
  Pallas kernels  10.2 us (6%)
  local copies, waits for them, and re-layouts  5.39 us (3%)
    all_to_all x7, blocking collectives, exchange(): lax.all_to_all(block, 'space', 0, 0, axis_index_groups=members, tiled=False)  105 us
    ppermute x4, starting transfers between devices, swap_cores(): lax.ppermute(block, 'space', [(i, i ^ 1) for i in range(lax.axis_size('sp...  16.9 us
    pallas_call x8, Pallas kernels, on_half(): pl.pallas_call(kernel, out_shape=out_shape, grid_spec=pltpu.PrefetchScala...  10.1 us
    all_to_all x1, waiting for transfers between devices, exchange(): lax.all_to_all(block, 'space', 0, 0, axis_index_groups=members, tiled=False)  7.56 us
    ppermute x6, starting transfers between devices, carried(): lax.ppermute(total, 'frames', [(i, (i + step) % frames) for i in range(fr...  7.07 us
    unnamed x22, local copies, waits for them, and re-layouts  5.15 us
    ppermute x4, waiting for transfers between devices, swap_cores(): lax.ppermute(block, 'space', [(i, i ^ 1) for i in range(lax.axis_size('sp...  5.02 us
    all_to_all x1, starting transfers between devices, exchange(): lax.all_to_all(block, 'space', 0, 0, axis_index_groups=members, tiled=False)  3.98 us
  transfers between devices with their start and end apart: 11, of which 6 were waited for; matrix products, arithmetic and copies ran while one was open for 0% of the time, Pallas kernels for 4%

profile of v2, /device:TPU:1, one launch (start us, length us, event | category | flops | bytes accessed | tf_op | source)
XLA Modules:
  0.0 166.4 jit_solution(1901185619384292818)
XLA Ops:
  1.9 1.3 copy-done.2
  4.4 3.3 %collective-permute-start = (f32[1152,256]{1,0:T(8,128)S(1)}, f32[1152,256]{1,0:T(8,128)S(1)}, u32[]{:S(2)}, u32[]{:S(2)}) collective-permute-start(f32[1152,256]{1,0:T(8,128)S(1)} %shard_map.77), channel_id=1, source_target_pairs={{0,1},{1,0},{2,3},{3,2},{4,5},{5,4},{6,7},{7,6},{8,9},{9,8},{10,11... | collective-permute-start | bytes 3538952 | tf_op jit(solution)/shard_map/ppermute | solution.py:186
  8.3 1.9 %collective-permute-done = f32[1152,256]{1,0:T(8,128)S(1)} collective-permute-done((f32[1152,256]{1,0:T(8,128)S(1)}, f32[1152,256]{1,0:T(8,128)S(1)}, u32[]{:S(2)}, u32[]{:S(2)}) %collective-permute-start) | collective-permute-done | bytes 1179680 | tf_op jit(solution)/shard_map/ppermute | solution.py:186
  10.3 19.8 %all_to_all.40.parts_ref = f32[8,144,256]{2,1,0:T(8,128)S(1)} all-to-all(f32[8,144,256]{2,1,0:T(8,128)S(1)} %bitcast.44), channel_id=1, replica_groups={{0,2,4,6,8,10,12,14},{16,18,20,22,24,26,28,30},{32,34,36,38,40,42,44,46..., dimensions={0} | all-to-all | bytes 2359296 | tf_op jit(solution)/shard_map/all_to_all | solution.py:204
  30.2 14.5 %all_to_all.41 = f32[4,40,256]{2,1,0:T(8,128)S(1)} all-to-all(f32[4,40,256]{2,1,0:T(8,128)S(1)} %shard_map.78), channel_id=1, replica_groups={{0,16,32,48},{2,18,34,50},{4,20,36,52},{6,22,38,54},{8,24,40,56},{10,26..., dimensions={0} | all-to-all | bytes 327680 | tf_op jit(solution)/shard_map/all_to_all | solution.py:204
  44.7 2.6 %collective-permute-start.3 = (f32[40,128]{1,0:T(8,128)S(1)}, f32[40,128]{1,0:T(8,128)S(1)}, u32[]{:S(2)}, u32[]{:S(2)}) collective-permute-start(f32[40,128]{1,0:T(8,128)S(1)} %slice_add_fusion.1), channel_id=1, source_target_pairs={{0,192},{64,0},{128,64},{192,128},{1,193},{65,1},{129,65},{193,129... | collective-permute-start | bytes 61448 | tf_op jit(solution)/shard_map/ppermute | solution.py:228
  48.4 3.0 %collective-permute-done.2 = f32[40,128]{1,0:T(8,128)S(1)} collective-permute-done((f32[40,128]{1,0:T(8,128)S(1)}, f32[40,128]{1,0:T(8,128)S(1)}, u32[]{:S(2)}, u32[]{:S(2)}) %collective-permute-start.2) | collective-permute-done | bytes 20512 | tf_op jit(solution)/shard_map/ppermute | solution.py:228
  51.7 10.0 %all_to_all.42 = f32[4,40,256]{2,1,0:T(8,128)S(1)} all-to-all(f32[4,40,256]{2,1,0:T(8,128)S(1)} %broadcast_in_dim.34), channel_id=1, replica_groups={{0,16,32,48},{2,18,34,50},{4,20,36,52},{6,22,38,54},{8,24,40,56},{10,26..., dimensions={0} | all-to-all | bytes 327680 | tf_op jit(solution)/shard_map/all_to_all | solution.py:204
  61.8 14.1 %all_to_all.43 = f32[8,144,256]{2,1,0:T(8,128)S(1)} all-to-all(f32[8,144,256]{2,1,0:T(8,128)S(1)} %broadcast_in_dim.35), channel_id=1, replica_groups={{0,2,4,6,8,10,12,14},{16,18,20,22,24,26,28,30},{32,34,36,38,40,42,44,46..., dimensions={0} | all-to-all | bytes 2359296 | tf_op jit(solution)/shard_map/all_to_all | solution.py:204
  75.9 8.0 %collective-permute-start.4 = (f32[1152,256]{1,0:T(8,128)S(1)}, f32[1152,256]{1,0:T(8,128)S(1)}, u32[]{:S(2)}, u32[]{:S(2)}) collective-permute-start(f32[1152,256]{1,0:T(8,128)S(1)} %bitcast.31), channel_id=1, source_target_pairs={{0,1},{1,0},{2,3},{3,2},{4,5},{5,4},{6,7},{7,6},{8,9},{9,8},{10,11... | collective-permute-start | bytes 3538952 | tf_op jit(solution)/shard_map/ppermute | solution.py:186
  83.9 2.5 %collective-permute-done.4.state_ref = f32[1152,256]{1,0:T(8,128)S(1)} collective-permute-done((f32[1152,256]{1,0:T(8,128)S(1)}, f32[1152,256]{1,0:T(8,128)S(1)}, u32[]{:S(2)}, u32[]{:S(2)}) %collective-permute-start.4) | collective-permute-done | bytes 1179680 | tf_op jit(solution)/shard_map/ppermute | solution.py:186
  89.4 1.4 shard_map.81.refs_0_
  90.9 18.7 %all_to_all.44.parts_ref = f32[8,144,256]{2,1,0:T(8,128)S(1)} all-to-all(f32[8,144,256]{2,1,0:T(8,128)S(1)} %bitcast.45), channel_id=1, replica_groups={{0,2,4,6,8,10,12,14},{16,18,20,22,24,26,28,30},{32,34,36,38,40,42,44,46..., dimensions={0} | all-to-all | bytes 2359296 | tf_op jit(solution)/shard_map/all_to_all | solution.py:204
  110.3 4.0 %all-to-all-start.5 = ((f32[4,40,256]{2,1,0:T(8,128)}), f32[4,40,256]{2,1,0:T(8,128)}, u32[]{:S(2)}, u32[]{:S(2)}) async-start(f32[4,40,256]{2,1,0:T(8,128)} %copy-done.8), calls=%async_computation.5 | async-start | bytes 327680 | tf_op jit(solution)/shard_map/all_to_all | solution.py:204
  114.3 7.6 %all-to-all-done.5 = f32[4,40,256]{2,1,0:T(8,128)} async-done(((f32[4,40,256]{2,1,0:T(8,128)}), f32[4,40,256]{2,1,0:T(8,128)}, u32[]{:S(2)}, u32[]{:S(2)}) %all-to-all-start.5) | async-done | bytes 163872 | tf_op jit(solution)/shard_map/all_to_all | solution.py:204
  122.9 1.3 collective-permute-start.7
  124.3 2.0 %collective-permute-start.6 = (f32[40,128]{1,0:T(8,128)S(1)}, f32[40,128]{1,0:T(8,128)S(1)}, u32[]{:S(2)}, u32[]{:S(2)}) collective-permute-start(f32[40,128]{1,0:T(8,128)S(1)} %slice_add_fusion), channel_id=1, source_target_pairs={{0,192},{64,0},{128,64},{192,128},{1,193},{65,1},{129,65},{193,129... | collective-permute-start | bytes 61448 | tf_op jit(solution)/shard_map/ppermute | solution.py:228
  126.2 1.3 copy-done.7
  127.5 1.4 shard_map.83
  129.0 9.8 %all_to_all.45 = f32[4,40,256]{2,1,0:T(8,128)S(1)} all-to-all(f32[4,40,256]{2,1,0:T(8,128)S(1)} %broadcast_in_dim.36), channel_id=1, replica_groups={{0,16,32,48},{2,18,34,50},{4,20,36,52},{6,22,38,54},{8,24,40,56},{10,26..., dimensions={0} | all-to-all | bytes 327680 | tf_op jit(solution)/shard_map/all_to_all | solution.py:204
  138.9 18.1 %all_to_all.46 = f32[8,144,256]{2,1,0:T(8,128)S(1)} all-to-all(f32[8,144,256]{2,1,0:T(8,128)S(1)} %broadcast_in_dim.37), channel_id=1, replica_groups={{0,2,4,6,8,10,12,14},{16,18,20,22,24,26,28,30},{32,34,36,38,40,42,44,46..., dimensions={0} | all-to-all | bytes 2359296 | tf_op jit(solution)/shard_map/all_to_all | solution.py:204
  157.0 5.1 %collective-permute-start.9 = (f32[1152,256]{1,0:T(8,128)S(1)}, f32[1152,256]{1,0:T(8,128)S(1)}, u32[]{:S(2)}, u32[]{:S(2)}) collective-permute-start(f32[1152,256]{1,0:T(8,128)S(1)} %bitcast.34), channel_id=1, source_target_pairs={{0,1},{1,0},{2,3},{3,2},{4,5},{5,4},{6,7},{7,6},{8,9},{9,8},{10,11... | collective-permute-start | bytes 3538952 | tf_op jit(solution)/shard_map/ppermute | solution.py:186
  162.1 1.9 %shard_map.84 = (bf16[2240,256]{1,0:T(8,128)(2,1)}, bf16[2240,256]{1,0:T(8,128)(2,1)}) custom-call(s32[1]{0:T(128)} %bitcast.half_ref, s32[1,256]{1,0:T(1,128)S(1)} %bitcast.42, bf16[2240,256]{1,0:T(8,128)(2,1)S(1)} %bitcast.17, bf16[2240,256]{1,0:T(8,128)(2,1)S(1)} %bitcast.21, f32[1152,256]{1,0:T(8,128)S(1)} %bitcast.35), custom_call_target="tpu_custom_call" | custom-call | flops 880803840 | bytes 2293760 | tf_op jit(solution)/shard_map/pallas_call | solution.py:171
  164.6 1.9 %shard_map.85 = (bf16[2240,256]{1,0:T(8,128)(2,1)}, bf16[2240,256]{1,0:T(8,128)(2,1)}) custom-call(s32[1]{0:T(128)S(6)} %sub.3.half_ref, s32[1,256]{1,0:T(1,128)S(1)} %bitcast.43, bf16[2240,256]{1,0:T(8,128)(2,1)S(1)} %bitcast.18, bf16[2240,256]{1,0:T(8,128)(2,1)S(1)} %bitcast.22, ...), custom_call_target="tpu_custom_call", output_to_operand_aliasing={{0}: (5, {}), {1}: (6, {})} | custom-call | flops 880803840 | bytes 2293760 | tf_op jit(solution)/shard_map/pallas_call | solution.py:171
  (55 shorter events, 10.4 us)
Async XLA Ops:
  0.6 1.3 copy-start
  1.9 1.3 copy-start.2
  3.2 0.7 copy-start.9
  3.8 3.9 %copy-start.1 = (bf16[256,2240]{0,1:T(8,128)(2,1)S(1)}, bf16[256,2240]{0,1:T(8,128)(2,1)}, u32[]{:S(2)}) copy-start(bf16[256,2240]{0,1:T(8,128)(2,1)} %param.6) | copy-start | bytes 3440644
  3.8 3.9 %copy-start.10 = (s32[256]{0:T(256)S(1)}, s32[256]{0:T(256)}, u32[]{:S(2)}) copy-start(s32[256]{0:T(256)} %param.9) | copy-start | bytes 3076
  4.4 5.8 %collective-permute-start = (f32[1152,256]{1,0:T(8,128)S(1)}, f32[1152,256]{1,0:T(8,128)S(1)}, u32[]{:S(2)}, u32[]{:S(2)}) collective-permute-start(f32[1152,256]{1,0:T(8,128)S(1)} %shard_map.77), channel_id=1, source_target_pairs={{0,1},{1,0},{2,3},{3,2},{4,5},{5,4},{6,7},{7,6},{8,9},{9,8},{10,11... | collective-permute-start | bytes 3538952 | tf_op jit(solution)/shard_map/ppermute | solution.py:186
  44.7 3.7 %collective-permute-start.3 = (f32[40,128]{1,0:T(8,128)S(1)}, f32[40,128]{1,0:T(8,128)S(1)}, u32[]{:S(2)}, u32[]{:S(2)}) collective-permute-start(f32[40,128]{1,0:T(8,128)S(1)} %slice_add_fusion.1), channel_id=1, source_target_pairs={{0,192},{64,0},{128,64},{192,128},{1,193},{65,1},{129,65},{193,129... | collective-permute-start | bytes 61448 | tf_op jit(solution)/shard_map/ppermute | solution.py:228
  47.3 4.1 %collective-permute-start.2 = (f32[40,128]{1,0:T(8,128)S(1)}, f32[40,128]{1,0:T(8,128)S(1)}, u32[]{:S(2)}, u32[]{:S(2)}) collective-permute-start(f32[40,128]{1,0:T(8,128)S(1)} %slice_add_fusion.1), channel_id=1, source_target_pairs={{0,128},{64,192},{128,0},{192,64},{1,129},{65,193},{129,1},{193,65... | collective-permute-start | bytes 61448 | tf_op jit(solution)/shard_map/ppermute | solution.py:228
  47.8 3.8 %collective-permute-start.1 = (f32[40,128]{1,0:T(8,128)S(1)}, f32[40,128]{1,0:T(8,128)S(1)}, u32[]{:S(2)}, u32[]{:S(2)}) collective-permute-start(f32[40,128]{1,0:T(8,128)S(1)} %slice_add_fusion.1), channel_id=1, source_target_pairs={{0,64},{64,128},{128,192},{192,0},{1,65},{65,129},{129,193},{193,1... | collective-permute-start | bytes 61448 | tf_op jit(solution)/shard_map/ppermute | solution.py:228
  61.8 24.6 %copy-start.4 = (bf16[256,2240]{0,1:T(8,128)(2,1)S(1)}, bf16[256,2240]{0,1:T(8,128)(2,1)}, u32[]{:S(2)}) copy-start(bf16[256,2240]{0,1:T(8,128)(2,1)} %param.5) | copy-start | bytes 3440644
  61.8 24.5 %copy-start.5 = (bf16[256,2240]{0,1:T(8,128)(2,1)S(1)}, bf16[256,2240]{0,1:T(8,128)(2,1)}, u32[]{:S(2)}) copy-start(bf16[256,2240]{0,1:T(8,128)(2,1)} %param.8) | copy-start | bytes 3440644
  75.9 12.2 %copy-start.6 = (f32[8,144,256]{2,1,0:T(8,128)}, f32[8,144,256]{2,1,0:T(8,128)S(1)}, u32[]{:S(2)}) copy-start(f32[8,144,256]{2,1,0:T(8,128)S(1)} %all_to_all.43) | copy-start | bytes 3538948
  75.9 10.4 %collective-permute-start.4 = (f32[1152,256]{1,0:T(8,128)S(1)}, f32[1152,256]{1,0:T(8,128)S(1)}, u32[]{:S(2)}, u32[]{:S(2)}) collective-permute-start(f32[1152,256]{1,0:T(8,128)S(1)} %bitcast.31), channel_id=1, source_target_pairs={{0,1},{1,0},{2,3},{3,2},{4,5},{5,4},{6,7},{7,6},{8,9},{9,8},{10,11... | collective-permute-start | bytes 3538952 | tf_op jit(solution)/shard_map/ppermute | solution.py:186
  87.6 3.1 %collective-permute-start.5 = (f32[1152,256]{1,0:T(8,128)S(1)}, f32[1152,256]{1,0:T(8,128)S(1)}, u32[]{:S(2)}, u32[]{:S(2)}) collective-permute-start(f32[1152,256]{1,0:T(8,128)S(1)} %get-tuple-element.20), channel_id=1, source_target_pairs={{0,1},{1,0},{2,3},{3,2},{4,5},{5,4},{6,7},{7,6},{8,9},{9,8},{10,11... | collective-permute-start | bytes 3538952 | tf_op jit(solution)/shard_map/ppermute | solution.py:186
  109.7 0.7 copy-start.8
  110.3 11.6 %all-to-all-start.5 = ((f32[4,40,256]{2,1,0:T(8,128)}), f32[4,40,256]{2,1,0:T(8,128)}, u32[]{:S(2)}, u32[]{:S(2)}) async-start(f32[4,40,256]{2,1,0:T(8,128)} %copy-done.8), calls=%async_computation.5 | async-start | bytes 327680 | tf_op jit(solution)/shard_map/all_to_all | solution.py:204
  122.8 6.1 %collective-permute-start.8 = (f32[40,128]{1,0:T(8,128)S(1)}, f32[40,128]{1,0:T(8,128)S(1)}, u32[]{:S(2)}, u32[]{:S(2)}) collective-permute-start(f32[40,128]{1,0:T(8,128)S(1)} %slice_add_fusion), channel_id=1, source_target_pairs={{0,64},{64,128},{128,192},{192,0},{1,65},{65,129},{129,193},{193,1... | collective-permute-start | bytes 61448 | tf_op jit(solution)/shard_map/ppermute | solution.py:228
  122.9 6.0 %collective-permute-start.7 = (f32[40,128]{1,0:T(8,128)S(1)}, f32[40,128]{1,0:T(8,128)S(1)}, u32[]{:S(2)}, u32[]{:S(2)}) collective-permute-start(f32[40,128]{1,0:T(8,128)S(1)} %slice_add_fusion), channel_id=1, source_target_pairs={{0,128},{64,192},{128,0},{192,64},{1,129},{65,193},{129,1},{193,65... | collective-permute-start | bytes 61448 | tf_op jit(solution)/shard_map/ppermute | solution.py:228
  124.3 4.6 %collective-permute-start.6 = (f32[40,128]{1,0:T(8,128)S(1)}, f32[40,128]{1,0:T(8,128)S(1)}, u32[]{:S(2)}, u32[]{:S(2)}) collective-permute-start(f32[40,128]{1,0:T(8,128)S(1)} %slice_add_fusion), channel_id=1, source_target_pairs={{0,192},{64,0},{128,64},{192,128},{1,193},{65,1},{129,65},{193,129... | collective-permute-start | bytes 61448 | tf_op jit(solution)/shard_map/ppermute | solution.py:228
  126.2 1.3 copy-start.7
  138.9 23.2 %copy-start.3 = (bf16[256,2240]{0,1:T(8,128)(2,1)S(1)}, bf16[256,2240]{0,1:T(8,128)(2,1)}, u32[]{:S(2)}) copy-start(bf16[256,2240]{0,1:T(8,128)(2,1)} %param.7) | copy-start | bytes 3440644
  157.0 7.6 %collective-permute-start.9 = (f32[1152,256]{1,0:T(8,128)S(1)}, f32[1152,256]{1,0:T(8,128)S(1)}, u32[]{:S(2)}, u32[]{:S(2)}) collective-permute-start(f32[1152,256]{1,0:T(8,128)S(1)} %bitcast.34), channel_id=1, source_target_pairs={{0,1},{1,0},{2,3},{3,2},{4,5},{5,4},{6,7},{7,6},{8,9},{9,8},{10,11... | collective-permute-start | bytes 3538952 | tf_op jit(solution)/shard_map/ppermute | solution.py:186

commit v3 on v2

--- a/solution.py
+++ b/solution.py
@@ -11,7 +11,9 @@
 CORES = 2
 HALF = H // CORES
 ROWS = HALF * E
-STATE_ROWS = 1152
+TILES = -(-ROWS // 128)
+SUMS = ROWS % 128
+STATE_ROWS = 1024
 WIDE = 2 * LANES
 F32 = jnp.float32
 BF16 = jnp.bfloat16
@@ -66,8 +68,57 @@
     return jnp.where(early, both[:LANES], both[LANES:])
 
 
-def fill_up(state_ref):
-    state_ref[ROWS:, :] = jnp.zeros((STATE_ROWS - ROWS, WIDE), F32)
+def roll(block, shift):
+    return pltpu.roll(block, shift % LANES, axis=1) if shift % LANES else block
+
+
+def lane_of():
+    return lax.broadcasted_iota(jnp.int32, (E, LANES), 1)
+
+
+def unpack(state_ref, h):
+    at, start = divmod(h * E, LANES)
+    lane = lane_of()
+    parts = []
+    for frame in range(2):
+        tile = lambda j: state_ref[j * E : (j + 1) * E, frame * LANES : (frame + 1) * LANES]
+        block = tile(at)
+        if start + E > LANES:
+            block = jnp.where(lane >= start, block, tile(at + 1))
+        sums = roll(tile(TILES - 1), E - SUMS - 3 * h)
+        parts.append(jnp.where(lane < E, roll(block, -start), sums))
+    return jnp.concatenate(parts, axis=1)
+
+
+def packer(state_ref):
+    lane = lane_of()
+    held = {}
+
+    def put(j, frame, block, start):
+        if (j, frame) in held:
+            block = jnp.where(lane >= start, block, held[j, frame])
+        held[j, frame] = block
+
+    def write(j, frame):
+        state_ref[j * E : (j + 1) * E, frame * LANES : (frame + 1) * LANES] = held[j, frame]
+
+    def add(h, block):
+        at, start = divmod(h * E, LANES)
+        for frame in range(2):
+            part = block[:, frame * LANES : (frame + 1) * LANES]
+            moved = roll(part, start)
+            put(at, frame, moved, start)
+            if start + E >= LANES:
+                write(at, frame)
+            if start + E > LANES:
+                put(at + 1, frame, moved, 0)
+            put(TILES, frame, roll(part, SUMS + 3 * h - E), SUMS + 3 * h)
+            if h == HALF - 1:
+                put(TILES - 1, frame, held[TILES, frame], SUMS)
+                write(TILES - 1, frame)
+
+    state_ref[TILES * E :, :] = jnp.zeros((STATE_ROWS - TILES * E, WIDE), F32)
+    return add
 
 
 def key_state(key, value, first, second):
@@ -76,10 +127,10 @@
 
 def key_kernel(half_ref, ids_ref, key_ref, value_ref, state_ref):
     _, first, second = frame_masks(ids_ref)
-    for h in range(HALF):
-        rows = pl.ds(h * E, E)
-        state_ref[rows, :] = key_state(key_ref[rows, :], value_ref[rows, :], first, second)
-    fill_up(state_ref)
+    add = packer(state_ref)
+    for h in range(HALF):
+        rows = pl.ds(h * E, E)
+        add(h, key_state(key_ref[rows, :], value_ref[rows, :], first, second))
 
 
 def query_kernel(half_ref, ids_ref, query_ref, cot_ref, state_ref, aux_ref, grad_state_ref):
@@ -87,11 +138,12 @@
     for h in range(HALF):
         rows = pl.ds(h * E, E)
         phi = jnp.maximum(query_ref[rows, :], 0)
-        numer = own_frame(over_rows(*stacked(state_ref[rows, :], phi)), early)
+        numer = own_frame(over_rows(*stacked(unpack(state_ref, h), phi)), early)
         inverse = 1.0 / (numer[E : E + 1] + 1.0)
         wide = cot_ref[rows, :].astype(F32)
         inner = -jnp.sum(wide * numer[:E], axis=0, keepdims=True) * inverse
         aux_ref[h] = jnp.concatenate([inverse, inner], axis=0)
+    add = packer(grad_state_ref)
     for h in range(HALF):
         rows = pl.ds(h * E, E)
         inverse, inner = aux_ref[h, 0:1, :], aux_ref[h, 1:2, :]
@@ -99,8 +151,7 @@
         wide = cot_ref[rows, :].astype(F32)
         high, low = split(with_rows(wide * inverse, inner * inverse))
         block = over_tokens(phi, high) + over_tokens(phi, low)
-        grad_state_ref[rows, :] = jnp.concatenate([block[:E], block[E:]], axis=1)
-    fill_up(grad_state_ref)
+        add(h, jnp.concatenate([block[:E], block[E:]], axis=1))
 
 
 def query_grad_kernel(half_ref, ids_ref, query_ref, cot_ref, state_ref, aux_ref, *refs):
@@ -108,7 +159,7 @@
     _, first, second = frame_masks(ids_ref)
     for h in range(HALF):
         rows = pl.ds(h * E, E)
-        high, low = split(state_ref[rows, :])
+        high, low = split(unpack(state_ref, h))
         inverse, inner = aux_ref[h, 0:1, :], aux_ref[h, 1:2, :]
         inner_high = inner.astype(BF16).astype(F32)
         inner_mid = (inner - inner_high).astype(BF16).astype(F32)
@@ -124,12 +175,13 @@
     early, first, second = frame_masks(ids_ref)
     for h in range(HALF):
         rows = pl.ds(h * E, E)
-        state = state_ref[rows, :]
+        state = unpack(state_ref, h)
         high, low = split(state)
         key = key_ref[rows, :]
         grad = own_frame(over_rows(*stacked(state, jnp.maximum(key, 0))), early)
         grad_value_ref[rows, :] = grad[:E].astype(BF16)
-        values = by_frame(with_ones(value_ref[rows, :]), first, second)
+        values = with_rows(value_ref[rows, :], jnp.ones((1, key.shape[1]), F32))
+        values = by_frame(values, first, second)
         grad = over_columns(high, values) + over_columns(low, values)
         grad_key_ref[rows, :] = jnp.where(key.astype(F32) > 0, grad, 0.0).astype(BF16)
 
@@ -210,7 +262,12 @@
     chips, places = len(near[0]), len(far[0])
     rows = summed.shape[0] // chips
     part = -(-rows // (8 * places)) * 8
+    extra = None
+    if beside is not None:
+        extra = beside(summed)
     summed = exchange(summed.reshape(chips, rows, WIDE), near)
+    if beside is not None:
+        summed, extra = lax.optimization_barrier((summed, extra))
     summed = pl.pallas_call(
         gather_kernel,
         out_shape=jax.ShapeDtypeStruct((places, part, WIDE), F32),
@@ -227,10 +284,6 @@
         arrived.append(
             lax.ppermute(total, "frames", [(i, (i + step) % frames) for i in range(frames)])
         )
-    extra = None
-    if beside is not None:
-        extra = beside(total)
-        arrived, extra = lax.optimization_barrier((arrived, extra))
     for hop, moved in enumerate(arrived, 1):
         reaches = (me + hop < frames) if backward else (me >= hop)
         carry = carry + jnp.where(reaches, moved, 0.0)
@@ -257,19 +310,17 @@
     aux_mine, keep = on_half(query_kernel, core, ids, (query, cot), (mine,), (), ("aux", "state"))
     aux, send = on_half(query_kernel, there, ids, (query, cot), (other,), (), ("aux", "state"))
     received = swap_cores(send)
-    late, _ = lax.optimization_barrier((other, send))
-    grads = on_half(query_grad_kernel, there, ids, (query, cot), (late, aux), (), ("grad",))
-    received, grads = lax.optimization_barrier((received, grads))
-
-    def beside(total):
-        late, _ = lax.optimization_barrier((aux_mine, total))
-        return on_half(query_grad_kernel, core, ids, (query, cot), (mine, late), grads, ("grad",))
-
-    mine, (grad_query,) = carried(keep + received, True, beside)
-    other = swap_cores(mine)
-    grads = on_half(value_kernel, core, ids, (key, value), (mine,), (), ("grad", "grad"))
+
+    def beside(summed):
+        own, others, _ = lax.optimization_barrier((mine, other, summed))
+        grads = on_half(query_grad_kernel, core, ids, (query, cot), (own, aux_mine), (), ("grad",))
+        return on_half(query_grad_kernel, there, ids, (query, cot), (others, aux), grads, ("grad",))
+
+    last, (grad_query,) = carried(keep + received, True, beside)
+    last_other = swap_cores(last)
+    grads = on_half(value_kernel, core, ids, (key, value), (last,), (), ("grad", "grad"))
     grad_key, grad_value = on_half(
-        value_kernel, there, ids, (key, value), (other,), grads, ("grad", "grad")
+        value_kernel, there, ids, (key, value), (last_other,), grads, ("grad", "grad")
     )
     return grad_query.T, grad_key.T, grad_value.T
 

time: 167 us -> 161 us (0.964)
  blocking collectives: 105 us -> 90.1 us
  Pallas kernels: 10.2 us -> 15.4 us
  waiting for transfers between devices: 15.8 us -> 18.5 us
    all_to_all x7, blocking collectives: 105 us -> 90.1 us  [exchange(): lax.all_to_all(block, 'space', 0, 0, axis_index_groups=members, tiled=False)]
    pallas_call x8, Pallas kernels: 10.1 us -> 14.1 us  [on_half(): pl.pallas_call(kernel, out_shape=out_shape, grid_spec=pltpu.PrefetchScala...]
    all_to_all x1, waiting for transfers between devices: 7.56 us -> 10.3 us  [exchange(): lax.all_to_all(block, 'space', 0, 0, axis_index_groups=members, tiled=False)]
    unnamed x22 -> x24, local copies, waits for them, and re-layouts: 5.15 us -> 4.44 us
  transfers between devices with their start and end apart: 11 -> 11, of which waited for: 6 -> 9; matrix products, arithmetic and copies ran while one was open for 0% -> 0% of each run, Pallas kernels for 4% -> 5%
where the time goes in v3:
time: 161 us; the launch traced here: 160 us
  blocking collectives  90.1 us (56%)
  starting transfers between devices  29.1 us (18%)
  waiting for transfers between devices  18.5 us (11%)
  Pallas kernels  15.4 us (10%)
  local copies, waits for them, and re-layouts  4.63 us (3%)
    all_to_all x7, blocking collectives, exchange(): lax.all_to_all(block, 'space', 0, 0, axis_index_groups=members, tiled=False)  90.1 us
    ppermute x4, starting transfers between devices, swap_cores(): lax.ppermute(block, 'space', [(i, i ^ 1) for i in range(lax.axis_size('sp...  17.7 us
    pallas_call x8, Pallas kernels, on_half(): pl.pallas_call(kernel, out_shape=out_shape, grid_spec=pltpu.PrefetchScala...  14.1 us
    all_to_all x1, waiting for transfers between devices, exchange(): lax.all_to_all(block, 'space', 0, 0, axis_index_groups=members, tiled=False)  10.3 us
    ppermute x6, starting transfers between devices, carried(): lax.ppermute(total, 'frames', [(i, (i + step) % frames) for i in range(fr...  7.05 us
    ppermute x6, waiting for transfers between devices, carried(): lax.ppermute(total, 'frames', [(i, (i + step) % frames) for i in range(fr...  4.44 us
    unnamed x24, local copies, waits for them, and re-layouts  4.44 us
    all_to_all x1, starting transfers between devices, exchange(): lax.all_to_all(block, 'space', 0, 0, axis_index_groups=members, tiled=False)  4.41 us
  transfers between devices with their start and end apart: 11, of which 9 were waited for; matrix products, arithmetic and copies ran while one was open for 0% of the time, Pallas kernels for 5%

profile of v3, /device:TPU:1, one launch (start us, length us, event | category | flops | bytes accessed | tf_op | source)
XLA Modules:
  0.0 160.0 jit_solution(5485723105873339150)
XLA Ops:
  4.7 3.3 %collective-permute-start = (f32[1024,256]{1,0:T(8,128)S(1)}, f32[1024,256]{1,0:T(8,128)S(1)}, u32[]{:S(2)}, u32[]{:S(2)}) collective-permute-start(f32[1024,256]{1,0:T(8,128)S(1)} %shard_map.77), channel_id=1, source_target_pairs={{0,1},{1,0},{2,3},{3,2},{4,5},{5,4},{6,7},{7,6},{8,9},{9,8},{10,11... | collective-permute-start | bytes 3145736 | tf_op jit(solution)/shard_map/ppermute | solution.py:238
  8.8 1.4 collective-permute-done
  10.4 18.0 %all_to_all.40.parts_ref = f32[8,128,256]{2,1,0:T(8,128)S(1)} all-to-all(f32[8,128,256]{2,1,0:T(8,128)S(1)} %bitcast.46), channel_id=1, replica_groups={{0,2,4,6,8,10,12,14},{16,18,20,22,24,26,28,30},{32,34,36,38,40,42,44,46..., dimensions={0} | all-to-all | bytes 2097152 | tf_op jit(solution)/shard_map/all_to_all | solution.py:256
  28.5 14.4 %all_to_all.41 = f32[4,32,256]{2,1,0:T(8,128)S(1)} all-to-all(f32[4,32,256]{2,1,0:T(8,128)S(1)} %shard_map.78), channel_id=1, replica_groups={{0,16,32,48},{2,18,34,50},{4,20,36,52},{6,22,38,54},{8,24,40,56},{10,26..., dimensions={0} | all-to-all | bytes 262144 | tf_op jit(solution)/shard_map/all_to_all | solution.py:256
  43.0 2.6 %collective-permute-start.3 = (f32[32,128]{1,0:T(8,128)S(1)}, f32[32,128]{1,0:T(8,128)S(1)}, u32[]{:S(2)}, u32[]{:S(2)}) collective-permute-start(f32[32,128]{1,0:T(8,128)S(1)} %slice_add_fusion.1), channel_id=1, source_target_pairs={{0,192},{64,0},{128,64},{192,128},{1,193},{65,1},{129,65},{193,129... | collective-permute-start | bytes 49160 | tf_op jit(solution)/shard_map/ppermute | solution.py:285
  46.6 3.0 %collective-permute-done.2 = f32[32,128]{1,0:T(8,128)S(1)} collective-permute-done((f32[32,128]{1,0:T(8,128)S(1)}, f32[32,128]{1,0:T(8,128)S(1)}, u32[]{:S(2)}, u32[]{:S(2)}) %collective-permute-start.2) | collective-permute-done | bytes 16416 | tf_op jit(solution)/shard_map/ppermute | solution.py:285
  49.9 9.6 %all_to_all.42 = f32[4,32,256]{2,1,0:T(8,128)S(1)} all-to-all(f32[4,32,256]{2,1,0:T(8,128)S(1)} %broadcast_in_dim.36), channel_id=1, replica_groups={{0,16,32,48},{2,18,34,50},{4,20,36,52},{6,22,38,54},{8,24,40,56},{10,26..., dimensions={0} | all-to-all | bytes 262144 | tf_op jit(solution)/shard_map/all_to_all | solution.py:256
  59.6 13.7 %all_to_all.43 = f32[8,128,256]{2,1,0:T(8,128)S(1)} all-to-all(f32[8,128,256]{2,1,0:T(8,128)S(1)} %broadcast_in_dim.38), channel_id=1, replica_groups={{0,2,4,6,8,10,12,14},{16,18,20,22,24,26,28,30},{32,34,36,38,40,42,44,46..., dimensions={0} | all-to-all | bytes 2097152 | tf_op jit(solution)/shard_map/all_to_all | solution.py:256
  73.3 7.6 %collective-permute-start.4 = (f32[1024,256]{1,0:T(8,128)S(1)}, f32[1024,256]{1,0:T(8,128)S(1)}, u32[]{:S(2)}, u32[]{:S(2)}) collective-permute-start(f32[1024,256]{1,0:T(8,128)S(1)} %bitcast.31), channel_id=1, source_target_pairs={{0,1},{1,0},{2,3},{3,2},{4,5},{5,4},{6,7},{7,6},{8,9},{9,8},{10,11... | collective-permute-start | bytes 3145736 | tf_op jit(solution)/shard_map/ppermute | solution.py:238
  81.0 2.3 %collective-permute-done.4.state_ref = f32[1024,256]{1,0:T(8,128)S(1)} collective-permute-done((f32[1024,256]{1,0:T(8,128)S(1)}, f32[1024,256]{1,0:T(8,128)S(1)}, u32[]{:S(2)}, u32[]{:S(2)}) %collective-permute-start.4) | collective-permute-done | bytes 1048608 | tf_op jit(solution)/shard_map/ppermute | solution.py:238
  83.3 2.2 %shard_map.80 = (f32[10,2,256]{2,1,0:T(2,128)S(1)}, f32[1024,256]{1,0:T(8,128)S(1)}) custom-call(s32[1]{0:T(128)S(6)} %sub.3.half_ref, s32[1,256]{1,0:T(1,128)S(1)} %bitcast.38, bf16[2240,256]{1,0:T(8,128)(2,1)S(1)} %bitcast.23, bf16[2240,256]{1,0:T(8,128)(2,1)S(1)} %bitcast.27, f32[1024,256]{1,0:T(8,128)S(1)} %collective-permute-done.4.state_ref), custom_call_target="tpu_custom_call" | custom-call | flops 880803840 | bytes 2293760 | tf_op jit(solution)/shard_map/pallas_call | solution.py:223
  85.9 2.2 %shard_map.79 = (f32[10,2,256]{2,1,0:T(2,128)S(1)}, f32[1024,256]{1,0:T(8,128)S(1)}) custom-call(s32[1]{0:T(128)} %bitcast.half_ref, s32[1,256]{1,0:T(1,128)S(1)} %bitcast.39, bf16[2240,256]{1,0:T(8,128)(2,1)S(1)} %bitcast.24, bf16[2240,256]{1,0:T(8,128)(2,1)S(1)} %bitcast.28, f32[1024,256]{1,0:T(8,128)S(1)} %bitcast.32), custom_call_target="tpu_custom_call" | custom-call | flops 880803840 | bytes 2293760 | tf_op jit(solution)/shard_map/pallas_call | solution.py:223
  89.3 4.4 %all-to-all-start.4 = ((f32[8,128,256]{2,1,0:T(8,128)}), f32[8,128,256]{2,1,0:T(8,128)}, u32[]{:S(2)}, u32[]{:S(2)}) async-start(f32[8,128,256]{2,1,0:T(8,128)} %bitcast.45), calls=%async_computation.4 | async-start | bytes 2097152 | tf_op jit(solution)/shard_map/all_to_all | solution.py:256
  95.0 1.7 %shard_map.81.refs_0_ = bf16[2240,256]{1,0:T(8,128)(2,1)} custom-call(s32[1]{0:T(128)} %bitcast.half_ref, s32[1,256]{1,0:T(1,128)S(1)} %bitcast.40, bf16[2240,256]{1,0:T(8,128)(2,1)S(1)} %bitcast.25, bf16[2240,256]{1,0:T(8,128)(2,1)S(1)} %bitcast.29, f32[1024,256]{1,0:T(8,128)S(1)} %bitcast.33, f32[10,2,256]{2,1,0:T(2,128)S(1)} %get-tuple-element.20.aux_ref), custom_call_target="tpu_custom_call" | custom-call | flops 880803840 | bytes 2293760 | tf_op jit(solution)/shard_map/pallas_call | solution.py:223
  96.6 1.7 %shard_map.82 = bf16[2240,256]{1,0:T(8,128)(2,1)} custom-call(s32[1]{0:T(128)S(6)} %sub.3.half_ref, s32[1,256]{1,0:T(1,128)S(1)} %bitcast.41, bf16[2240,256]{1,0:T(8,128)(2,1)S(1)} %bitcast.26, bf16[2240,256]{1,0:T(8,128)(2,1)S(1)} %bitcast.30, f32[1024,256]{1,0:T(8,128)S(1)} %copy-done.9, ...), custom_call_target="tpu_custom_call", output_to_operand_aliasing={{}: (6, {})} | custom-call | flops 880803840 | bytes 2293760 | tf_op jit(solution)/shard_map/pallas_call | solution.py:223
  98.3 10.3 %all-to-all-done.4.parts_ref = f32[8,128,256]{2,1,0:T(8,128)} async-done(((f32[8,128,256]{2,1,0:T(8,128)}), f32[8,128,256]{2,1,0:T(8,128)}, u32[]{:S(2)}, u32[]{:S(2)}) %all-to-all-start.4) | async-done | bytes 1048608 | tf_op jit(solution)/shard_map/all_to_all | solution.py:256
  109.8 9.8 %all_to_all.44 = f32[4,32,256]{2,1,0:T(8,128)S(1)} all-to-all(f32[4,32,256]{2,1,0:T(8,128)S(1)} %shard_map.83), channel_id=1, replica_groups={{0,16,32,48},{2,18,34,50},{4,20,36,52},{6,22,38,54},{8,24,40,56},{10,26..., dimensions={0} | all-to-all | bytes 262144 | tf_op jit(solution)/shard_map/all_to_all | solution.py:256
  119.8 1.3 collective-permute-start.7
  121.1 2.0 %collective-permute-start.6 = (f32[32,128]{1,0:T(8,128)S(1)}, f32[32,128]{1,0:T(8,128)S(1)}, u32[]{:S(2)}, u32[]{:S(2)}) collective-permute-start(f32[32,128]{1,0:T(8,128)S(1)} %slice_add_fusion), channel_id=1, source_target_pairs={{0,192},{64,0},{128,64},{192,128},{1,193},{65,1},{129,65},{193,129... | collective-permute-start | bytes 49160 | tf_op jit(solution)/shard_map/ppermute | solution.py:285
  124.4 10.0 %all_to_all.45 = f32[4,32,256]{2,1,0:T(8,128)S(1)} all-to-all(f32[4,32,256]{2,1,0:T(8,128)S(1)} %broadcast_in_dim.39), channel_id=1, replica_groups={{0,16,32,48},{2,18,34,50},{4,20,36,52},{6,22,38,54},{8,24,40,56},{10,26..., dimensions={0} | all-to-all | bytes 262144 | tf_op jit(solution)/shard_map/all_to_all | solution.py:256
  134.5 14.5 %all_to_all.46 = f32[8,128,256]{2,1,0:T(8,128)S(1)} all-to-all(f32[8,128,256]{2,1,0:T(8,128)S(1)} %broadcast_in_dim.41), channel_id=1, replica_groups={{0,2,4,6,8,10,12,14},{16,18,20,22,24,26,28,30},{32,34,36,38,40,42,44,46..., dimensions={0} | all-to-all | bytes 2097152 | tf_op jit(solution)/shard_map/all_to_all | solution.py:256
  149.0 6.2 %collective-permute-start.9 = (f32[1024,256]{1,0:T(8,128)S(1)}, f32[1024,256]{1,0:T(8,128)S(1)}, u32[]{:S(2)}, u32[]{:S(2)}) collective-permute-start(f32[1024,256]{1,0:T(8,128)S(1)} %bitcast.34), channel_id=1, source_target_pairs={{0,1},{1,0},{2,3},{3,2},{4,5},{5,4},{6,7},{7,6},{8,9},{9,8},{10,11... | collective-permute-start | bytes 3145736 | tf_op jit(solution)/shard_map/ppermute | solution.py:238
  155.2 2.4 %shard_map.84 = (bf16[2240,256]{1,0:T(8,128)(2,1)}, bf16[2240,256]{1,0:T(8,128)(2,1)}) custom-call(s32[1]{0:T(128)} %bitcast.half_ref, s32[1,256]{1,0:T(1,128)S(1)} %bitcast.42, bf16[2240,256]{1,0:T(8,128)(2,1)S(1)} %bitcast.17, bf16[2240,256]{1,0:T(8,128)(2,1)S(1)} %bitcast.21, f32[1024,256]{1,0:T(8,128)S(1)} %bitcast.35), custom_call_target="tpu_custom_call" | custom-call | flops 880803840 | bytes 2293760 | tf_op jit(solution)/shard_map/pallas_call | solution.py:223
  157.6 2.4 %shard_map.85 = (bf16[2240,256]{1,0:T(8,128)(2,1)}, bf16[2240,256]{1,0:T(8,128)(2,1)}) custom-call(s32[1]{0:T(128)S(6)} %sub.3.half_ref, s32[1,256]{1,0:T(1,128)S(1)} %bitcast.43, bf16[2240,256]{1,0:T(8,128)(2,1)S(1)} %bitcast.18, bf16[2240,256]{1,0:T(8,128)(2,1)S(1)} %bitcast.22, ...), custom_call_target="tpu_custom_call", output_to_operand_aliasing={{0}: (5, {}), {1}: (6, {})} | custom-call | flops 880803840 | bytes 2293760 | tf_op jit(solution)/shard_map/pallas_call | solution.py:223
  (55 shorter events, 12.2 us)
Async XLA Ops:
  0.6 1.3 copy-start
  1.9 1.3 copy-start.2
  3.2 0.7 copy-start.10
  3.8 4.2 %copy-start.1 = (bf16[256,2240]{0,1:T(8,128)(2,1)S(1)}, bf16[256,2240]{0,1:T(8,128)(2,1)}, u32[]{:S(2)}) copy-start(bf16[256,2240]{0,1:T(8,128)(2,1)} %param.6) | copy-start | bytes 3440644
  3.8 4.2 %copy-start.11 = (s32[256]{0:T(256)S(1)}, s32[256]{0:T(256)}, u32[]{:S(2)}) copy-start(s32[256]{0:T(256)} %param.9) | copy-start | bytes 3076
  4.7 5.6 %collective-permute-start = (f32[1024,256]{1,0:T(8,128)S(1)}, f32[1024,256]{1,0:T(8,128)S(1)}, u32[]{:S(2)}, u32[]{:S(2)}) collective-permute-start(f32[1024,256]{1,0:T(8,128)S(1)} %shard_map.77), channel_id=1, source_target_pairs={{0,1},{1,0},{2,3},{3,2},{4,5},{5,4},{6,7},{7,6},{8,9},{9,8},{10,11... | collective-permute-start | bytes 3145736 | tf_op jit(solution)/shard_map/ppermute | solution.py:238
  43.0 3.7 %collective-permute-start.3 = (f32[32,128]{1,0:T(8,128)S(1)}, f32[32,128]{1,0:T(8,128)S(1)}, u32[]{:S(2)}, u32[]{:S(2)}) collective-permute-start(f32[32,128]{1,0:T(8,128)S(1)} %slice_add_fusion.1), channel_id=1, source_target_pairs={{0,192},{64,0},{128,64},{192,128},{1,193},{65,1},{129,65},{193,129... | collective-permute-start | bytes 49160 | tf_op jit(solution)/shard_map/ppermute | solution.py:285
  45.5 4.1 %collective-permute-start.2 = (f32[32,128]{1,0:T(8,128)S(1)}, f32[32,128]{1,0:T(8,128)S(1)}, u32[]{:S(2)}, u32[]{:S(2)}) collective-permute-start(f32[32,128]{1,0:T(8,128)S(1)} %slice_add_fusion.1), channel_id=1, source_target_pairs={{0,128},{64,192},{128,0},{192,64},{1,129},{65,193},{129,1},{193,65... | collective-permute-start | bytes 49160 | tf_op jit(solution)/shard_map/ppermute | solution.py:285
  46.0 3.8 %collective-permute-start.1 = (f32[32,128]{1,0:T(8,128)S(1)}, f32[32,128]{1,0:T(8,128)S(1)}, u32[]{:S(2)}, u32[]{:S(2)}) collective-permute-start(f32[32,128]{1,0:T(8,128)S(1)} %slice_add_fusion.1), channel_id=1, source_target_pairs={{0,64},{64,128},{128,192},{192,0},{1,65},{65,129},{129,193},{193,1... | collective-permute-start | bytes 49160 | tf_op jit(solution)/shard_map/ppermute | solution.py:285
  59.5 23.7 %copy-start.5 = (bf16[256,2240]{0,1:T(8,128)(2,1)S(1)}, bf16[256,2240]{0,1:T(8,128)(2,1)}, u32[]{:S(2)}) copy-start(bf16[256,2240]{0,1:T(8,128)(2,1)} %param.8) | copy-start | bytes 3440644
  59.6 23.7 %copy-start.4 = (bf16[256,2240]{0,1:T(8,128)(2,1)S(1)}, bf16[256,2240]{0,1:T(8,128)(2,1)}, u32[]{:S(2)}) copy-start(bf16[256,2240]{0,1:T(8,128)(2,1)} %param.5) | copy-start | bytes 3440644
  73.3 12.6 %copy-start.6 = (f32[8,128,256]{2,1,0:T(8,128)}, f32[8,128,256]{2,1,0:T(8,128)S(1)}, u32[]{:S(2)}) copy-start(f32[8,128,256]{2,1,0:T(8,128)S(1)} %all_to_all.43) | copy-start | bytes 3145732
  73.3 9.9 %collective-permute-start.4 = (f32[1024,256]{1,0:T(8,128)S(1)}, f32[1024,256]{1,0:T(8,128)S(1)}, u32[]{:S(2)}, u32[]{:S(2)}) collective-permute-start(f32[1024,256]{1,0:T(8,128)S(1)} %bitcast.31), channel_id=1, source_target_pairs={{0,1},{1,0},{2,3},{3,2},{4,5},{5,4},{6,7},{7,6},{8,9},{9,8},{10,11... | collective-permute-start | bytes 3145736 | tf_op jit(solution)/shard_map/ppermute | solution.py:238
  83.3 2.2 %copy-start.8 = (f32[1024,256]{1,0:T(8,128)}, f32[1024,256]{1,0:T(8,128)S(1)}, u32[]{:S(2)}) copy-start(f32[1024,256]{1,0:T(8,128)S(1)} %collective-permute-done.4.state_ref) | copy-start | bytes 3145732
  85.5 2.8 %collective-permute-start.5 = (f32[1024,256]{1,0:T(8,128)S(1)}, f32[1024,256]{1,0:T(8,128)S(1)}, u32[]{:S(2)}, u32[]{:S(2)}) collective-permute-start(f32[1024,256]{1,0:T(8,128)S(1)} %get-tuple-element.16), channel_id=1, source_target_pairs={{0,1},{1,0},{2,3},{3,2},{4,5},{5,4},{6,7},{7,6},{8,9},{9,8},{10,11... | collective-permute-start | bytes 3145736 | tf_op jit(solution)/shard_map/ppermute | solution.py:238
  89.3 19.2 %all-to-all-start.4 = ((f32[8,128,256]{2,1,0:T(8,128)}), f32[8,128,256]{2,1,0:T(8,128)}, u32[]{:S(2)}, u32[]{:S(2)}) async-start(f32[8,128,256]{2,1,0:T(8,128)} %bitcast.45), calls=%async_computation.4 | async-start | bytes 2097152 | tf_op jit(solution)/shard_map/all_to_all | solution.py:256
  93.7 1.2 copy-start.7
  95.0 1.7 %copy-start.9 = (f32[1024,256]{1,0:T(8,128)S(1)}, f32[1024,256]{1,0:T(8,128)}, u32[]{:S(2)}) copy-start(f32[1024,256]{1,0:T(8,128)} %copy-done.8) | copy-start | bytes 3145732
  119.7 3.9 %collective-permute-start.8 = (f32[32,128]{1,0:T(8,128)S(1)}, f32[32,128]{1,0:T(8,128)S(1)}, u32[]{:S(2)}, u32[]{:S(2)}) collective-permute-start(f32[32,128]{1,0:T(8,128)S(1)} %slice_add_fusion), channel_id=1, source_target_pairs={{0,64},{64,128},{128,192},{192,0},{1,65},{65,129},{129,193},{193,1... | collective-permute-start | bytes 49160 | tf_op jit(solution)/shard_map/ppermute | solution.py:285
  119.8 4.2 %collective-permute-start.7 = (f32[32,128]{1,0:T(8,128)S(1)}, f32[32,128]{1,0:T(8,128)S(1)}, u32[]{:S(2)}, u32[]{:S(2)}) collective-permute-start(f32[32,128]{1,0:T(8,128)S(1)} %slice_add_fusion), channel_id=1, source_target_pairs={{0,128},{64,192},{128,0},{192,64},{1,129},{65,193},{129,1},{193,65... | collective-permute-start | bytes 49160 | tf_op jit(solution)/shard_map/ppermute | solution.py:285
  121.1 3.2 %collective-permute-start.6 = (f32[32,128]{1,0:T(8,128)S(1)}, f32[32,128]{1,0:T(8,128)S(1)}, u32[]{:S(2)}, u32[]{:S(2)}) collective-permute-start(f32[32,128]{1,0:T(8,128)S(1)} %slice_add_fusion), channel_id=1, source_target_pairs={{0,192},{64,0},{128,64},{192,128},{1,193},{65,1},{129,65},{193,129... | collective-permute-start | bytes 49160 | tf_op jit(solution)/shard_map/ppermute | solution.py:285
  134.5 20.7 %copy-start.3 = (bf16[256,2240]{0,1:T(8,128)(2,1)S(1)}, bf16[256,2240]{0,1:T(8,128)(2,1)}, u32[]{:S(2)}) copy-start(bf16[256,2240]{0,1:T(8,128)(2,1)} %param.7) | copy-start | bytes 3440644
  149.0 8.6 %collective-permute-start.9 = (f32[1024,256]{1,0:T(8,128)S(1)}, f32[1024,256]{1,0:T(8,128)S(1)}, u32[]{:S(2)}, u32[]{:S(2)}) collective-permute-start(f32[1024,256]{1,0:T(8,128)S(1)} %bitcast.34), channel_id=1, source_target_pairs={{0,1},{1,0},{2,3},{3,2},{4,5},{5,4},{6,7},{7,6},{8,9},{9,8},{10,11... | collective-permute-start | bytes 3145736 | tf_op jit(solution)/shard_map/ppermute | solution.py:238

commit v4 on v3

--- a/solution.py
+++ b/solution.py
@@ -256,18 +256,13 @@
     return lax.all_to_all(block, "space", 0, 0, axis_index_groups=members, tiled=False)
 
 
-def carried(summed, backward, beside=None):
+def carried(summed, backward):
     frames = lax.axis_size("frames")
     near, far = groups(lax.axis_size("space") // (Y * CORES))
     chips, places = len(near[0]), len(far[0])
     rows = summed.shape[0] // chips
     part = -(-rows // (8 * places)) * 8
-    extra = None
-    if beside is not None:
-        extra = beside(summed)
     summed = exchange(summed.reshape(chips, rows, WIDE), near)
-    if beside is not None:
-        summed, extra = lax.optimization_barrier((summed, extra))
     summed = pl.pallas_call(
         gather_kernel,
         out_shape=jax.ShapeDtypeStruct((places, part, WIDE), F32),
@@ -294,7 +289,7 @@
     done = exchange(jnp.broadcast_to(done[None], (places,) + done.shape), far)
     done = done.reshape(places * part, WIDE)[:rows]
     done = exchange(jnp.broadcast_to(done[None], (chips,) + done.shape), near)
-    return done.reshape(chips * rows, WIDE), extra
+    return done.reshape(chips * rows, WIDE)
 
 
 def on_device(queries, key_inputs, value_inputs, out_cotangent, frame_ids):
@@ -305,18 +300,19 @@
     (send,) = on_half(key_kernel, there, ids, (key, value), (), (), ("state",))
     received = swap_cores(send)
     (keep,) = on_half(key_kernel, core, ids, (key, value), (), (), ("state",))
-    mine, _ = carried(keep + received, False)
+    mine = carried(keep + received, False)
     other = swap_cores(mine)
     aux_mine, keep = on_half(query_kernel, core, ids, (query, cot), (mine,), (), ("aux", "state"))
+    other, keep = lax.optimization_barrier((other, keep))
     aux, send = on_half(query_kernel, there, ids, (query, cot), (other,), (), ("aux", "state"))
     received = swap_cores(send)
-
-    def beside(summed):
-        own, others, _ = lax.optimization_barrier((mine, other, summed))
-        grads = on_half(query_grad_kernel, core, ids, (query, cot), (own, aux_mine), (), ("grad",))
-        return on_half(query_grad_kernel, there, ids, (query, cot), (others, aux), grads, ("grad",))
-
-    last, (grad_query,) = carried(keep + received, True, beside)
+    late, late_other, _ = lax.optimization_barrier((mine, other, send))
+    grads = on_half(query_grad_kernel, core, ids, (query, cot), (late, aux_mine), (), ("grad",))
+    (grad_query,) = on_half(
+        query_grad_kernel, there, ids, (query, cot), (late_other, aux), grads, ("grad",)
+    )
+    received, grad_query = lax.optimization_barrier((received, grad_query))
+    last = carried(keep + received, True)
     last_other = swap_cores(last)
     grads = on_half(value_kernel, core, ids, (key, value), (last,), (), ("grad", "grad"))
     grad_key, grad_value = on_half(

time: 161 us -> 157 us (0.975)
  blocking collectives: 90.1 us -> 107 us
  waiting for transfers between devices: 18.5 us -> 5.99 us
  starting transfers between devices: 29.1 us -> 24.7 us
    all_to_all x7 -> x8, blocking collectives: 90.1 us -> 107 us  [exchange(): lax.all_to_all(block, 'space', 0, 0, axis_index_groups=members, tiled=False)]
    all_to_all x1 -> x0, waiting for transfers between devices: 10.3 us -> none  [exchange(): lax.all_to_all(block, 'space', 0, 0, axis_index_groups=members, tiled=False)]
    all_to_all x1 -> x0, starting transfers between devices: 4.41 us -> none  [exchange(): lax.all_to_all(block, 'space', 0, 0, axis_index_groups=members, tiled=False)]
    ppermute x4, waiting for transfers between devices: 3.83 us -> 1.54 us  [swap_cores(): lax.ppermute(block, 'space', [(i, i ^ 1) for i in range(lax.axis_size('sp...]
    unnamed x24 -> x16, local copies, waits for them, and re-layouts: 4.44 us -> 3.21 us
  transfers between devices with their start and end apart: 11 -> 10, of which waited for: 9 -> 7; matrix products, arithmetic and copies ran while one was open for 0% -> 0% of each run, Pallas kernels for 5% -> 6%
where the time goes in v4:
time: 157 us; the launch traced here: 156 us
  blocking collectives  107 us (68%)
  starting transfers between devices  24.7 us (16%)
  Pallas kernels  14.2 us (9%)
  waiting for transfers between devices  5.99 us (4%)
  local copies, waits for them, and re-layouts  3.4 us (2%)
    all_to_all x8, blocking collectives, exchange(): lax.all_to_all(block, 'space', 0, 0, axis_index_groups=members, tiled=False)  107 us
    ppermute x4, starting transfers between devices, swap_cores(): lax.ppermute(block, 'space', [(i, i ^ 1) for i in range(lax.axis_size('sp...  17.7 us
    pallas_call x8, Pallas kernels, on_half(): pl.pallas_call(kernel, out_shape=out_shape, grid_spec=pltpu.PrefetchScala...  14.1 us
    ppermute x6, starting transfers between devices, carried(): lax.ppermute(total, 'frames', [(i, (i + step) % frames) for i in range(fr...  7.05 us
    ppermute x6, waiting for transfers between devices, carried(): lax.ppermute(total, 'frames', [(i, (i + step) % frames) for i in range(fr...  4.44 us
    unnamed x16, local copies, waits for them, and re-layouts  3.21 us
  transfers between devices with their start and end apart: 10, of which 7 were waited for; matrix products, arithmetic and copies ran while one was open for 0% of the time, Pallas kernels for 6%

profile of v4, /device:TPU:1, one launch (start us, length us, event | category | flops | bytes accessed | tf_op | source)
XLA Modules:
  0.0 156.2 jit_solution(17855844935241993976)
XLA Ops:
  0.7 1.2 copy-done
  1.9 1.3 copy-done.2
  4.7 3.3 %collective-permute-start = (f32[1024,256]{1,0:T(8,128)S(1)}, f32[1024,256]{1,0:T(8,128)S(1)}, u32[]{:S(2)}, u32[]{:S(2)}) collective-permute-start(f32[1024,256]{1,0:T(8,128)S(1)} %shard_map.77), channel_id=1, source_target_pairs={{0,1},{1,0},{2,3},{3,2},{4,5},{5,4},{6,7},{7,6},{8,9},{9,8},{10,11... | collective-permute-start | bytes 3145736 | tf_op jit(solution)/shard_map/ppermute | solution.py:238
  8.8 1.4 collective-permute-done
  10.4 18.0 %all_to_all.40.parts_ref = f32[8,128,256]{2,1,0:T(8,128)S(1)} all-to-all(f32[8,128,256]{2,1,0:T(8,128)S(1)} %bitcast.45), channel_id=1, replica_groups={{0,2,4,6,8,10,12,14},{16,18,20,22,24,26,28,30},{32,34,36,38,40,42,44,46..., dimensions={0} | all-to-all | bytes 2097152 | tf_op jit(solution)/shard_map/all_to_all | solution.py:256
  28.5 14.4 %all_to_all.41 = f32[4,32,256]{2,1,0:T(8,128)S(1)} all-to-all(f32[4,32,256]{2,1,0:T(8,128)S(1)} %shard_map.78), channel_id=1, replica_groups={{0,16,32,48},{2,18,34,50},{4,20,36,52},{6,22,38,54},{8,24,40,56},{10,26..., dimensions={0} | all-to-all | bytes 262144 | tf_op jit(solution)/shard_map/all_to_all | solution.py:256
  43.0 2.6 %collective-permute-start.3 = (f32[32,128]{1,0:T(8,128)S(1)}, f32[32,128]{1,0:T(8,128)S(1)}, u32[]{:S(2)}, u32[]{:S(2)}) collective-permute-start(f32[32,128]{1,0:T(8,128)S(1)} %slice_add_fusion.1), channel_id=1, source_target_pairs={{0,192},{64,0},{128,64},{192,128},{1,193},{65,1},{129,65},{193,129... | collective-permute-start | bytes 49160 | tf_op jit(solution)/shard_map/ppermute | solution.py:280
  46.6 3.0 %collective-permute-done.2 = f32[32,128]{1,0:T(8,128)S(1)} collective-permute-done((f32[32,128]{1,0:T(8,128)S(1)}, f32[32,128]{1,0:T(8,128)S(1)}, u32[]{:S(2)}, u32[]{:S(2)}) %collective-permute-start.2) | collective-permute-done | bytes 16416 | tf_op jit(solution)/shard_map/ppermute | solution.py:280
  49.9 9.6 %all_to_all.42 = f32[4,32,256]{2,1,0:T(8,128)S(1)} all-to-all(f32[4,32,256]{2,1,0:T(8,128)S(1)} %broadcast_in_dim.36), channel_id=1, replica_groups={{0,16,32,48},{2,18,34,50},{4,20,36,52},{6,22,38,54},{8,24,40,56},{10,26..., dimensions={0} | all-to-all | bytes 262144 | tf_op jit(solution)/shard_map/all_to_all | solution.py:256
  59.6 13.7 %all_to_all.43 = f32[8,128,256]{2,1,0:T(8,128)S(1)} all-to-all(f32[8,128,256]{2,1,0:T(8,128)S(1)} %broadcast_in_dim.38), channel_id=1, replica_groups={{0,2,4,6,8,10,12,14},{16,18,20,22,24,26,28,30},{32,34,36,38,40,42,44,46..., dimensions={0} | all-to-all | bytes 2097152 | tf_op jit(solution)/shard_map/all_to_all | solution.py:256
  73.3 7.6 %collective-permute-start.4 = (f32[1024,256]{1,0:T(8,128)S(1)}, f32[1024,256]{1,0:T(8,128)S(1)}, u32[]{:S(2)}, u32[]{:S(2)}) collective-permute-start(f32[1024,256]{1,0:T(8,128)S(1)} %bitcast.31), channel_id=1, source_target_pairs={{0,1},{1,0},{2,3},{3,2},{4,5},{5,4},{6,7},{7,6},{8,9},{9,8},{10,11... | collective-permute-start | bytes 3145736 | tf_op jit(solution)/shard_map/ppermute | solution.py:238
  81.0 2.2 %shard_map.79 = (f32[10,2,256]{2,1,0:T(2,128)S(1)}, f32[1024,256]{1,0:T(8,128)S(1)}) custom-call(s32[1]{0:T(128)} %bitcast.half_ref, s32[1,256]{1,0:T(1,128)S(1)} %bitcast.38, bf16[2240,256]{1,0:T(8,128)(2,1)S(1)} %bitcast.23, bf16[2240,256]{1,0:T(8,128)(2,1)S(1)} %bitcast.27, f32[1024,256]{1,0:T(8,128)S(1)} %bitcast.32), custom_call_target="tpu_custom_call" | custom-call | flops 880803840 | bytes 2293760 | tf_op jit(solution)/shard_map/pallas_call | solution.py:223
  83.2 2.2 %shard_map.80 = (f32[10,2,256]{2,1,0:T(2,128)S(1)}, f32[1024,256]{1,0:T(8,128)S(1)}) custom-call(s32[1]{0:T(128)S(6)} %sub.3.half_ref, s32[1,256]{1,0:T(1,128)S(1)} %bitcast.39, bf16[2240,256]{1,0:T(8,128)(2,1)S(1)} %bitcast.24, bf16[2240,256]{1,0:T(8,128)(2,1)S(1)} %bitcast.28, f32[1024,256]{1,0:T(8,128)S(1)} %collective-permute-done.4.state_ref), custom_call_target="tpu_custom_call" | custom-call | flops 880803840 | bytes 2293760 | tf_op jit(solution)/shard_map/pallas_call | solution.py:223
  85.9 1.7 %shard_map.81.refs_0_ = bf16[2240,256]{1,0:T(8,128)(2,1)} custom-call(s32[1]{0:T(128)} %bitcast.half_ref, s32[1,256]{1,0:T(1,128)S(1)} %bitcast.40, bf16[2240,256]{1,0:T(8,128)(2,1)S(1)} %bitcast.25, bf16[2240,256]{1,0:T(8,128)(2,1)S(1)} %bitcast.29, f32[1024,256]{1,0:T(8,128)S(1)} %bitcast.33, f32[10,2,256]{2,1,0:T(2,128)S(1)} %get-tuple-element.23.aux_ref), custom_call_target="tpu_custom_call" | custom-call | flops 880803840 | bytes 2293760 | tf_op jit(solution)/shard_map/pallas_call | solution.py:223
  87.6 1.7 %shard_map.82 = bf16[2240,256]{1,0:T(8,128)(2,1)} custom-call(s32[1]{0:T(128)S(6)} %sub.3.half_ref, s32[1,256]{1,0:T(1,128)S(1)} %bitcast.41, bf16[2240,256]{1,0:T(8,128)(2,1)S(1)} %bitcast.26, bf16[2240,256]{1,0:T(8,128)(2,1)S(1)} %bitcast.30, f32[1024,256]{1,0:T(8,128)S(1)} %collective-permute-done.4.state_ref, ...), custom_call_target="tpu_custom_call", output_to_operand_aliasing={{}: (6, {})} | custom-call | flops 880803840 | bytes 2293760 | tf_op jit(solution)/shard_map/pallas_call | solution.py:223
  89.4 16.9 %all_to_all.44.parts_ref = f32[8,128,256]{2,1,0:T(8,128)S(1)} all-to-all(f32[8,128,256]{2,1,0:T(8,128)S(1)} %bitcast.46), channel_id=1, replica_groups={{0,2,4,6,8,10,12,14},{16,18,20,22,24,26,28,30},{32,34,36,38,40,42,44,46..., dimensions={0} | all-to-all | bytes 2097152 | tf_op jit(solution)/shard_map/all_to_all | solution.py:256
  106.4 9.6 %all_to_all.45 = f32[4,32,256]{2,1,0:T(8,128)S(1)} all-to-all(f32[4,32,256]{2,1,0:T(8,128)S(1)} %shard_map.83), channel_id=1, replica_groups={{0,16,32,48},{2,18,34,50},{4,20,36,52},{6,22,38,54},{8,24,40,56},{10,26..., dimensions={0} | all-to-all | bytes 262144 | tf_op jit(solution)/shard_map/all_to_all | solution.py:256
  116.1 1.3 collective-permute-start.7
  117.5 2.0 %collective-permute-start.6 = (f32[32,128]{1,0:T(8,128)S(1)}, f32[32,128]{1,0:T(8,128)S(1)}, u32[]{:S(2)}, u32[]{:S(2)}) collective-permute-start(f32[32,128]{1,0:T(8,128)S(1)} %slice_add_fusion), channel_id=1, source_target_pairs={{0,192},{64,0},{128,64},{192,128},{1,193},{65,1},{129,65},{193,129... | collective-permute-start | bytes 49160 | tf_op jit(solution)/shard_map/ppermute | solution.py:280
  120.7 9.6 %all_to_all.46 = f32[4,32,256]{2,1,0:T(8,128)S(1)} all-to-all(f32[4,32,256]{2,1,0:T(8,128)S(1)} %broadcast_in_dim.39), channel_id=1, replica_groups={{0,16,32,48},{2,18,34,50},{4,20,36,52},{6,22,38,54},{8,24,40,56},{10,26..., dimensions={0} | all-to-all | bytes 262144 | tf_op jit(solution)/shard_map/all_to_all | solution.py:256
  130.4 14.7 %all_to_all.47 = f32[8,128,256]{2,1,0:T(8,128)S(1)} all-to-all(f32[8,128,256]{2,1,0:T(8,128)S(1)} %broadcast_in_dim.41), channel_id=1, replica_groups={{0,2,4,6,8,10,12,14},{16,18,20,22,24,26,28,30},{32,34,36,38,40,42,44,46..., dimensions={0} | all-to-all | bytes 2097152 | tf_op jit(solution)/shard_map/all_to_all | solution.py:256
  145.2 6.2 %collective-permute-start.9 = (f32[1024,256]{1,0:T(8,128)S(1)}, f32[1024,256]{1,0:T(8,128)S(1)}, u32[]{:S(2)}, u32[]{:S(2)}) collective-permute-start(f32[1024,256]{1,0:T(8,128)S(1)} %bitcast.34), channel_id=1, source_target_pairs={{0,1},{1,0},{2,3},{3,2},{4,5},{5,4},{6,7},{7,6},{8,9},{9,8},{10,11... | collective-permute-start | bytes 3145736 | tf_op jit(solution)/shard_map/ppermute | solution.py:238
  151.4 2.4 %shard_map.84 = (bf16[2240,256]{1,0:T(8,128)(2,1)}, bf16[2240,256]{1,0:T(8,128)(2,1)}) custom-call(s32[1]{0:T(128)} %bitcast.half_ref, s32[1,256]{1,0:T(1,128)S(1)} %bitcast.42, bf16[2240,256]{1,0:T(8,128)(2,1)S(1)} %bitcast.17, bf16[2240,256]{1,0:T(8,128)(2,1)S(1)} %bitcast.21, f32[1024,256]{1,0:T(8,128)S(1)} %bitcast.35), custom_call_target="tpu_custom_call" | custom-call | flops 880803840 | bytes 2293760 | tf_op jit(solution)/shard_map/pallas_call | solution.py:223
  153.8 2.4 %shard_map.85 = (bf16[2240,256]{1,0:T(8,128)(2,1)}, bf16[2240,256]{1,0:T(8,128)(2,1)}) custom-call(s32[1]{0:T(128)S(6)} %sub.3.half_ref, s32[1,256]{1,0:T(1,128)S(1)} %bitcast.43, bf16[2240,256]{1,0:T(8,128)(2,1)S(1)} %bitcast.18, bf16[2240,256]{1,0:T(8,128)(2,1)S(1)} %bitcast.22, ...), custom_call_target="tpu_custom_call", output_to_operand_aliasing={{0}: (5, {}), {1}: (6, {})} | custom-call | flops 880803840 | bytes 2293760 | tf_op jit(solution)/shard_map/pallas_call | solution.py:223
  (46 shorter events, 6.2 us)
Async XLA Ops:
  0.6 1.3 copy-start
  1.9 1.3 copy-start.2
  3.2 0.7 copy-start.6
  3.8 4.2 %copy-start.1 = (bf16[256,2240]{0,1:T(8,128)(2,1)S(1)}, bf16[256,2240]{0,1:T(8,128)(2,1)}, u32[]{:S(2)}) copy-start(bf16[256,2240]{0,1:T(8,128)(2,1)} %param.6) | copy-start | bytes 3440644
  3.8 4.2 %copy-start.7 = (s32[256]{0:T(256)S(1)}, s32[256]{0:T(256)}, u32[]{:S(2)}) copy-start(s32[256]{0:T(256)} %param.9) | copy-start | bytes 3076
  4.7 5.6 %collective-permute-start = (f32[1024,256]{1,0:T(8,128)S(1)}, f32[1024,256]{1,0:T(8,128)S(1)}, u32[]{:S(2)}, u32[]{:S(2)}) collective-permute-start(f32[1024,256]{1,0:T(8,128)S(1)} %shard_map.77), channel_id=1, source_target_pairs={{0,1},{1,0},{2,3},{3,2},{4,5},{5,4},{6,7},{7,6},{8,9},{9,8},{10,11... | collective-permute-start | bytes 3145736 | tf_op jit(solution)/shard_map/ppermute | solution.py:238
  43.0 3.7 %collective-permute-start.3 = (f32[32,128]{1,0:T(8,128)S(1)}, f32[32,128]{1,0:T(8,128)S(1)}, u32[]{:S(2)}, u32[]{:S(2)}) collective-permute-start(f32[32,128]{1,0:T(8,128)S(1)} %slice_add_fusion.1), channel_id=1, source_target_pairs={{0,192},{64,0},{128,64},{192,128},{1,193},{65,1},{129,65},{193,129... | collective-permute-start | bytes 49160 | tf_op jit(solution)/shard_map/ppermute | solution.py:280
  45.5 4.1 %collective-permute-start.2 = (f32[32,128]{1,0:T(8,128)S(1)}, f32[32,128]{1,0:T(8,128)S(1)}, u32[]{:S(2)}, u32[]{:S(2)}) collective-permute-start(f32[32,128]{1,0:T(8,128)S(1)} %slice_add_fusion.1), channel_id=1, source_target_pairs={{0,128},{64,192},{128,0},{192,64},{1,129},{65,193},{129,1},{193,65... | collective-permute-start | bytes 49160 | tf_op jit(solution)/shard_map/ppermute | solution.py:280
  46.0 3.8 %collective-permute-start.1 = (f32[32,128]{1,0:T(8,128)S(1)}, f32[32,128]{1,0:T(8,128)S(1)}, u32[]{:S(2)}, u32[]{:S(2)}) collective-permute-start(f32[32,128]{1,0:T(8,128)S(1)} %slice_add_fusion.1), channel_id=1, source_target_pairs={{0,64},{64,128},{128,192},{192,0},{1,65},{65,129},{129,193},{193,1... | collective-permute-start | bytes 49160 | tf_op jit(solution)/shard_map/ppermute | solution.py:280
  59.5 21.5 %copy-start.5 = (bf16[256,2240]{0,1:T(8,128)(2,1)S(1)}, bf16[256,2240]{0,1:T(8,128)(2,1)}, u32[]{:S(2)}) copy-start(bf16[256,2240]{0,1:T(8,128)(2,1)} %param.8) | copy-start | bytes 3440644
  59.6 21.4 %copy-start.4 = (bf16[256,2240]{0,1:T(8,128)(2,1)S(1)}, bf16[256,2240]{0,1:T(8,128)(2,1)}, u32[]{:S(2)}) copy-start(bf16[256,2240]{0,1:T(8,128)(2,1)} %param.5) | copy-start | bytes 3440644
  73.3 9.9 %collective-permute-start.4 = (f32[1024,256]{1,0:T(8,128)S(1)}, f32[1024,256]{1,0:T(8,128)S(1)}, u32[]{:S(2)}, u32[]{:S(2)}) collective-permute-start(f32[1024,256]{1,0:T(8,128)S(1)} %bitcast.31), channel_id=1, source_target_pairs={{0,1},{1,0},{2,3},{3,2},{4,5},{5,4},{6,7},{7,6},{8,9},{9,8},{10,11... | collective-permute-start | bytes 3145736 | tf_op jit(solution)/shard_map/ppermute | solution.py:238
  85.4 3.8 %collective-permute-start.5 = (f32[1024,256]{1,0:T(8,128)S(1)}, f32[1024,256]{1,0:T(8,128)S(1)}, u32[]{:S(2)}, u32[]{:S(2)}) collective-permute-start(f32[1024,256]{1,0:T(8,128)S(1)} %get-tuple-element.19), channel_id=1, source_target_pairs={{0,1},{1,0},{2,3},{3,2},{4,5},{5,4},{6,7},{7,6},{8,9},{9,8},{10,11... | collective-permute-start | bytes 3145736 | tf_op jit(solution)/shard_map/ppermute | solution.py:238
  116.0 3.9 %collective-permute-start.8 = (f32[32,128]{1,0:T(8,128)S(1)}, f32[32,128]{1,0:T(8,128)S(1)}, u32[]{:S(2)}, u32[]{:S(2)}) collective-permute-start(f32[32,128]{1,0:T(8,128)S(1)} %slice_add_fusion), channel_id=1, source_target_pairs={{0,64},{64,128},{128,192},{192,0},{1,65},{65,129},{129,193},{193,1... | collective-permute-start | bytes 49160 | tf_op jit(solution)/shard_map/ppermute | solution.py:280
  116.1 4.2 %collective-permute-start.7 = (f32[32,128]{1,0:T(8,128)S(1)}, f32[32,128]{1,0:T(8,128)S(1)}, u32[]{:S(2)}, u32[]{:S(2)}) collective-permute-start(f32[32,128]{1,0:T(8,128)S(1)} %slice_add_fusion), channel_id=1, source_target_pairs={{0,128},{64,192},{128,0},{192,64},{1,129},{65,193},{129,1},{193,65... | collective-permute-start | bytes 49160 | tf_op jit(solution)/shard_map/ppermute | solution.py:280
  117.5 3.2 %collective-permute-start.6 = (f32[32,128]{1,0:T(8,128)S(1)}, f32[32,128]{1,0:T(8,128)S(1)}, u32[]{:S(2)}, u32[]{:S(2)}) collective-permute-start(f32[32,128]{1,0:T(8,128)S(1)} %slice_add_fusion), channel_id=1, source_target_pairs={{0,192},{64,0},{128,64},{192,128},{1,193},{65,1},{129,65},{193,129... | collective-permute-start | bytes 49160 | tf_op jit(solution)/shard_map/ppermute | solution.py:280
  130.4 21.0 %copy-start.3 = (bf16[256,2240]{0,1:T(8,128)(2,1)S(1)}, bf16[256,2240]{0,1:T(8,128)(2,1)}, u32[]{:S(2)}) copy-start(bf16[256,2240]{0,1:T(8,128)(2,1)} %param.7) | copy-start | bytes 3440644
  145.2 8.6 %collective-permute-start.9 = (f32[1024,256]{1,0:T(8,128)S(1)}, f32[1024,256]{1,0:T(8,128)S(1)}, u32[]{:S(2)}, u32[]{:S(2)}) collective-permute-start(f32[1024,256]{1,0:T(8,128)S(1)} %bitcast.34), channel_id=1, source_target_pairs={{0,1},{1,0},{2,3},{3,2},{4,5},{5,4},{6,7},{7,6},{8,9},{9,8},{10,11... | collective-permute-start | bytes 3145736 | tf_op jit(solution)/shard_map/ppermute | solution.py:238

commit v5 on v4

--- a/solution.py
+++ b/solution.py
@@ -125,7 +125,7 @@
     return over_tokens(jnp.maximum(key, 0), by_frame(with_ones(value), first, second))
 
 
-def key_kernel(half_ref, ids_ref, key_ref, value_ref, state_ref):
+def key_kernel(ids_ref, key_ref, value_ref, state_ref):
     _, first, second = frame_masks(ids_ref)
     add = packer(state_ref)
     for h in range(HALF):
@@ -232,6 +232,18 @@
             flops=2 * 6 * ROWS * WIDE * tokens, bytes_accessed=4 * ROWS * tokens * 2, transcendentals=0
         ),
     )(half, *operands)
+
+
+def key_states(half, ids, key, value):
+    rows = lambda array: lax.dynamic_slice(array, (half[0] * ROWS, 0), (ROWS, array.shape[1]))
+    return pl.pallas_call(
+        key_kernel,
+        out_shape=jax.ShapeDtypeStruct((STATE_ROWS, WIDE), F32),
+        compiler_params=params(),
+        cost_estimate=pl.CostEstimate(
+            flops=2 * ROWS * WIDE * ids.shape[1], bytes_accessed=4 * STATE_ROWS * WIDE, transcendentals=0
+        ),
+    )(ids, rows(key), rows(value))
 
 
 def swap_cores(block):
@@ -297,9 +309,9 @@
     query, key, value, cot = (a.T for a in (queries, key_inputs, value_inputs, out_cotangent))
     core = (lax.axis_index("space") % CORES).astype(jnp.int32).reshape(1)
     there = 1 - core
-    (send,) = on_half(key_kernel, there, ids, (key, value), (), (), ("state",))
+    send = key_states(there, ids, key, value)
     received = swap_cores(send)
-    (keep,) = on_half(key_kernel, core, ids, (key, value), (), (), ("state",))
+    keep = key_states(core, ids, key, value)
     mine = carried(keep + received, False)
     other = swap_cores(mine)
     aux_mine, keep = on_half(query_kernel, core, ids, (query, cot), (mine,), (), ("aux", "state"))

time: 157 us -> 155 us (0.987)
    unnamed x16 -> x10, local copies, waits for them, and re-layouts: 3.21 us -> 0.02 us
    dynamic_slice x0 -> x1, local copies, waits for them, and re-layouts: none -> 1.73 us  [key_states(): lax.dynamic_slice(array, (half[0] * ROWS, 0), (ROWS, array.shape[1]))]
    pallas_call x0 -> x2, Pallas kernels: none -> 1.65 us  [key_states(): pl.pallas_call(key_kernel, out_shape=jax.ShapeDtypeStruct((STATE_ROWS, WI...]
    pallas_call x8 -> x6, Pallas kernels: 14.1 us -> 12.5 us  [on_half(): pl.pallas_call(kernel, out_shape=out_shape, grid_spec=pltpu.PrefetchScala...]
where the time goes in v5:
time: 155 us
  blocking collectives  107 us (69%)
  starting transfers between devices  24.7 us (16%)
  Pallas kernels  14.2 us (9%)
  waiting for transfers between devices  5.99 us (4%)
  local copies, waits for them, and re-layouts  1.94 us (1%)
    all_to_all x8, blocking collectives, exchange(): lax.all_to_all(block, 'space', 0, 0, axis_index_groups=members, tiled=False)  107 us
    ppermute x4, starting transfers between devices, swap_cores(): lax.ppermute(block, 'space', [(i, i ^ 1) for i in range(lax.axis_size('sp...  17.6 us
    pallas_call x6, Pallas kernels, on_half(): pl.pallas_call(kernel, out_shape=out_shape, grid_spec=pltpu.PrefetchScala...  12.5 us
    ppermute x6, starting transfers between devices, carried(): lax.ppermute(total, 'frames', [(i, (i + step) % frames) for i in range(fr...  7.05 us
    ppermute x6, waiting for transfers between devices, carried(): lax.ppermute(total, 'frames', [(i, (i + step) % frames) for i in range(fr...  4.44 us
  transfers between devices with their start and end apart: 10, of which 7 were waited for; matrix products, arithmetic and copies ran while one was open for 0% of the time, Pallas kernels for 6%

profile of v5, /device:TPU:1, one launch (start us, length us, event | category | flops | bytes accessed | tf_op | source)
XLA Modules:
  0.0 154.9 jit_solution(3370157649539717271)
XLA Ops:
  0.7 1.7 %dynamic-slice_bitcast_fusion = (bf16[1120,256]{1,0:T(8,128)(2,1)S(1)}, bf16[1120,256]{1,0:T(8,128)(2,1)S(1)}, bf16[1120,256]{1,0:T(8,128)(2,1)S(1)}, bf16[1120,256]{1,0:T(8,128)(2,1)S(1)}) fusion(bf16[256,2240]{0,1:T(8,128)(2,1)} %param.7, s32[]{:T(128)S(6)} %select_n.56, s32[]{:T(128)S(6)} %select_n.55, bf16[256,2240]{0,1:T(8,128)(2,1)} %param.6), kind=kLoop, calls=%fused_computation | loop fusion | bytes 4587528 | tf_op jit(solution)/shard_map/dynamic_slice | solution.py:238
  3.2 3.3 %collective-permute-start = (f32[1024,256]{1,0:T(8,128)S(1)}, f32[1024,256]{1,0:T(8,128)S(1)}, u32[]{:S(2)}, u32[]{:S(2)}) collective-permute-start(f32[1024,256]{1,0:T(8,128)S(1)} %shard_map.77), channel_id=1, source_target_pairs={{0,1},{1,0},{2,3},{3,2},{4,5},{5,4},{6,7},{7,6},{8,9},{9,8},{10,11... | collective-permute-start | bytes 3145736 | tf_op jit(solution)/shard_map/ppermute | solution.py:250
  6.6 0.8 shard_map.76
  7.4 1.5 collective-permute-done
  9.0 18.0 %all_to_all.40.parts_ref = f32[8,128,256]{2,1,0:T(8,128)S(1)} all-to-all(f32[8,128,256]{2,1,0:T(8,128)S(1)} %bitcast.50), channel_id=1, replica_groups={{0,2,4,6,8,10,12,14},{16,18,20,22,24,26,28,30},{32,34,36,38,40,42,44,46..., dimensions={0} | all-to-all | bytes 2097152 | tf_op jit(solution)/shard_map/all_to_all | solution.py:268
  27.1 14.4 %all_to_all.41 = f32[4,32,256]{2,1,0:T(8,128)S(1)} all-to-all(f32[4,32,256]{2,1,0:T(8,128)S(1)} %shard_map.78), channel_id=1, replica_groups={{0,16,32,48},{2,18,34,50},{4,20,36,52},{6,22,38,54},{8,24,40,56},{10,26..., dimensions={0} | all-to-all | bytes 262144 | tf_op jit(solution)/shard_map/all_to_all | solution.py:268
  41.5 2.6 %collective-permute-start.3 = (f32[32,128]{1,0:T(8,128)S(1)}, f32[32,128]{1,0:T(8,128)S(1)}, u32[]{:S(2)}, u32[]{:S(2)}) collective-permute-start(f32[32,128]{1,0:T(8,128)S(1)} %slice_add_fusion.1), channel_id=1, source_target_pairs={{0,192},{64,0},{128,64},{192,128},{1,193},{65,1},{129,65},{193,129... | collective-permute-start | bytes 49160 | tf_op jit(solution)/shard_map/ppermute | solution.py:292
  45.2 3.0 %collective-permute-done.2 = f32[32,128]{1,0:T(8,128)S(1)} collective-permute-done((f32[32,128]{1,0:T(8,128)S(1)}, f32[32,128]{1,0:T(8,128)S(1)}, u32[]{:S(2)}, u32[]{:S(2)}) %collective-permute-start.2) | collective-permute-done | bytes 16416 | tf_op jit(solution)/shard_map/ppermute | solution.py:292
  48.5 9.6 %all_to_all.42 = f32[4,32,256]{2,1,0:T(8,128)S(1)} all-to-all(f32[4,32,256]{2,1,0:T(8,128)S(1)} %broadcast_in_dim.36), channel_id=1, replica_groups={{0,16,32,48},{2,18,34,50},{4,20,36,52},{6,22,38,54},{8,24,40,56},{10,26..., dimensions={0} | all-to-all | bytes 262144 | tf_op jit(solution)/shard_map/all_to_all | solution.py:268
  58.2 13.7 %all_to_all.43 = f32[8,128,256]{2,1,0:T(8,128)S(1)} all-to-all(f32[8,128,256]{2,1,0:T(8,128)S(1)} %broadcast_in_dim.38), channel_id=1, replica_groups={{0,2,4,6,8,10,12,14},{16,18,20,22,24,26,28,30},{32,34,36,38,40,42,44,46..., dimensions={0} | all-to-all | bytes 2097152 | tf_op jit(solution)/shard_map/all_to_all | solution.py:268
  71.9 7.6 %collective-permute-start.4 = (f32[1024,256]{1,0:T(8,128)S(1)}, f32[1024,256]{1,0:T(8,128)S(1)}, u32[]{:S(2)}, u32[]{:S(2)}) collective-permute-start(f32[1024,256]{1,0:T(8,128)S(1)} %bitcast.36), channel_id=1, source_target_pairs={{0,1},{1,0},{2,3},{3,2},{4,5},{5,4},{6,7},{7,6},{8,9},{9,8},{10,11... | collective-permute-start | bytes 3145736 | tf_op jit(solution)/shard_map/ppermute | solution.py:250
  79.5 2.2 %shard_map.79 = (f32[10,2,256]{2,1,0:T(2,128)S(1)}, f32[1024,256]{1,0:T(8,128)S(1)}) custom-call(s32[1]{0:T(128)} %bitcast.half_ref, s32[1,256]{1,0:T(1,128)S(1)} %bitcast.43, bf16[2240,256]{1,0:T(8,128)(2,1)S(1)} %bitcast.24, bf16[2240,256]{1,0:T(8,128)(2,1)S(1)} %bitcast.28, f32[1024,256]{1,0:T(8,128)S(1)} %bitcast.37), custom_call_target="tpu_custom_call" | custom-call | flops 880803840 | bytes 2293760 | tf_op jit(solution)/shard_map/pallas_call | solution.py:223
  81.8 2.2 %shard_map.80 = (f32[10,2,256]{2,1,0:T(2,128)S(1)}, f32[1024,256]{1,0:T(8,128)S(1)}) custom-call(s32[1]{0:T(128)S(6)} %sub.3.half_ref, s32[1,256]{1,0:T(1,128)S(1)} %bitcast.44, bf16[2240,256]{1,0:T(8,128)(2,1)S(1)} %bitcast.25, bf16[2240,256]{1,0:T(8,128)(2,1)S(1)} %bitcast.29, f32[1024,256]{1,0:T(8,128)S(1)} %collective-permute-done.4.state_ref), custom_call_target="tpu_custom_call" | custom-call | flops 880803840 | bytes 2293760 | tf_op jit(solution)/shard_map/pallas_call | solution.py:223
  84.5 1.7 %shard_map.81.refs_0_ = bf16[2240,256]{1,0:T(8,128)(2,1)} custom-call(s32[1]{0:T(128)} %bitcast.half_ref, s32[1,256]{1,0:T(1,128)S(1)} %bitcast.45, bf16[2240,256]{1,0:T(8,128)(2,1)S(1)} %bitcast.26, bf16[2240,256]{1,0:T(8,128)(2,1)S(1)} %bitcast.30, f32[1024,256]{1,0:T(8,128)S(1)} %bitcast.38, f32[10,2,256]{2,1,0:T(2,128)S(1)} %get-tuple-element.23.aux_ref), custom_call_target="tpu_custom_call" | custom-call | flops 880803840 | bytes 2293760 | tf_op jit(solution)/shard_map/pallas_call | solution.py:223
  86.1 1.7 %shard_map.82 = bf16[2240,256]{1,0:T(8,128)(2,1)} custom-call(s32[1]{0:T(128)S(6)} %sub.3.half_ref, s32[1,256]{1,0:T(1,128)S(1)} %bitcast.46, bf16[2240,256]{1,0:T(8,128)(2,1)S(1)} %bitcast.27, bf16[2240,256]{1,0:T(8,128)(2,1)S(1)} %bitcast.31, f32[1024,256]{1,0:T(8,128)S(1)} %collective-permute-done.4.state_ref, ...), custom_call_target="tpu_custom_call", output_to_operand_aliasing={{}: (6, {})} | custom-call | flops 880803840 | bytes 2293760 | tf_op jit(solution)/shard_map/pallas_call | solution.py:223
  87.9 17.1 %all_to_all.44.parts_ref = f32[8,128,256]{2,1,0:T(8,128)S(1)} all-to-all(f32[8,128,256]{2,1,0:T(8,128)S(1)} %bitcast.51), channel_id=1, replica_groups={{0,2,4,6,8,10,12,14},{16,18,20,22,24,26,28,30},{32,34,36,38,40,42,44,46..., dimensions={0} | all-to-all | bytes 2097152 | tf_op jit(solution)/shard_map/all_to_all | solution.py:268
  105.1 9.6 %all_to_all.45 = f32[4,32,256]{2,1,0:T(8,128)S(1)} all-to-all(f32[4,32,256]{2,1,0:T(8,128)S(1)} %shard_map.83), channel_id=1, replica_groups={{0,16,32,48},{2,18,34,50},{4,20,36,52},{6,22,38,54},{8,24,40,56},{10,26..., dimensions={0} | all-to-all | bytes 262144 | tf_op jit(solution)/shard_map/all_to_all | solution.py:268
  114.9 1.3 collective-permute-start.7
  116.2 2.0 %collective-permute-start.6 = (f32[32,128]{1,0:T(8,128)S(1)}, f32[32,128]{1,0:T(8,128)S(1)}, u32[]{:S(2)}, u32[]{:S(2)}) collective-permute-start(f32[32,128]{1,0:T(8,128)S(1)} %slice_add_fusion), channel_id=1, source_target_pairs={{0,192},{64,0},{128,64},{192,128},{1,193},{65,1},{129,65},{193,129... | collective-permute-start | bytes 49160 | tf_op jit(solution)/shard_map/ppermute | solution.py:292
  119.5 9.6 %all_to_all.46 = f32[4,32,256]{2,1,0:T(8,128)S(1)} all-to-all(f32[4,32,256]{2,1,0:T(8,128)S(1)} %broadcast_in_dim.39), channel_id=1, replica_groups={{0,16,32,48},{2,18,34,50},{4,20,36,52},{6,22,38,54},{8,24,40,56},{10,26..., dimensions={0} | all-to-all | bytes 262144 | tf_op jit(solution)/shard_map/all_to_all | solution.py:268
  129.2 14.8 %all_to_all.47 = f32[8,128,256]{2,1,0:T(8,128)S(1)} all-to-all(f32[8,128,256]{2,1,0:T(8,128)S(1)} %broadcast_in_dim.41), channel_id=1, replica_groups={{0,2,4,6,8,10,12,14},{16,18,20,22,24,26,28,30},{32,34,36,38,40,42,44,46..., dimensions={0} | all-to-all | bytes 2097152 | tf_op jit(solution)/shard_map/all_to_all | solution.py:268
  144.0 6.2 %collective-permute-start.9 = (f32[1024,256]{1,0:T(8,128)S(1)}, f32[1024,256]{1,0:T(8,128)S(1)}, u32[]{:S(2)}, u32[]{:S(2)}) collective-permute-start(f32[1024,256]{1,0:T(8,128)S(1)} %bitcast.39), channel_id=1, source_target_pairs={{0,1},{1,0},{2,3},{3,2},{4,5},{5,4},{6,7},{7,6},{8,9},{9,8},{10,11... | collective-permute-start | bytes 3145736 | tf_op jit(solution)/shard_map/ppermute | solution.py:250
  150.2 2.4 %shard_map.84 = (bf16[2240,256]{1,0:T(8,128)(2,1)}, bf16[2240,256]{1,0:T(8,128)(2,1)}) custom-call(s32[1]{0:T(128)} %bitcast.half_ref, s32[1,256]{1,0:T(1,128)S(1)} %bitcast.47, bf16[2240,256]{1,0:T(8,128)(2,1)S(1)} %bitcast.34, bf16[2240,256]{1,0:T(8,128)(2,1)S(1)} %bitcast.32, f32[1024,256]{1,0:T(8,128)S(1)} %bitcast.40), custom_call_target="tpu_custom_call" | custom-call | flops 880803840 | bytes 2293760 | tf_op jit(solution)/shard_map/pallas_call | solution.py:223
  152.5 2.4 %shard_map.85 = (bf16[2240,256]{1,0:T(8,128)(2,1)}, bf16[2240,256]{1,0:T(8,128)(2,1)}) custom-call(s32[1]{0:T(128)S(6)} %sub.3.half_ref, s32[1,256]{1,0:T(1,128)S(1)} %bitcast.48, bf16[2240,256]{1,0:T(8,128)(2,1)S(1)} %bitcast.35, bf16[2240,256]{1,0:T(8,128)(2,1)S(1)} %bitcast.33, ...), custom_call_target="tpu_custom_call", output_to_operand_aliasing={{0}: (5, {}), {1}: (6, {})} | custom-call | flops 880803840 | bytes 2293760 | tf_op jit(solution)/shard_map/pallas_call | solution.py:223
  (41 shorter events, 4.7 us)
Async XLA Ops:
  0.7 1.7 %copy-start.4 = (s32[256]{0:T(256)S(1)}, s32[256]{0:T(256)}, u32[]{:S(2)}) copy-start(s32[256]{0:T(256)} %param.9) | copy-start | bytes 3076
  3.2 5.6 %collective-permute-start = (f32[1024,256]{1,0:T(8,128)S(1)}, f32[1024,256]{1,0:T(8,128)S(1)}, u32[]{:S(2)}, u32[]{:S(2)}) collective-permute-start(f32[1024,256]{1,0:T(8,128)S(1)} %shard_map.77), channel_id=1, source_target_pairs={{0,1},{1,0},{2,3},{3,2},{4,5},{5,4},{6,7},{7,6},{8,9},{9,8},{10,11... | collective-permute-start | bytes 3145736 | tf_op jit(solution)/shard_map/ppermute | solution.py:250
  41.5 3.7 %collective-permute-start.3 = (f32[32,128]{1,0:T(8,128)S(1)}, f32[32,128]{1,0:T(8,128)S(1)}, u32[]{:S(2)}, u32[]{:S(2)}) collective-permute-start(f32[32,128]{1,0:T(8,128)S(1)} %slice_add_fusion.1), channel_id=1, source_target_pairs={{0,192},{64,0},{128,64},{192,128},{1,193},{65,1},{129,65},{193,129... | collective-permute-start | bytes 49160 | tf_op jit(solution)/shard_map/ppermute | solution.py:292
  44.1 4.1 %collective-permute-start.2 = (f32[32,128]{1,0:T(8,128)S(1)}, f32[32,128]{1,0:T(8,128)S(1)}, u32[]{:S(2)}, u32[]{:S(2)}) collective-permute-start(f32[32,128]{1,0:T(8,128)S(1)} %slice_add_fusion.1), channel_id=1, source_target_pairs={{0,128},{64,192},{128,0},{192,64},{1,129},{65,193},{129,1},{193,65... | collective-permute-start | bytes 49160 | tf_op jit(solution)/shard_map/ppermute | solution.py:292
  44.6 3.8 %collective-permute-start.1 = (f32[32,128]{1,0:T(8,128)S(1)}, f32[32,128]{1,0:T(8,128)S(1)}, u32[]{:S(2)}, u32[]{:S(2)}) collective-permute-start(f32[32,128]{1,0:T(8,128)S(1)} %slice_add_fusion.1), channel_id=1, source_target_pairs={{0,64},{64,128},{128,192},{192,0},{1,65},{65,129},{129,193},{193,1... | collective-permute-start | bytes 49160 | tf_op jit(solution)/shard_map/ppermute | solution.py:292
  58.1 21.5 %copy-start.1 = (bf16[256,2240]{0,1:T(8,128)(2,1)S(1)}, bf16[256,2240]{0,1:T(8,128)(2,1)}, u32[]{:S(2)}) copy-start(bf16[256,2240]{0,1:T(8,128)(2,1)} %param.8) | copy-start | bytes 3440644
  58.2 21.4 %copy-start = (bf16[256,2240]{0,1:T(8,128)(2,1)S(1)}, bf16[256,2240]{0,1:T(8,128)(2,1)}, u32[]{:S(2)}) copy-start(bf16[256,2240]{0,1:T(8,128)(2,1)} %param.5) | copy-start | bytes 3440644
  71.9 9.9 %collective-permute-start.4 = (f32[1024,256]{1,0:T(8,128)S(1)}, f32[1024,256]{1,0:T(8,128)S(1)}, u32[]{:S(2)}, u32[]{:S(2)}) collective-permute-start(f32[1024,256]{1,0:T(8,128)S(1)} %bitcast.36), channel_id=1, source_target_pairs={{0,1},{1,0},{2,3},{3,2},{4,5},{5,4},{6,7},{7,6},{8,9},{9,8},{10,11... | collective-permute-start | bytes 3145736 | tf_op jit(solution)/shard_map/ppermute | solution.py:250
  84.0 3.8 %collective-permute-start.5 = (f32[1024,256]{1,0:T(8,128)S(1)}, f32[1024,256]{1,0:T(8,128)S(1)}, u32[]{:S(2)}, u32[]{:S(2)}) collective-permute-start(f32[1024,256]{1,0:T(8,128)S(1)} %get-tuple-element.19), channel_id=1, source_target_pairs={{0,1},{1,0},{2,3},{3,2},{4,5},{5,4},{6,7},{7,6},{8,9},{9,8},{10,11... | collective-permute-start | bytes 3145736 | tf_op jit(solution)/shard_map/ppermute | solution.py:250
  114.8 3.9 %collective-permute-start.8 = (f32[32,128]{1,0:T(8,128)S(1)}, f32[32,128]{1,0:T(8,128)S(1)}, u32[]{:S(2)}, u32[]{:S(2)}) collective-permute-start(f32[32,128]{1,0:T(8,128)S(1)} %slice_add_fusion), channel_id=1, source_target_pairs={{0,64},{64,128},{128,192},{192,0},{1,65},{65,129},{129,193},{193,1... | collective-permute-start | bytes 49160 | tf_op jit(solution)/shard_map/ppermute | solution.py:292
  114.9 4.2 %collective-permute-start.7 = (f32[32,128]{1,0:T(8,128)S(1)}, f32[32,128]{1,0:T(8,128)S(1)}, u32[]{:S(2)}, u32[]{:S(2)}) collective-permute-start(f32[32,128]{1,0:T(8,128)S(1)} %slice_add_fusion), channel_id=1, source_target_pairs={{0,128},{64,192},{128,0},{192,64},{1,129},{65,193},{129,1},{193,65... | collective-permute-start | bytes 49160 | tf_op jit(solution)/shard_map/ppermute | solution.py:292
  116.2 3.2 %collective-permute-start.6 = (f32[32,128]{1,0:T(8,128)S(1)}, f32[32,128]{1,0:T(8,128)S(1)}, u32[]{:S(2)}, u32[]{:S(2)}) collective-permute-start(f32[32,128]{1,0:T(8,128)S(1)} %slice_add_fusion), channel_id=1, source_target_pairs={{0,192},{64,0},{128,64},{192,128},{1,193},{65,1},{129,65},{193,129... | collective-permute-start | bytes 49160 | tf_op jit(solution)/shard_map/ppermute | solution.py:292
  129.1 21.1 %copy-start.3 = (bf16[256,2240]{0,1:T(8,128)(2,1)S(1)}, bf16[256,2240]{0,1:T(8,128)(2,1)}, u32[]{:S(2)}) copy-start(bf16[256,2240]{0,1:T(8,128)(2,1)} %param.6) | copy-start | bytes 3440644
  129.2 21.0 %copy-start.2 = (bf16[256,2240]{0,1:T(8,128)(2,1)S(1)}, bf16[256,2240]{0,1:T(8,128)(2,1)}, u32[]{:S(2)}) copy-start(bf16[256,2240]{0,1:T(8,128)(2,1)} %param.7) | copy-start | bytes 3440644
  144.0 8.6 %collective-permute-start.9 = (f32[1024,256]{1,0:T(8,128)S(1)}, f32[1024,256]{1,0:T(8,128)S(1)}, u32[]{:S(2)}, u32[]{:S(2)}) collective-permute-start(f32[1024,256]{1,0:T(8,128)S(1)} %bitcast.39), channel_id=1, source_target_pairs={{0,1},{1,0},{2,3},{3,2},{4,5},{5,4},{6,7},{7,6},{8,9},{9,8},{10,11... | collective-permute-start | bytes 3145736 | tf_op jit(solution)/shard_map/ppermute | solution.py:250

commit v6 on v5

--- a/solution.py
+++ b/solution.py
@@ -13,6 +13,7 @@
 ROWS = HALF * E
 TILES = -(-ROWS // 128)
 SUMS = ROWS % 128
+GROUP = 5
 STATE_ROWS = 1024
 WIDE = 2 * LANES
 F32 = jnp.float32
@@ -40,10 +41,14 @@
     return jnp.concatenate([rows, jnp.ones((LANES - E, rows.shape[1]), rows.dtype)], axis=0)
 
 
-def with_rows(rows, *extra):
+def sums_of(h):
+    return 3 * (h % GROUP)
+
+
+def with_rows(rows, h, *extra):
     at = lax.broadcasted_iota(jnp.int32, (LANES - E, rows.shape[1]), 0)
     tail = jnp.zeros((LANES - E, rows.shape[1]), F32)
-    for place, row in enumerate(extra):
+    for place, row in enumerate(extra, sums_of(h)):
         tail = jnp.where(at == place, row, tail)
     return jnp.concatenate([rows, tail.astype(rows.dtype)], axis=0)
 
@@ -76,18 +81,26 @@
     return lax.broadcasted_iota(jnp.int32, (E, LANES), 1)
 
 
-def unpack(state_ref, h):
-    at, start = divmod(h * E, LANES)
+def unpacker(state_ref):
     lane = lane_of()
-    parts = []
-    for frame in range(2):
-        tile = lambda j: state_ref[j * E : (j + 1) * E, frame * LANES : (frame + 1) * LANES]
-        block = tile(at)
-        if start + E > LANES:
-            block = jnp.where(lane >= start, block, tile(at + 1))
-        sums = roll(tile(TILES - 1), E - SUMS - 3 * h)
-        parts.append(jnp.where(lane < E, roll(block, -start), sums))
-    return jnp.concatenate(parts, axis=1)
+
+    def tile(j, frame):
+        return state_ref[j * E : (j + 1) * E, frame * LANES : (frame + 1) * LANES]
+
+    last = [tile(TILES - 1, frame) for frame in range(2)]
+    sums = (last, [roll(block, LANES - E) for block in last])
+
+    def get(h):
+        at, start = divmod(h * E, LANES)
+        parts = []
+        for frame in range(2):
+            block = tile(at, frame)
+            if start + E > LANES:
+                block = jnp.where(lane >= start, block, tile(at + 1, frame))
+            parts.append(jnp.where(lane < E, roll(block, -start), sums[h // GROUP][frame]))
+        return jnp.concatenate(parts, axis=1)
+
+    return get
 
 
 def packer(state_ref):
@@ -112,9 +125,10 @@
                 write(at, frame)
             if start + E > LANES:
                 put(at + 1, frame, moved, 0)
-            put(TILES, frame, roll(part, SUMS + 3 * h - E), SUMS + 3 * h)
+            put(TILES + h // GROUP, frame, part, E + sums_of(h))
             if h == HALF - 1:
-                put(TILES - 1, frame, held[TILES, frame], SUMS)
+                put(TILES - 1, frame, roll(held[TILES + 1, frame], E - LANES), SUMS)
+                put(TILES - 1, frame, held[TILES, frame], E)
                 write(TILES - 1, frame)
 
     state_ref[TILES * E :, :] = jnp.zeros((STATE_ROWS - TILES * E, WIDE), F32)
@@ -135,11 +149,12 @@
 
 def query_kernel(half_ref, ids_ref, query_ref, cot_ref, state_ref, aux_ref, grad_state_ref):
     early, first, second = frame_masks(ids_ref)
+    state_of = unpacker(state_ref)
     for h in range(HALF):
         rows = pl.ds(h * E, E)
         phi = jnp.maximum(query_ref[rows, :], 0)
-        numer = own_frame(over_rows(*stacked(unpack(state_ref, h), phi)), early)
-        inverse = 1.0 / (numer[E : E + 1] + 1.0)
+        numer = own_frame(over_rows(*stacked(state_of(h), phi)), early)
+        inverse = 1.0 / (numer[E + sums_of(h) : E + sums_of(h) + 1] + 1.0)
         wide = cot_ref[rows, :].astype(F32)
         inner = -jnp.sum(wide * numer[:E], axis=0, keepdims=True) * inverse
         aux_ref[h] = jnp.concatenate([inverse, inner], axis=0)
@@ -149,7 +164,7 @@
         inverse, inner = aux_ref[h, 0:1, :], aux_ref[h, 1:2, :]
         phi = by_frame(jnp.maximum(query_ref[rows, :], 0), first, second)
         wide = cot_ref[rows, :].astype(F32)
-        high, low = split(with_rows(wide * inverse, inner * inverse))
+        high, low = split(with_rows(wide * inverse, h, inner * inverse))
         block = over_tokens(phi, high) + over_tokens(phi, low)
         add(h, jnp.concatenate([block[:E], block[E:]], axis=1))
 
@@ -157,14 +172,15 @@
 def query_grad_kernel(half_ref, ids_ref, query_ref, cot_ref, state_ref, aux_ref, *refs):
     grad_ref = refs[-1]
     _, first, second = frame_masks(ids_ref)
-    for h in range(HALF):
-        rows = pl.ds(h * E, E)
-        high, low = split(unpack(state_ref, h))
+    state_of = unpacker(state_ref)
+    for h in range(HALF):
+        rows = pl.ds(h * E, E)
+        high, low = split(state_of(h))
         inverse, inner = aux_ref[h, 0:1, :], aux_ref[h, 1:2, :]
         inner_high = inner.astype(BF16).astype(F32)
         inner_mid = (inner - inner_high).astype(BF16).astype(F32)
         inner_low = inner - inner_high - inner_mid
-        cots = with_rows(cot_ref[rows, :], inner_high, inner_mid, inner_low)
+        cots = with_rows(cot_ref[rows, :], h, inner_high, inner_mid, inner_low)
         cots = by_frame(cots, first, second)
         grad = (over_columns(high, cots) + over_columns(low, cots)) * inverse
         grad_ref[rows, :] = jnp.where(query_ref[rows, :].astype(F32) > 0, grad, 0.0).astype(BF16)
@@ -173,14 +189,15 @@
 def value_kernel(half_ref, ids_ref, key_ref, value_ref, state_ref, *refs):
     grad_key_ref, grad_value_ref = refs[-2:]
     early, first, second = frame_masks(ids_ref)
-    for h in range(HALF):
-        rows = pl.ds(h * E, E)
-        state = unpack(state_ref, h)
+    state_of = unpacker(state_ref)
+    for h in range(HALF):
+        rows = pl.ds(h * E, E)
+        state = state_of(h)
         high, low = split(state)
         key = key_ref[rows, :]
         grad = own_frame(over_rows(*stacked(state, jnp.maximum(key, 0))), early)
         grad_value_ref[rows, :] = grad[:E].astype(BF16)
-        values = with_rows(value_ref[rows, :], jnp.ones((1, key.shape[1]), F32))
+        values = with_rows(value_ref[rows, :], h, jnp.ones((1, key.shape[1]), F32))
         values = by_frame(values, first, second)
         grad = over_columns(high, values) + over_columns(low, values)
         grad_key_ref[rows, :] = jnp.where(key.astype(F32) > 0, grad, 0.0).astype(BF16)

time: 155 us -> 154 us (level)
  Pallas kernels: 14.2 us -> 12.5 us
  transfers between devices with their start and end apart: 10 -> 10, of which waited for: 7 -> 7; matrix products, arithmetic and copies ran while one was open for 0% -> 0% of each run, Pallas kernels for 6% -> 5%
where the time goes in v6:
time: 154 us
  blocking collectives  107 us (69%)
  starting transfers between devices  24.7 us (16%)
  Pallas kernels  12.5 us (8%)
  waiting for transfers between devices  6.59 us (4%)
  local copies, waits for them, and re-layouts  1.94 us (1%)
    all_to_all x8, blocking collectives, exchange(): lax.all_to_all(block, 'space', 0, 0, axis_index_groups=members, tiled=False)  107 us
    ppermute x4, starting transfers between devices, swap_cores(): lax.ppermute(block, 'space', [(i, i ^ 1) for i in range(lax.axis_size('sp...  17.6 us
    pallas_call x6, Pallas kernels, on_half(): pl.pallas_call(kernel, out_shape=out_shape, grid_spec=pltpu.PrefetchScala...  11.1 us
    ppermute x6, starting transfers between devices, carried(): lax.ppermute(total, 'frames', [(i, (i + step) % frames) for i in range(fr...  7.05 us
    ppermute x6, waiting for transfers between devices, carried(): lax.ppermute(total, 'frames', [(i, (i + step) % frames) for i in range(fr...  4.45 us
  transfers between devices with their start and end apart: 10, of which 7 were waited for; matrix products, arithmetic and copies ran while one was open for 0% of the time, Pallas kernels for 5%

profile of v6, /device:TPU:1, one launch (start us, length us, event | category | flops | bytes accessed | tf_op | source)
XLA Modules:
  0.0 153.6 jit_solution(10375278743138165604)
XLA Ops:
  0.7 1.7 %dynamic-slice_bitcast_fusion = (bf16[1120,256]{1,0:T(8,128)(2,1)S(1)}, bf16[1120,256]{1,0:T(8,128)(2,1)S(1)}, bf16[1120,256]{1,0:T(8,128)(2,1)S(1)}, bf16[1120,256]{1,0:T(8,128)(2,1)S(1)}) fusion(bf16[256,2240]{0,1:T(8,128)(2,1)} %param.7, s32[]{:T(128)S(6)} %select_n.56, s32[]{:T(128)S(6)} %select_n.55, bf16[256,2240]{0,1:T(8,128)(2,1)} %param.6), kind=kLoop, calls=%fused_computation | loop fusion | bytes 4587528 | tf_op jit(solution)/shard_map/dynamic_slice | solution.py:255
  2.4 0.7 shard_map.77
  3.1 3.3 %collective-permute-start = (f32[1024,256]{1,0:T(8,128)S(1)}, f32[1024,256]{1,0:T(8,128)S(1)}, u32[]{:S(2)}, u32[]{:S(2)}) collective-permute-start(f32[1024,256]{1,0:T(8,128)S(1)} %shard_map.77), channel_id=1, source_target_pairs={{0,1},{1,0},{2,3},{3,2},{4,5},{5,4},{6,7},{7,6},{8,9},{9,8},{10,11... | collective-permute-start | bytes 3145736 | tf_op jit(solution)/shard_map/ppermute | solution.py:267
  7.1 1.6 %collective-permute-done = f32[1024,256]{1,0:T(8,128)S(1)} collective-permute-done((f32[1024,256]{1,0:T(8,128)S(1)}, f32[1024,256]{1,0:T(8,128)S(1)}, u32[]{:S(2)}, u32[]{:S(2)}) %collective-permute-start) | collective-permute-done | bytes 1048608 | tf_op jit(solution)/shard_map/ppermute | solution.py:267
  8.8 18.0 %all_to_all.40.parts_ref = f32[8,128,256]{2,1,0:T(8,128)S(1)} all-to-all(f32[8,128,256]{2,1,0:T(8,128)S(1)} %bitcast.50), channel_id=1, replica_groups={{0,2,4,6,8,10,12,14},{16,18,20,22,24,26,28,30},{32,34,36,38,40,42,44,46..., dimensions={0} | all-to-all | bytes 2097152 | tf_op jit(solution)/shard_map/all_to_all | solution.py:285
  26.9 14.4 %all_to_all.41 = f32[4,32,256]{2,1,0:T(8,128)S(1)} all-to-all(f32[4,32,256]{2,1,0:T(8,128)S(1)} %shard_map.78), channel_id=1, replica_groups={{0,16,32,48},{2,18,34,50},{4,20,36,52},{6,22,38,54},{8,24,40,56},{10,26..., dimensions={0} | all-to-all | bytes 262144 | tf_op jit(solution)/shard_map/all_to_all | solution.py:285
  41.4 2.6 %collective-permute-start.3 = (f32[32,128]{1,0:T(8,128)S(1)}, f32[32,128]{1,0:T(8,128)S(1)}, u32[]{:S(2)}, u32[]{:S(2)}) collective-permute-start(f32[32,128]{1,0:T(8,128)S(1)} %slice_add_fusion.1), channel_id=1, source_target_pairs={{0,192},{64,0},{128,64},{192,128},{1,193},{65,1},{129,65},{193,129... | collective-permute-start | bytes 49160 | tf_op jit(solution)/shard_map/ppermute | solution.py:309
  45.0 3.0 %collective-permute-done.2 = f32[32,128]{1,0:T(8,128)S(1)} collective-permute-done((f32[32,128]{1,0:T(8,128)S(1)}, f32[32,128]{1,0:T(8,128)S(1)}, u32[]{:S(2)}, u32[]{:S(2)}) %collective-permute-start.2) | collective-permute-done | bytes 16416 | tf_op jit(solution)/shard_map/ppermute | solution.py:309
  48.3 9.6 %all_to_all.42 = f32[4,32,256]{2,1,0:T(8,128)S(1)} all-to-all(f32[4,32,256]{2,1,0:T(8,128)S(1)} %broadcast_in_dim.36), channel_id=1, replica_groups={{0,16,32,48},{2,18,34,50},{4,20,36,52},{6,22,38,54},{8,24,40,56},{10,26..., dimensions={0} | all-to-all | bytes 262144 | tf_op jit(solution)/shard_map/all_to_all | solution.py:285
  58.0 13.7 %all_to_all.43 = f32[8,128,256]{2,1,0:T(8,128)S(1)} all-to-all(f32[8,128,256]{2,1,0:T(8,128)S(1)} %broadcast_in_dim.38), channel_id=1, replica_groups={{0,2,4,6,8,10,12,14},{16,18,20,22,24,26,28,30},{32,34,36,38,40,42,44,46..., dimensions={0} | all-to-all | bytes 2097152 | tf_op jit(solution)/shard_map/all_to_all | solution.py:285
  71.7 7.6 %collective-permute-start.4 = (f32[1024,256]{1,0:T(8,128)S(1)}, f32[1024,256]{1,0:T(8,128)S(1)}, u32[]{:S(2)}, u32[]{:S(2)}) collective-permute-start(f32[1024,256]{1,0:T(8,128)S(1)} %bitcast.36), channel_id=1, source_target_pairs={{0,1},{1,0},{2,3},{3,2},{4,5},{5,4},{6,7},{7,6},{8,9},{9,8},{10,11... | collective-permute-start | bytes 3145736 | tf_op jit(solution)/shard_map/ppermute | solution.py:267
  79.4 1.8 %shard_map.79 = (f32[10,2,256]{2,1,0:T(2,128)S(1)}, f32[1024,256]{1,0:T(8,128)S(1)}) custom-call(s32[1]{0:T(128)} %bitcast.half_ref, s32[1,256]{1,0:T(1,128)S(1)} %bitcast.43, bf16[2240,256]{1,0:T(8,128)(2,1)S(1)} %bitcast.24, bf16[2240,256]{1,0:T(8,128)(2,1)S(1)} %bitcast.28, f32[1024,256]{1,0:T(8,128)S(1)} %bitcast.37), custom_call_target="tpu_custom_call" | custom-call | flops 880803840 | bytes 2293760 | tf_op jit(solution)/shard_map/pallas_call | solution.py:240
  81.6 1.8 %shard_map.80 = (f32[10,2,256]{2,1,0:T(2,128)S(1)}, f32[1024,256]{1,0:T(8,128)S(1)}) custom-call(s32[1]{0:T(128)S(6)} %sub.3.half_ref, s32[1,256]{1,0:T(1,128)S(1)} %bitcast.44, bf16[2240,256]{1,0:T(8,128)(2,1)S(1)} %bitcast.25, bf16[2240,256]{1,0:T(8,128)(2,1)S(1)} %bitcast.29, f32[1024,256]{1,0:T(8,128)S(1)} %collective-permute-done.4.state_ref), custom_call_target="tpu_custom_call" | custom-call | flops 880803840 | bytes 2293760 | tf_op jit(solution)/shard_map/pallas_call | solution.py:240
  83.9 1.5 shard_map.81.refs_0_
  85.4 1.5 shard_map.82
  87.0 16.9 %all_to_all.44.parts_ref = f32[8,128,256]{2,1,0:T(8,128)S(1)} all-to-all(f32[8,128,256]{2,1,0:T(8,128)S(1)} %bitcast.51), channel_id=1, replica_groups={{0,2,4,6,8,10,12,14},{16,18,20,22,24,26,28,30},{32,34,36,38,40,42,44,46..., dimensions={0} | all-to-all | bytes 2097152 | tf_op jit(solution)/shard_map/all_to_all | solution.py:285
  104.0 9.6 %all_to_all.45 = f32[4,32,256]{2,1,0:T(8,128)S(1)} all-to-all(f32[4,32,256]{2,1,0:T(8,128)S(1)} %shard_map.83), channel_id=1, replica_groups={{0,16,32,48},{2,18,34,50},{4,20,36,52},{6,22,38,54},{8,24,40,56},{10,26..., dimensions={0} | all-to-all | bytes 262144 | tf_op jit(solution)/shard_map/all_to_all | solution.py:285
  113.7 1.5 collective-permute-start.7
  115.2 1.8 %collective-permute-start.6 = (f32[32,128]{1,0:T(8,128)S(1)}, f32[32,128]{1,0:T(8,128)S(1)}, u32[]{:S(2)}, u32[]{:S(2)}) collective-permute-start(f32[32,128]{1,0:T(8,128)S(1)} %slice_add_fusion), channel_id=1, source_target_pairs={{0,192},{64,0},{128,64},{192,128},{1,193},{65,1},{129,65},{193,129... | collective-permute-start | bytes 49160 | tf_op jit(solution)/shard_map/ppermute | solution.py:309
  118.3 9.6 %all_to_all.46 = f32[4,32,256]{2,1,0:T(8,128)S(1)} all-to-all(f32[4,32,256]{2,1,0:T(8,128)S(1)} %broadcast_in_dim.39), channel_id=1, replica_groups={{0,16,32,48},{2,18,34,50},{4,20,36,52},{6,22,38,54},{8,24,40,56},{10,26..., dimensions={0} | all-to-all | bytes 262144 | tf_op jit(solution)/shard_map/all_to_all | solution.py:285
  128.1 14.8 %all_to_all.47 = f32[8,128,256]{2,1,0:T(8,128)S(1)} all-to-all(f32[8,128,256]{2,1,0:T(8,128)S(1)} %broadcast_in_dim.41), channel_id=1, replica_groups={{0,2,4,6,8,10,12,14},{16,18,20,22,24,26,28,30},{32,34,36,38,40,42,44,46..., dimensions={0} | all-to-all | bytes 2097152 | tf_op jit(solution)/shard_map/all_to_all | solution.py:285
  142.8 6.2 %collective-permute-start.9 = (f32[1024,256]{1,0:T(8,128)S(1)}, f32[1024,256]{1,0:T(8,128)S(1)}, u32[]{:S(2)}, u32[]{:S(2)}) collective-permute-start(f32[1024,256]{1,0:T(8,128)S(1)} %bitcast.39), channel_id=1, source_target_pairs={{0,1},{1,0},{2,3},{3,2},{4,5},{5,4},{6,7},{7,6},{8,9},{9,8},{10,11... | collective-permute-start | bytes 3145736 | tf_op jit(solution)/shard_map/ppermute | solution.py:267
  149.0 2.3 %shard_map.84 = (bf16[2240,256]{1,0:T(8,128)(2,1)}, bf16[2240,256]{1,0:T(8,128)(2,1)}) custom-call(s32[1]{0:T(128)} %bitcast.half_ref, s32[1,256]{1,0:T(1,128)S(1)} %bitcast.47, bf16[2240,256]{1,0:T(8,128)(2,1)S(1)} %bitcast.34, bf16[2240,256]{1,0:T(8,128)(2,1)S(1)} %bitcast.32, f32[1024,256]{1,0:T(8,128)S(1)} %bitcast.40), custom_call_target="tpu_custom_call" | custom-call | flops 880803840 | bytes 2293760 | tf_op jit(solution)/shard_map/pallas_call | solution.py:240
  151.3 2.3 %shard_map.85 = (bf16[2240,256]{1,0:T(8,128)(2,1)}, bf16[2240,256]{1,0:T(8,128)(2,1)}) custom-call(s32[1]{0:T(128)S(6)} %sub.3.half_ref, s32[1,256]{1,0:T(1,128)S(1)} %bitcast.48, bf16[2240,256]{1,0:T(8,128)(2,1)S(1)} %bitcast.35, bf16[2240,256]{1,0:T(8,128)(2,1)S(1)} %bitcast.33, ...), custom_call_target="tpu_custom_call", output_to_operand_aliasing={{0}: (5, {}), {1}: (6, {})} | custom-call | flops 880803840 | bytes 2293760 | tf_op jit(solution)/shard_map/pallas_call | solution.py:240
  (41 shorter events, 5.0 us)
Async XLA Ops:
  0.7 1.7 %copy-start.4 = (s32[256]{0:T(256)S(1)}, s32[256]{0:T(256)}, u32[]{:S(2)}) copy-start(s32[256]{0:T(256)} %param.9) | copy-start | bytes 3076
  3.1 5.6 %collective-permute-start = (f32[1024,256]{1,0:T(8,128)S(1)}, f32[1024,256]{1,0:T(8,128)S(1)}, u32[]{:S(2)}, u32[]{:S(2)}) collective-permute-start(f32[1024,256]{1,0:T(8,128)S(1)} %shard_map.77), channel_id=1, source_target_pairs={{0,1},{1,0},{2,3},{3,2},{4,5},{5,4},{6,7},{7,6},{8,9},{9,8},{10,11... | collective-permute-start | bytes 3145736 | tf_op jit(solution)/shard_map/ppermute | solution.py:267
  41.4 3.7 %collective-permute-start.3 = (f32[32,128]{1,0:T(8,128)S(1)}, f32[32,128]{1,0:T(8,128)S(1)}, u32[]{:S(2)}, u32[]{:S(2)}) collective-permute-start(f32[32,128]{1,0:T(8,128)S(1)} %slice_add_fusion.1), channel_id=1, source_target_pairs={{0,192},{64,0},{128,64},{192,128},{1,193},{65,1},{129,65},{193,129... | collective-permute-start | bytes 49160 | tf_op jit(solution)/shard_map/ppermute | solution.py:309
  43.9 4.1 %collective-permute-start.2 = (f32[32,128]{1,0:T(8,128)S(1)}, f32[32,128]{1,0:T(8,128)S(1)}, u32[]{:S(2)}, u32[]{:S(2)}) collective-permute-start(f32[32,128]{1,0:T(8,128)S(1)} %slice_add_fusion.1), channel_id=1, source_target_pairs={{0,128},{64,192},{128,0},{192,64},{1,129},{65,193},{129,1},{193,65... | collective-permute-start | bytes 49160 | tf_op jit(solution)/shard_map/ppermute | solution.py:309
  44.4 3.8 %collective-permute-start.1 = (f32[32,128]{1,0:T(8,128)S(1)}, f32[32,128]{1,0:T(8,128)S(1)}, u32[]{:S(2)}, u32[]{:S(2)}) collective-permute-start(f32[32,128]{1,0:T(8,128)S(1)} %slice_add_fusion.1), channel_id=1, source_target_pairs={{0,64},{64,128},{128,192},{192,0},{1,65},{65,129},{129,193},{193,1... | collective-permute-start | bytes 49160 | tf_op jit(solution)/shard_map/ppermute | solution.py:309
  57.9 21.5 %copy-start.1 = (bf16[256,2240]{0,1:T(8,128)(2,1)S(1)}, bf16[256,2240]{0,1:T(8,128)(2,1)}, u32[]{:S(2)}) copy-start(bf16[256,2240]{0,1:T(8,128)(2,1)} %param.8) | copy-start | bytes 3440644
  58.0 21.4 %copy-start = (bf16[256,2240]{0,1:T(8,128)(2,1)S(1)}, bf16[256,2240]{0,1:T(8,128)(2,1)}, u32[]{:S(2)}) copy-start(bf16[256,2240]{0,1:T(8,128)(2,1)} %param.5) | copy-start | bytes 3440644
  71.7 9.9 %collective-permute-start.4 = (f32[1024,256]{1,0:T(8,128)S(1)}, f32[1024,256]{1,0:T(8,128)S(1)}, u32[]{:S(2)}, u32[]{:S(2)}) collective-permute-start(f32[1024,256]{1,0:T(8,128)S(1)} %bitcast.36), channel_id=1, source_target_pairs={{0,1},{1,0},{2,3},{3,2},{4,5},{5,4},{6,7},{7,6},{8,9},{9,8},{10,11... | collective-permute-start | bytes 3145736 | tf_op jit(solution)/shard_map/ppermute | solution.py:267
  83.4 3.4 %collective-permute-start.5 = (f32[1024,256]{1,0:T(8,128)S(1)}, f32[1024,256]{1,0:T(8,128)S(1)}, u32[]{:S(2)}, u32[]{:S(2)}) collective-permute-start(f32[1024,256]{1,0:T(8,128)S(1)} %get-tuple-element.19), channel_id=1, source_target_pairs={{0,1},{1,0},{2,3},{3,2},{4,5},{5,4},{6,7},{7,6},{8,9},{9,8},{10,11... | collective-permute-start | bytes 3145736 | tf_op jit(solution)/shard_map/ppermute | solution.py:267
  113.6 3.9 %collective-permute-start.8 = (f32[32,128]{1,0:T(8,128)S(1)}, f32[32,128]{1,0:T(8,128)S(1)}, u32[]{:S(2)}, u32[]{:S(2)}) collective-permute-start(f32[32,128]{1,0:T(8,128)S(1)} %slice_add_fusion), channel_id=1, source_target_pairs={{0,64},{64,128},{128,192},{192,0},{1,65},{65,129},{129,193},{193,1... | collective-permute-start | bytes 49160 | tf_op jit(solution)/shard_map/ppermute | solution.py:309
  113.7 4.4 %collective-permute-start.7 = (f32[32,128]{1,0:T(8,128)S(1)}, f32[32,128]{1,0:T(8,128)S(1)}, u32[]{:S(2)}, u32[]{:S(2)}) collective-permute-start(f32[32,128]{1,0:T(8,128)S(1)} %slice_add_fusion), channel_id=1, source_target_pairs={{0,128},{64,192},{128,0},{192,64},{1,129},{65,193},{129,1},{193,65... | collective-permute-start | bytes 49160 | tf_op jit(solution)/shard_map/ppermute | solution.py:309
  115.2 3.0 %collective-permute-start.6 = (f32[32,128]{1,0:T(8,128)S(1)}, f32[32,128]{1,0:T(8,128)S(1)}, u32[]{:S(2)}, u32[]{:S(2)}) collective-permute-start(f32[32,128]{1,0:T(8,128)S(1)} %slice_add_fusion), channel_id=1, source_target_pairs={{0,192},{64,0},{128,64},{192,128},{1,193},{65,1},{129,65},{193,129... | collective-permute-start | bytes 49160 | tf_op jit(solution)/shard_map/ppermute | solution.py:309
  127.9 21.1 %copy-start.3 = (bf16[256,2240]{0,1:T(8,128)(2,1)S(1)}, bf16[256,2240]{0,1:T(8,128)(2,1)}, u32[]{:S(2)}) copy-start(bf16[256,2240]{0,1:T(8,128)(2,1)} %param.6) | copy-start | bytes 3440644
  128.0 21.0 %copy-start.2 = (bf16[256,2240]{0,1:T(8,128)(2,1)S(1)}, bf16[256,2240]{0,1:T(8,128)(2,1)}, u32[]{:S(2)}) copy-start(bf16[256,2240]{0,1:T(8,128)(2,1)} %param.7) | copy-start | bytes 3440644
  142.8 8.5 %collective-permute-start.9 = (f32[1024,256]{1,0:T(8,128)S(1)}, f32[1024,256]{1,0:T(8,128)S(1)}, u32[]{:S(2)}, u32[]{:S(2)}) collective-permute-start(f32[1024,256]{1,0:T(8,128)S(1)} %bitcast.39), channel_id=1, source_target_pairs={{0,1},{1,0},{2,3},{3,2},{4,5},{5,4},{6,7},{7,6},{8,9},{9,8},{10,11... | collective-permute-start | bytes 3145736 | tf_op jit(solution)/shard_map/ppermute | solution.py:267

commit v7 on v6

--- a/solution.py
+++ b/solution.py
@@ -328,7 +328,8 @@
     there = 1 - core
     send = key_states(there, ids, key, value)
     received = swap_cores(send)
-    keep = key_states(core, ids, key, value)
+    own, _ = lax.optimization_barrier((core, send))
+    keep = key_states(own, ids, key, value)
     mine = carried(keep + received, False)
     other = swap_cores(mine)
     aux_mine, keep = on_half(query_kernel, core, ids, (query, cot), (mine,), (), ("aux", "state"))

time: 154 us -> 155 us (level)
  no operation moved by 1% of the time
where the time goes in v7:
time: 155 us; the launch traced here: 154 us
  blocking collectives  107 us (69%)
  starting transfers between devices  24.7 us (16%)
  Pallas kernels  12.5 us (8%)
  waiting for transfers between devices  6.57 us (4%)
  local copies, waits for them, and re-layouts  1.61 us (1%)
  other arithmetic  1.57 us (1%)
    all_to_all x8, blocking collectives, exchange(): lax.all_to_all(block, 'space', 0, 0, axis_index_groups=members, tiled=False)  107 us
    ppermute x4, starting transfers between devices, swap_cores(): lax.ppermute(block, 'space', [(i, i ^ 1) for i in range(lax.axis_size('sp...  17.6 us
    pallas_call x6, Pallas kernels, on_half(): pl.pallas_call(kernel, out_shape=out_shape, grid_spec=pltpu.PrefetchScala...  11.1 us
    ppermute x6, starting transfers between devices, carried(): lax.ppermute(total, 'frames', [(i, (i + step) % frames) for i in range(fr...  7.07 us
    ppermute x6, waiting for transfers between devices, carried(): lax.ppermute(total, 'frames', [(i, (i + step) % frames) for i in range(fr...  4.41 us
  transfers between devices with their start and end apart: 10, of which 7 were waited for; matrix products, arithmetic and copies ran while one was open for 0% of the time, Pallas kernels for 5%

profile of v7, /device:TPU:1, one launch (start us, length us, event | category | flops | bytes accessed | tf_op | source)
XLA Modules:
  0.0 154.4 jit_solution(6228500903602326258)
XLA Ops:
  0.7 1.3 dynamic-slice_bitcast_fusion.2
  2.7 3.3 %collective-permute-start = (f32[1024,256]{1,0:T(8,128)S(1)}, f32[1024,256]{1,0:T(8,128)}, u32[]{:S(2)}, u32[]{:S(2)}) collective-permute-start(f32[1024,256]{1,0:T(8,128)S(1)} %shard_map.76), channel_id=1, source_target_pairs={{0,1},{1,0},{2,3},{3,2},{4,5},{5,4},{6,7},{7,6},{8,9},{9,8},{10,11... | collective-permute-start | bytes 3145736 | tf_op jit(solution)/shard_map/ppermute | solution.py:267
  6.8 1.6 %collective-permute-done = f32[1024,256]{1,0:T(8,128)} collective-permute-done((f32[1024,256]{1,0:T(8,128)S(1)}, f32[1024,256]{1,0:T(8,128)}, u32[]{:S(2)}, u32[]{:S(2)}) %collective-permute-start) | collective-permute-done | bytes 1048608 | tf_op jit(solution)/shard_map/ppermute | solution.py:267
  8.4 1.4 add.60
  9.8 18.0 %all_to_all.40.parts_ref = f32[8,128,256]{2,1,0:T(8,128)S(1)} all-to-all(f32[8,128,256]{2,1,0:T(8,128)S(1)} %bitcast.51), channel_id=1, replica_groups={{0,2,4,6,8,10,12,14},{16,18,20,22,24,26,28,30},{32,34,36,38,40,42,44,46..., dimensions={0} | all-to-all | bytes 2097152 | tf_op jit(solution)/shard_map/all_to_all | solution.py:285
  27.9 14.4 %all_to_all.41 = f32[4,32,256]{2,1,0:T(8,128)S(1)} all-to-all(f32[4,32,256]{2,1,0:T(8,128)S(1)} %shard_map.78), channel_id=1, replica_groups={{0,16,32,48},{2,18,34,50},{4,20,36,52},{6,22,38,54},{8,24,40,56},{10,26..., dimensions={0} | all-to-all | bytes 262144 | tf_op jit(solution)/shard_map/all_to_all | solution.py:285
  42.3 2.6 %collective-permute-start.3 = (f32[32,128]{1,0:T(8,128)S(1)}, f32[32,128]{1,0:T(8,128)S(1)}, u32[]{:S(2)}, u32[]{:S(2)}) collective-permute-start(f32[32,128]{1,0:T(8,128)S(1)} %slice_add_fusion.1), channel_id=1, source_target_pairs={{0,192},{64,0},{128,64},{192,128},{1,193},{65,1},{129,65},{193,129... | collective-permute-start | bytes 49160 | tf_op jit(solution)/shard_map/ppermute | solution.py:309
  46.0 3.0 %collective-permute-done.2 = f32[32,128]{1,0:T(8,128)S(1)} collective-permute-done((f32[32,128]{1,0:T(8,128)S(1)}, f32[32,128]{1,0:T(8,128)S(1)}, u32[]{:S(2)}, u32[]{:S(2)}) %collective-permute-start.2) | collective-permute-done | bytes 16416 | tf_op jit(solution)/shard_map/ppermute | solution.py:309
  49.2 9.6 %all_to_all.42 = f32[4,32,256]{2,1,0:T(8,128)S(1)} all-to-all(f32[4,32,256]{2,1,0:T(8,128)S(1)} %broadcast_in_dim.36), channel_id=1, replica_groups={{0,16,32,48},{2,18,34,50},{4,20,36,52},{6,22,38,54},{8,24,40,56},{10,26..., dimensions={0} | all-to-all | bytes 262144 | tf_op jit(solution)/shard_map/all_to_all | solution.py:285
  59.0 13.7 %all_to_all.43 = f32[8,128,256]{2,1,0:T(8,128)S(1)} all-to-all(f32[8,128,256]{2,1,0:T(8,128)S(1)} %broadcast_in_dim.38), channel_id=1, replica_groups={{0,2,4,6,8,10,12,14},{16,18,20,22,24,26,28,30},{32,34,36,38,40,42,44,46..., dimensions={0} | all-to-all | bytes 2097152 | tf_op jit(solution)/shard_map/all_to_all | solution.py:285
  72.7 7.6 %collective-permute-start.4 = (f32[1024,256]{1,0:T(8,128)S(1)}, f32[1024,256]{1,0:T(8,128)S(1)}, u32[]{:S(2)}, u32[]{:S(2)}) collective-permute-start(f32[1024,256]{1,0:T(8,128)S(1)} %bitcast.37), channel_id=1, source_target_pairs={{0,1},{1,0},{2,3},{3,2},{4,5},{5,4},{6,7},{7,6},{8,9},{9,8},{10,11... | collective-permute-start | bytes 3145736 | tf_op jit(solution)/shard_map/ppermute | solution.py:267
  80.3 1.8 %shard_map.79 = (f32[10,2,256]{2,1,0:T(2,128)S(1)}, f32[1024,256]{1,0:T(8,128)S(1)}) custom-call(s32[1]{0:T(128)} %bitcast.half_ref, s32[1,256]{1,0:T(1,128)S(1)} %bitcast.44, bf16[2240,256]{1,0:T(8,128)(2,1)S(1)} %bitcast.25, bf16[2240,256]{1,0:T(8,128)(2,1)S(1)} %bitcast.29, f32[1024,256]{1,0:T(8,128)S(1)} %bitcast.38), custom_call_target="tpu_custom_call" | custom-call | flops 880803840 | bytes 2293760 | tf_op jit(solution)/shard_map/pallas_call | solution.py:240
  82.6 1.8 %shard_map.80 = (f32[10,2,256]{2,1,0:T(2,128)S(1)}, f32[1024,256]{1,0:T(8,128)S(1)}) custom-call(s32[1]{0:T(128)S(6)} %sub.3.half_ref, s32[1,256]{1,0:T(1,128)S(1)} %bitcast.45, bf16[2240,256]{1,0:T(8,128)(2,1)S(1)} %bitcast.26, bf16[2240,256]{1,0:T(8,128)(2,1)S(1)} %bitcast.30, f32[1024,256]{1,0:T(8,128)S(1)} %collective-permute-done.4.state_ref), custom_call_target="tpu_custom_call" | custom-call | flops 880803840 | bytes 2293760 | tf_op jit(solution)/shard_map/pallas_call | solution.py:240
  84.8 1.5 shard_map.81.refs_0_
  86.3 1.5 shard_map.82
  87.9 16.9 %all_to_all.44.parts_ref = f32[8,128,256]{2,1,0:T(8,128)S(1)} all-to-all(f32[8,128,256]{2,1,0:T(8,128)S(1)} %bitcast.52), channel_id=1, replica_groups={{0,2,4,6,8,10,12,14},{16,18,20,22,24,26,28,30},{32,34,36,38,40,42,44,46..., dimensions={0} | all-to-all | bytes 2097152 | tf_op jit(solution)/shard_map/all_to_all | solution.py:285
  104.9 9.6 %all_to_all.45 = f32[4,32,256]{2,1,0:T(8,128)S(1)} all-to-all(f32[4,32,256]{2,1,0:T(8,128)S(1)} %shard_map.83), channel_id=1, replica_groups={{0,16,32,48},{2,18,34,50},{4,20,36,52},{6,22,38,54},{8,24,40,56},{10,26..., dimensions={0} | all-to-all | bytes 262144 | tf_op jit(solution)/shard_map/all_to_all | solution.py:285
  114.7 1.5 collective-permute-start.7
  116.2 1.8 %collective-permute-start.6 = (f32[32,128]{1,0:T(8,128)S(1)}, f32[32,128]{1,0:T(8,128)S(1)}, u32[]{:S(2)}, u32[]{:S(2)}) collective-permute-start(f32[32,128]{1,0:T(8,128)S(1)} %slice_add_fusion), channel_id=1, source_target_pairs={{0,192},{64,0},{128,64},{192,128},{1,193},{65,1},{129,65},{193,129... | collective-permute-start | bytes 49160 | tf_op jit(solution)/shard_map/ppermute | solution.py:309
  119.3 9.6 %all_to_all.46 = f32[4,32,256]{2,1,0:T(8,128)S(1)} all-to-all(f32[4,32,256]{2,1,0:T(8,128)S(1)} %broadcast_in_dim.39), channel_id=1, replica_groups={{0,16,32,48},{2,18,34,50},{4,20,36,52},{6,22,38,54},{8,24,40,56},{10,26..., dimensions={0} | all-to-all | bytes 262144 | tf_op jit(solution)/shard_map/all_to_all | solution.py:285
  129.0 14.7 %all_to_all.47 = f32[8,128,256]{2,1,0:T(8,128)S(1)} all-to-all(f32[8,128,256]{2,1,0:T(8,128)S(1)} %broadcast_in_dim.41), channel_id=1, replica_groups={{0,2,4,6,8,10,12,14},{16,18,20,22,24,26,28,30},{32,34,36,38,40,42,44,46..., dimensions={0} | all-to-all | bytes 2097152 | tf_op jit(solution)/shard_map/all_to_all | solution.py:285
  143.6 6.2 %collective-permute-start.9 = (f32[1024,256]{1,0:T(8,128)S(1)}, f32[1024,256]{1,0:T(8,128)S(1)}, u32[]{:S(2)}, u32[]{:S(2)}) collective-permute-start(f32[1024,256]{1,0:T(8,128)S(1)} %bitcast.40), channel_id=1, source_target_pairs={{0,1},{1,0},{2,3},{3,2},{4,5},{5,4},{6,7},{7,6},{8,9},{9,8},{10,11... | collective-permute-start | bytes 3145736 | tf_op jit(solution)/shard_map/ppermute | solution.py:267
  149.8 2.3 %shard_map.84 = (bf16[2240,256]{1,0:T(8,128)(2,1)}, bf16[2240,256]{1,0:T(8,128)(2,1)}) custom-call(s32[1]{0:T(128)} %bitcast.half_ref, s32[1,256]{1,0:T(1,128)S(1)} %bitcast.48, bf16[2240,256]{1,0:T(8,128)(2,1)S(1)} %bitcast.33, bf16[2240,256]{1,0:T(8,128)(2,1)S(1)} %bitcast.35, f32[1024,256]{1,0:T(8,128)S(1)} %bitcast.41), custom_call_target="tpu_custom_call" | custom-call | flops 880803840 | bytes 2293760 | tf_op jit(solution)/shard_map/pallas_call | solution.py:240
  152.1 2.3 %shard_map.85 = (bf16[2240,256]{1,0:T(8,128)(2,1)}, bf16[2240,256]{1,0:T(8,128)(2,1)}) custom-call(s32[1]{0:T(128)S(6)} %sub.3.half_ref, s32[1,256]{1,0:T(1,128)S(1)} %bitcast.49, bf16[2240,256]{1,0:T(8,128)(2,1)S(1)} %bitcast.34, bf16[2240,256]{1,0:T(8,128)(2,1)S(1)} %bitcast.36, ...), custom_call_target="tpu_custom_call", output_to_operand_aliasing={{0}: (5, {}), {1}: (6, {})} | custom-call | flops 880803840 | bytes 2293760 | tf_op jit(solution)/shard_map/pallas_call | solution.py:240
  (43 shorter events, 5.6 us)
Async XLA Ops:
  0.6 1.3 copy-start.4
  2.0 4.0 %copy-start.3 = (bf16[256,2240]{0,1:T(8,128)(2,1)S(1)}, bf16[256,2240]{0,1:T(8,128)(2,1)}, u32[]{:S(2)}) copy-start(bf16[256,2240]{0,1:T(8,128)(2,1)} %param.7) | copy-start | bytes 3440644
  2.0 4.0 %copy-start.2 = (bf16[256,2240]{0,1:T(8,128)(2,1)S(1)}, bf16[256,2240]{0,1:T(8,128)(2,1)}, u32[]{:S(2)}) copy-start(bf16[256,2240]{0,1:T(8,128)(2,1)} %param.6) | copy-start | bytes 3440644
  2.7 5.7 %collective-permute-start = (f32[1024,256]{1,0:T(8,128)S(1)}, f32[1024,256]{1,0:T(8,128)}, u32[]{:S(2)}, u32[]{:S(2)}) collective-permute-start(f32[1024,256]{1,0:T(8,128)S(1)} %shard_map.76), channel_id=1, source_target_pairs={{0,1},{1,0},{2,3},{3,2},{4,5},{5,4},{6,7},{7,6},{8,9},{9,8},{10,11... | collective-permute-start | bytes 3145736 | tf_op jit(solution)/shard_map/ppermute | solution.py:267
  42.3 3.7 %collective-permute-start.3 = (f32[32,128]{1,0:T(8,128)S(1)}, f32[32,128]{1,0:T(8,128)S(1)}, u32[]{:S(2)}, u32[]{:S(2)}) collective-permute-start(f32[32,128]{1,0:T(8,128)S(1)} %slice_add_fusion.1), channel_id=1, source_target_pairs={{0,192},{64,0},{128,64},{192,128},{1,193},{65,1},{129,65},{193,129... | collective-permute-start | bytes 49160 | tf_op jit(solution)/shard_map/ppermute | solution.py:309
  44.9 4.1 %collective-permute-start.2 = (f32[32,128]{1,0:T(8,128)S(1)}, f32[32,128]{1,0:T(8,128)S(1)}, u32[]{:S(2)}, u32[]{:S(2)}) collective-permute-start(f32[32,128]{1,0:T(8,128)S(1)} %slice_add_fusion.1), channel_id=1, source_target_pairs={{0,128},{64,192},{128,0},{192,64},{1,129},{65,193},{129,1},{193,65... | collective-permute-start | bytes 49160 | tf_op jit(solution)/shard_map/ppermute | solution.py:309
  45.4 3.8 %collective-permute-start.1 = (f32[32,128]{1,0:T(8,128)S(1)}, f32[32,128]{1,0:T(8,128)S(1)}, u32[]{:S(2)}, u32[]{:S(2)}) collective-permute-start(f32[32,128]{1,0:T(8,128)S(1)} %slice_add_fusion.1), channel_id=1, source_target_pairs={{0,64},{64,128},{128,192},{192,0},{1,65},{65,129},{129,193},{193,1... | collective-permute-start | bytes 49160 | tf_op jit(solution)/shard_map/ppermute | solution.py:309
  58.9 21.5 %copy-start.1 = (bf16[256,2240]{0,1:T(8,128)(2,1)S(1)}, bf16[256,2240]{0,1:T(8,128)(2,1)}, u32[]{:S(2)}) copy-start(bf16[256,2240]{0,1:T(8,128)(2,1)} %param.8) | copy-start | bytes 3440644
  58.9 21.4 %copy-start = (bf16[256,2240]{0,1:T(8,128)(2,1)S(1)}, bf16[256,2240]{0,1:T(8,128)(2,1)}, u32[]{:S(2)}) copy-start(bf16[256,2240]{0,1:T(8,128)(2,1)} %param.5) | copy-start | bytes 3440644
  72.7 9.9 %collective-permute-start.4 = (f32[1024,256]{1,0:T(8,128)S(1)}, f32[1024,256]{1,0:T(8,128)S(1)}, u32[]{:S(2)}, u32[]{:S(2)}) collective-permute-start(f32[1024,256]{1,0:T(8,128)S(1)} %bitcast.37), channel_id=1, source_target_pairs={{0,1},{1,0},{2,3},{3,2},{4,5},{5,4},{6,7},{7,6},{8,9},{9,8},{10,11... | collective-permute-start | bytes 3145736 | tf_op jit(solution)/shard_map/ppermute | solution.py:267
  84.4 3.4 %collective-permute-start.5 = (f32[1024,256]{1,0:T(8,128)S(1)}, f32[1024,256]{1,0:T(8,128)S(1)}, u32[]{:S(2)}, u32[]{:S(2)}) collective-permute-start(f32[1024,256]{1,0:T(8,128)S(1)} %get-tuple-element.21), channel_id=1, source_target_pairs={{0,1},{1,0},{2,3},{3,2},{4,5},{5,4},{6,7},{7,6},{8,9},{9,8},{10,11... | collective-permute-start | bytes 3145736 | tf_op jit(solution)/shard_map/ppermute | solution.py:267
  114.6 3.9 %collective-permute-start.8 = (f32[32,128]{1,0:T(8,128)S(1)}, f32[32,128]{1,0:T(8,128)S(1)}, u32[]{:S(2)}, u32[]{:S(2)}) collective-permute-start(f32[32,128]{1,0:T(8,128)S(1)} %slice_add_fusion), channel_id=1, source_target_pairs={{0,64},{64,128},{128,192},{192,0},{1,65},{65,129},{129,193},{193,1... | collective-permute-start | bytes 49160 | tf_op jit(solution)/shard_map/ppermute | solution.py:309
  114.7 4.4 %collective-permute-start.7 = (f32[32,128]{1,0:T(8,128)S(1)}, f32[32,128]{1,0:T(8,128)S(1)}, u32[]{:S(2)}, u32[]{:S(2)}) collective-permute-start(f32[32,128]{1,0:T(8,128)S(1)} %slice_add_fusion), channel_id=1, source_target_pairs={{0,128},{64,192},{128,0},{192,64},{1,129},{65,193},{129,1},{193,65... | collective-permute-start | bytes 49160 | tf_op jit(solution)/shard_map/ppermute | solution.py:309
  116.2 3.0 %collective-permute-start.6 = (f32[32,128]{1,0:T(8,128)S(1)}, f32[32,128]{1,0:T(8,128)S(1)}, u32[]{:S(2)}, u32[]{:S(2)}) collective-permute-start(f32[32,128]{1,0:T(8,128)S(1)} %slice_add_fusion), channel_id=1, source_target_pairs={{0,192},{64,0},{128,64},{192,128},{1,193},{65,1},{129,65},{193,129... | collective-permute-start | bytes 49160 | tf_op jit(solution)/shard_map/ppermute | solution.py:309
  143.6 8.5 %collective-permute-start.9 = (f32[1024,256]{1,0:T(8,128)S(1)}, f32[1024,256]{1,0:T(8,128)S(1)}, u32[]{:S(2)}, u32[]{:S(2)}) collective-permute-start(f32[1024,256]{1,0:T(8,128)S(1)} %bitcast.40), channel_id=1, source_target_pairs={{0,1},{1,0},{2,3},{3,2},{4,5},{5,4},{6,7},{7,6},{8,9},{9,8},{10,11... | collective-permute-start | bytes 3145736 | tf_op jit(solution)/shard_map/ppermute | solution.py:267
